TPU v7x, 32 devices: a whole 2x2x4 slice. The times are simulated.
32 devices in a mesh: shard: 4 (over x, core), ctx: 2 (over y), tensor: 4 (over z).
Axes of the slice: x: 2, y: 2, z: 4, core: 2. Of those that a mesh axis runs over, the one named last changes fastest.
Arguments:
- tokens: bfloat16 [16, 2048, 768], P('shard', 'ctx'), may hold values from -6 to 6
- cotangent: bfloat16 [16, 2048, 768], P('shard', 'ctx'), may hold values from -6 to 6
- segments: int32 [16, 2048], P('shard'), may hold values from 0 to 5, never falling along the last dimension, each value on 1 to 800 neighbouring positions
- rand_blocks: int32 [16, 32, 3], P('shard'), may hold values from 0 to 31
- attn_w: float32 [4, 768, 768], P(None, ('shard', 'ctx'), 'tensor'), may hold values from -3.4641016 to 3.4641016, as said below
- attn_m: float32 [4, 768, 768], P(None, ('shard', 'ctx'), 'tensor'), may hold values from -119.47276 to 119.47276, as said below
- attn_v: float32 [4, 768, 768], P(None, ('shard', 'ctx'), 'tensor'), may hold values from 0.1605632 to 131.072, as said below
- ffn_w: float32 [2, 768, 3072], P(None, ('shard', 'ctx'), 'tensor'), may hold values from -0.21650635 to 0.21650635, as said below
- ffn_m: float32 [2, 768, 3072], P(None, ('shard', 'ctx'), 'tensor'), may hold values from -64 to 64
- ffn_v: float32 [2, 768, 3072], P(None, ('shard', 'ctx'), 'tensor'), may hold values from 8.192 to 32.768
- qv_bias: float32 [2, 768], P(None, 'tensor'), may hold values from -3 to 3
- qv_m: float32 [2, 768], P(None, 'tensor'), may hold values from -128 to 128
- qv_v: float32 [2, 768], P(None, 'tensor'), may hold values from 32.768 to 131.072
- hid_bias: float32 [3072], P('tensor'), may hold values from -3 to 3
- hid_m: float32 [3072], P('tensor'), may hold values from -64 to 64
- hid_v: float32 [3072], P('tensor'), may hold values from 8.192 to 32.768
- vec_par: float32 [6, 768], replicated, may hold values from -3 to 3, as said below
- vec_m: float32 [6, 768], replicated, may hold values from -128 to 128
- vec_v: float32 [6, 768], replicated, may hold values from 32.768 to 131.072
Outputs:
- output: bfloat16 [16, 2048, 768], P('shard', 'ctx')
- grad_tokens: float32 [16, 2048, 768], P('shard', 'ctx')
- attn_moment: float32 [3, 768, 768], P(None, ('shard', 'ctx'), 'tensor')
- attn_square: float32 [3, 768, 768], P(None, ('shard', 'ctx'), 'tensor')
- out_states: float32 [2, 768, 768], P(None, ('shard', 'ctx'), 'tensor')
- attn_new: float32 [4, 768, 768], P(None, ('shard', 'ctx'), 'tensor')
- attn_copy: bfloat16 [4, 768, 768], P(None, ('shard', 'ctx'), 'tensor')
- ffn_moment: float32 [2, 768, 3072], P(None, ('shard', 'ctx'), 'tensor')
- ffn_square: float32 [2, 768, 3072], P(None, ('shard', 'ctx'), 'tensor')
- ffn_new: float32 [2, 768, 3072], P(None, ('shard', 'ctx'), 'tensor')
- ffn_copy: bfloat16 [2, 768, 3072], P(None, ('shard', 'ctx'), 'tensor')
- qv_moment: float32 [2, 768], P(None, 'tensor')
- qv_square: float32 [2, 768], P(None, 'tensor')
- qv_new: float32 [2, 768], P(None, 'tensor')
- hid_moment: float32 [3072], P('tensor')
- hid_square: float32 [3072], P('tensor')
- hid_new: float32 [3072], P('tensor')
- vec_moment: float32 [6, 768], replicated
- vec_square: float32 [6, 768], replicated
- vec_new: float32 [6, 768], replicated
Inputs may be any that keep to these rules, and one draw needn't show every extreme that they name: `segments`: within a sequence the document numbers never fall; a document holds at most 800 tokens. `attn_w`: independent entries, spread 1 / sqrt(768) in the first three matrices and 1 / sqrt(3) in the fourth. `attn_m`: independent entries of both signs. `attn_v`: positive entries. `ffn_w`: independent entries, spread 1 / sqrt(768) in the first matrix and 1 / sqrt(3072) in the second. `vec_par`: gains near 1, shifts and biases of both signs.
All inputs are finite; a program needn't handle non-finite values.
Results may differ from a plain program's by a relative error of at most 0.02.
Values may be sent and summed in bfloat16 or wider, within the bound.
A program may use at most 384 MiB of HBM per device.

v0:
```python
from functools import partial

import jax
import jax.numpy as jnp
from jax import lax
from jax.sharding import PartitionSpec as P

D = 768
HEAD_DIM = 64
FF = 3072
BLOCK = 64
MICRO = 2
STEP = 5


beta_first = 0.9
beta_second = 0.999
adam_eps = 1e-08
decay_rate = 0.01
norm_eps = 1e-06
neg_large = -1e30


def matmul(left, right):
    return jnp.dot(left, right, preferred_element_type=jnp.float32)


def matmul_tn(left, right):
    return lax.dot_general(
        left, right, (((0,), (0,)), ((), ())), preferred_element_type=jnp.float32
    )


def matmul_nt(left, right):
    return lax.dot_general(
        left, right, (((1,), (1,)), ((), ())), preferred_element_type=jnp.float32
    )


def layer_norm(hidden, norm_gain, norm_shift):
    centred = hidden - jnp.mean(hidden, axis=-1, keepdims=True)
    spread = jnp.mean(centred * centred, axis=-1, keepdims=True)
    return centred * lax.rsqrt(spread + norm_eps) * norm_gain + norm_shift


def column_sum(array_in):
    return jnp.sum(array_in.astype(jnp.float32), axis=0)


def adam_update(weight, moment, square, gradient, step_rates, decay_on):
    moment_new = beta_first * moment + (1.0 - beta_first) * gradient
    square_new = beta_second * square + (1.0 - beta_second) * gradient * gradient
    step_ratio = (
        moment_new
        / (1.0 - beta_first**STEP)
        / (jnp.sqrt(square_new / (1.0 - beta_second**STEP)) + adam_eps)
    )
    weight_new = weight - step_rates * (step_ratio + decay_on * weight)
    return (moment_new, square_new, weight_new)


def block_lists(random_part, ctx_index, local_blocks, total_blocks):
    seq_count = random_part.shape[0]
    own_blocks = ctx_index * local_blocks + jnp.arange(local_blocks, dtype=jnp.int32)
    zero_col = jnp.zeros_like(own_blocks)
    fixed_part = jnp.stack(
        [own_blocks - 1, own_blocks, own_blocks + 1, zero_col, zero_col + 1], axis=-1
    )
    listed = jnp.concatenate(
        [jnp.broadcast_to(fixed_part[None], (seq_count, local_blocks, 5)), random_part], axis=-1
    )
    list_width = listed.shape[-1]
    earlier = jnp.arange(list_width)[None, :] < jnp.arange(list_width)[:, None]
    repeated = jnp.any((listed[..., :, None] == listed[..., None, :]) & earlier, axis=-1)
    inside = (listed >= 0) & (listed < total_blocks)
    return (jnp.clip(listed, 0, total_blocks - 1), inside & jnp.logical_not(repeated))


def take_blocks(source, chosen):
    return jax.vmap(lambda block_table, picked_ids: block_table[picked_ids])(source, chosen)


def sparse_setup(keys_full, values_full, segment_part, random_part, ctx_index, piece_len):
    seq_count, total_len, local_width = keys_full.shape
    local_blocks = piece_len // BLOCK
    total_blocks = total_len // BLOCK
    local_heads = local_width // HEAD_DIM
    random_local = lax.dynamic_slice_in_dim(random_part, ctx_index * local_blocks, local_blocks, 1)
    chosen, usable = block_lists(random_local, ctx_index, local_blocks, total_blocks)
    key_rows = take_blocks(keys_full.reshape(seq_count, total_blocks, BLOCK * local_width), chosen)
    key_rows = key_rows.reshape(seq_count, local_blocks, -1, local_heads, HEAD_DIM)
    value_rows = take_blocks(
        values_full.reshape(seq_count, total_blocks, BLOCK * local_width), chosen
    )
    value_rows = value_rows.reshape(seq_count, local_blocks, -1, local_heads, HEAD_DIM)
    key_segments = take_blocks(
        segment_part.reshape(seq_count, total_blocks, BLOCK), chosen
    ).reshape(seq_count, local_blocks, -1)
    query_segments = lax.dynamic_slice_in_dim(
        segment_part, ctx_index * piece_len, piece_len, 1
    ).reshape(seq_count, local_blocks, BLOCK)
    key_usable = jnp.repeat(usable, BLOCK, axis=-1)
    key_global = jnp.repeat(chosen < 2, BLOCK, axis=-1)
    allowed = key_usable[:, :, None, :] & (
        (query_segments[:, :, :, None] == key_segments[:, :, None, :]) | key_global[:, :, None, :]
    )
    block_hits = (
        chosen.reshape(seq_count, -1)[:, :, None] == jnp.arange(total_blocks)[None, None, :]
    ).astype(jnp.float32)
    return (key_rows, value_rows, allowed[:, :, None], block_hits)


def sparse_scores(query_blocks, key_rows):
    return (
        jnp.einsum("sbqhd,sbkhd->sbhqk", query_blocks, key_rows, preferred_element_type=jnp.float32)
        * 0.125
    )


def global_scores(query_top, keys_heads):
    return (
        jnp.einsum("sqhd,skhd->shqk", query_top, keys_heads, preferred_element_type=jnp.float32)
        * 0.125
    )


def attend_forward(queries, keys_full, values_full, segment_part, random_part, ctx_index):
    seq_count, piece_len, local_width = queries.shape
    local_heads = local_width // HEAD_DIM
    local_blocks = piece_len // BLOCK
    top_rows = 2 * BLOCK
    key_rows, value_rows, allowed, block_hits = sparse_setup(
        keys_full, values_full, segment_part, random_part, ctx_index, piece_len
    )
    query_blocks = queries.reshape(seq_count, local_blocks, BLOCK, local_heads, HEAD_DIM)
    scores = jnp.where(allowed, sparse_scores(query_blocks, key_rows), neg_large)
    largest = jnp.max(scores, axis=-1, keepdims=True)
    weights = jnp.where(allowed, jnp.exp(scores - largest), 0.0)
    totals = jnp.sum(weights, axis=-1, keepdims=True)
    probs = (weights / totals).astype(jnp.bfloat16)
    sparse_out = jnp.einsum(
        "sbhqk,sbkhd->sbqhd", probs, value_rows, preferred_element_type=jnp.float32
    )
    sparse_out = sparse_out.reshape(seq_count, piece_len, local_width)
    sparse_lse = largest + jnp.log(totals)
    keys_heads = keys_full.reshape(seq_count, -1, local_heads, HEAD_DIM)
    values_heads = values_full.reshape(seq_count, -1, local_heads, HEAD_DIM)
    query_top = queries[:, :top_rows].reshape(seq_count, top_rows, local_heads, HEAD_DIM)

    def global_part():
        top_scores = global_scores(query_top, keys_heads)
        top_largest = jnp.max(top_scores, axis=-1, keepdims=True)
        top_weights = jnp.exp(top_scores - top_largest)
        top_totals = jnp.sum(top_weights, axis=-1, keepdims=True)
        top_probs = (top_weights / top_totals).astype(jnp.bfloat16)
        top_out = jnp.einsum(
            "shqk,skhd->sqhd", top_probs, values_heads, preferred_element_type=jnp.float32
        )
        return (
            top_out.reshape(seq_count, top_rows, local_width),
            top_largest + jnp.log(top_totals),
        )

    def skip_part():
        return (
            jnp.zeros((seq_count, top_rows, local_width), jnp.float32),
            jnp.zeros((seq_count, local_heads, top_rows, 1), jnp.float32),
        )

    top_out, top_lse = lax.cond(ctx_index == 0, global_part, skip_part)
    is_top = (ctx_index == 0) & (jnp.arange(piece_len) < top_rows)
    padded = jnp.pad(top_out, ((0, 0), (0, piece_len - top_rows), (0, 0)))
    mixed = jnp.where(is_top[None, :, None], padded, sparse_out)
    return (mixed, sparse_lse, top_lse)


def attend_backward(
    queries,
    keys_full,
    values_full,
    segment_part,
    random_part,
    ctx_index,
    sparse_lse,
    top_lse,
    grad_mixed,
):
    seq_count, piece_len, local_width = queries.shape
    total_len = keys_full.shape[1]
    local_heads = local_width // HEAD_DIM
    local_blocks = piece_len // BLOCK
    top_rows = 2 * BLOCK
    key_rows, value_rows, allowed, block_hits = sparse_setup(
        keys_full, values_full, segment_part, random_part, ctx_index, piece_len
    )
    query_blocks = queries.reshape(seq_count, local_blocks, BLOCK, local_heads, HEAD_DIM)
    is_top = (ctx_index == 0) & (jnp.arange(piece_len) < top_rows)
    grad_sparse = jnp.where(is_top[None, :, None], jnp.zeros_like(grad_mixed), grad_mixed)
    grad_sparse = grad_sparse.reshape(seq_count, local_blocks, BLOCK, local_heads, HEAD_DIM)
    scores = sparse_scores(query_blocks, key_rows)
    probs = jnp.where(allowed, jnp.exp(scores - sparse_lse), 0.0)
    grad_probs = jnp.einsum(
        "sbqhd,sbkhd->sbhqk", grad_sparse, value_rows, preferred_element_type=jnp.float32
    )
    centre = jnp.sum(probs * grad_probs, axis=-1, keepdims=True)
    grad_scores = (probs * (grad_probs - centre)).astype(jnp.bfloat16)
    grad_query = (
        jnp.einsum("sbhqk,sbkhd->sbqhd", grad_scores, key_rows, preferred_element_type=jnp.float32)
        * 0.125
    )
    grad_query = grad_query.reshape(seq_count, piece_len, local_width)
    grad_key_rows = (
        jnp.einsum(
            "sbhqk,sbqhd->sbkhd", grad_scores, query_blocks, preferred_element_type=jnp.float32
        )
        * 0.125
    )
    grad_value_rows = jnp.einsum(
        "sbhqk,sbqhd->sbkhd",
        probs.astype(jnp.bfloat16),
        grad_sparse,
        preferred_element_type=jnp.float32,
    )
    grad_keys_full = jnp.einsum(
        "sjn,sjc->snc",
        block_hits,
        grad_key_rows.reshape(seq_count, block_hits.shape[1], -1),
        precision=lax.Precision.HIGHEST,
    )
    grad_values_full = jnp.einsum(
        "sjn,sjc->snc",
        block_hits,
        grad_value_rows.reshape(seq_count, block_hits.shape[1], -1),
        precision=lax.Precision.HIGHEST,
    )
    grad_keys_full = grad_keys_full.reshape(seq_count, total_len, local_width)
    grad_values_full = grad_values_full.reshape(seq_count, total_len, local_width)
    keys_heads = keys_full.reshape(seq_count, -1, local_heads, HEAD_DIM)
    values_heads = values_full.reshape(seq_count, -1, local_heads, HEAD_DIM)
    query_top = queries[:, :top_rows].reshape(seq_count, top_rows, local_heads, HEAD_DIM)
    grad_top = grad_mixed[:, :top_rows].reshape(seq_count, top_rows, local_heads, HEAD_DIM)

    def global_back():
        top_probs = jnp.exp(global_scores(query_top, keys_heads) - top_lse)
        top_grad_probs = jnp.einsum(
            "sqhd,skhd->shqk", grad_top, values_heads, preferred_element_type=jnp.float32
        )
        top_centre = jnp.sum(top_probs * top_grad_probs, axis=-1, keepdims=True)
        top_grad_scores = (top_probs * (top_grad_probs - top_centre)).astype(jnp.bfloat16)
        query_part = (
            jnp.einsum(
                "shqk,skhd->sqhd", top_grad_scores, keys_heads, preferred_element_type=jnp.float32
            )
            * 0.125
        )
        key_part = (
            jnp.einsum(
                "shqk,sqhd->skhd", top_grad_scores, query_top, preferred_element_type=jnp.float32
            )
            * 0.125
        )
        value_part = jnp.einsum(
            "shqk,sqhd->skhd",
            top_probs.astype(jnp.bfloat16),
            grad_top,
            preferred_element_type=jnp.float32,
        )
        return (
            query_part.reshape(seq_count, top_rows, local_width),
            key_part.reshape(seq_count, total_len, local_width),
            value_part.reshape(seq_count, total_len, local_width),
        )

    def skip_back():
        return (
            jnp.zeros((seq_count, top_rows, local_width), jnp.float32),
            jnp.zeros((seq_count, total_len, local_width), jnp.float32),
            jnp.zeros((seq_count, total_len, local_width), jnp.float32),
        )

    query_part, key_part, value_part = lax.cond(ctx_index == 0, global_back, skip_back)
    grad_query = grad_query + jnp.pad(query_part, ((0, 0), (0, piece_len - top_rows), (0, 0)))
    return (grad_query, grad_keys_full + key_part, grad_values_full + value_part)


def micro_step(
    tokens_mb,
    cot_mb,
    segment_mb,
    random_mb,
    attn_full,
    ffn_full,
    qv_bias,
    hid_bias,
    vec_par,
    ctx_index,
):
    seq_count, piece_len, model_width = tokens_mb.shape
    local_width = attn_full.shape[2]
    flat_rows = tokens_mb.reshape(-1, model_width)
    queries = (matmul(flat_rows, attn_full[0]) + qv_bias[0]).astype(jnp.bfloat16)
    keys_local = matmul(flat_rows, attn_full[1]).astype(jnp.bfloat16)
    values_local = (matmul(flat_rows, attn_full[2]) + qv_bias[1]).astype(jnp.bfloat16)
    keys_full, values_full = (
        lax.all_gather(
            keys_local.reshape(seq_count, piece_len, local_width), "ctx", axis=1, tiled=True
        ),
        lax.all_gather(
            values_local.reshape(seq_count, piece_len, local_width), "ctx", axis=1, tiled=True
        ),
    )
    query_seq = queries.reshape(seq_count, piece_len, local_width)
    mixed, sparse_lse, top_lse = attend_forward(
        query_seq, keys_full, values_full, segment_mb, random_mb, ctx_index
    )
    mixed_low = mixed.reshape(-1, local_width).astype(jnp.bfloat16)
    branch = lax.psum(matmul_nt(mixed_low, attn_full[3]), "tensor") + vec_par[4]
    first_in = flat_rows.astype(jnp.float32) + branch
    first_out = layer_norm(first_in, vec_par[0], vec_par[1])
    first_low = first_out.astype(jnp.bfloat16)
    hidden_pre = matmul(first_low, ffn_full[0]) + hid_bias
    hidden_low = jax.nn.gelu(hidden_pre, approximate=False).astype(jnp.bfloat16)
    down_out = (
        lax.psum(matmul_nt(hidden_low, ffn_full[1]).astype(jnp.bfloat16), "tensor").astype(
            jnp.float32
        )
        + vec_par[5]
    )
    second_in = first_out + down_out
    result = layer_norm(second_in, vec_par[2], vec_par[3])
    cot_flat = cot_mb.reshape(-1, model_width).astype(jnp.float32)
    second_back = jax.vjp(layer_norm, second_in, vec_par[2], vec_par[3])[1]
    grad_second, gain_second, shift_second = second_back(cot_flat)
    grad_down = grad_second.astype(jnp.bfloat16)
    grad_act = matmul(grad_down, ffn_full[1]).astype(jnp.bfloat16)
    gelu_back = jax.vjp(partial(jax.nn.gelu, approximate=False), hidden_pre)[1]
    grad_pre = gelu_back(grad_act.astype(jnp.float32))[0].astype(jnp.bfloat16)
    grad_first = grad_second + lax.psum(
        matmul_nt(grad_pre, ffn_full[0]).astype(jnp.bfloat16), "tensor"
    ).astype(jnp.float32)
    first_back = jax.vjp(layer_norm, first_in, vec_par[0], vec_par[1])[1]
    grad_first_in, gain_first, shift_first = first_back(grad_first)
    grad_branch = grad_first_in.astype(jnp.bfloat16)
    grad_mixed = matmul(grad_branch, attn_full[3]).astype(jnp.bfloat16)
    grad_mixed_seq = grad_mixed.reshape(seq_count, piece_len, local_width)
    grad_query, grad_keys_full, grad_values_full = attend_backward(
        query_seq,
        keys_full,
        values_full,
        segment_mb,
        random_mb,
        ctx_index,
        sparse_lse,
        top_lse,
        grad_mixed_seq,
    )
    grad_keys, grad_values = (
        lax.psum_scatter(
            grad_keys_full.astype(jnp.bfloat16), "ctx", scatter_dimension=1, tiled=True
        ).astype(jnp.float32),
        lax.psum_scatter(
            grad_values_full.astype(jnp.bfloat16), "ctx", scatter_dimension=1, tiled=True
        ).astype(jnp.float32),
    )
    grad_query_low = grad_query.reshape(-1, local_width).astype(jnp.bfloat16)
    grad_keys_low = grad_keys.reshape(-1, local_width).astype(jnp.bfloat16)
    grad_values_low = grad_values.reshape(-1, local_width).astype(jnp.bfloat16)
    into_tokens = (
        matmul_nt(grad_query_low, attn_full[0])
        + matmul_nt(grad_keys_low, attn_full[1])
        + matmul_nt(grad_values_low, attn_full[2])
    )
    grad_tokens = grad_first_in + lax.psum(into_tokens.astype(jnp.bfloat16), "tensor").astype(
        jnp.float32
    )
    attn_grad = jnp.stack(
        [
            matmul_tn(flat_rows, grad_query_low),
            matmul_tn(flat_rows, grad_keys_low),
            matmul_tn(flat_rows, grad_values_low),
            matmul_tn(grad_branch, mixed_low),
        ]
    )
    ffn_grad = jnp.stack([matmul_tn(first_low, grad_pre), matmul_tn(grad_down, hidden_low)])
    qv_grad = jnp.stack([column_sum(grad_query_low), column_sum(grad_values_low)])
    hid_grad = column_sum(grad_pre)
    vec_grad = jnp.stack(
        [
            gain_first,
            shift_first,
            gain_second,
            shift_second,
            column_sum(grad_branch),
            column_sum(grad_down),
        ]
    )
    return (
        result.astype(jnp.bfloat16).reshape(tokens_mb.shape),
        grad_tokens.reshape(tokens_mb.shape),
        (attn_grad, ffn_grad),
        (qv_grad, hid_grad, vec_grad),
    )


def body(
    tokens,
    cotangent,
    segments,
    rand_blocks,
    attn_w,
    attn_m,
    attn_v,
    ffn_w,
    ffn_m,
    ffn_v,
    qv_bias,
    qv_m,
    qv_v,
    hid_bias,
    hid_m,
    hid_v,
    vec_par,
    vec_m,
    vec_v,
):
    attn_cast = attn_w.astype(jnp.bfloat16)
    ffn_cast = ffn_w.astype(jnp.bfloat16)
    ctx_index = lax.axis_index("ctx")
    seq_count = tokens.shape[0] // MICRO
    results = []
    input_grads = []
    kept_attn = jnp.zeros((attn_w.shape[0], D, attn_w.shape[2]), jnp.float32)
    kept_ffn = jnp.zeros((ffn_w.shape[0], D, ffn_w.shape[2]), jnp.float32)
    small_acc = (jnp.zeros_like(qv_bias), jnp.zeros_like(hid_bias), jnp.zeros_like(vec_par))
    for micro_idx in range(MICRO):
        attn_full, ffn_full = (
            lax.all_gather(attn_cast, ("shard", "ctx"), axis=1, tiled=True),
            lax.all_gather(ffn_cast, ("shard", "ctx"), axis=1, tiled=True),
        )
        first_row = micro_idx * seq_count
        last_row = first_row + seq_count
        out_mb, grad_mb, big_grads, small_grads = micro_step(
            tokens[first_row:last_row],
            cotangent[first_row:last_row],
            segments[first_row:last_row],
            rand_blocks[first_row:last_row],
            attn_full,
            ffn_full,
            qv_bias,
            hid_bias,
            vec_par,
            ctx_index,
        )
        results.append(out_mb)
        input_grads.append(grad_mb)
        small_acc = jax.tree.map(jnp.add, small_acc, small_grads)
        kept_attn = kept_attn + big_grads[0]
        kept_ffn = kept_ffn + big_grads[1]
    reduced_attn, reduced_ffn = (
        lax.psum_scatter(kept_attn, ("shard", "ctx"), scatter_dimension=1, tiled=True),
        lax.psum_scatter(kept_ffn, ("shard", "ctx"), scatter_dimension=1, tiled=True),
    )
    qv_grad, hid_grad, vec_grad = lax.psum(
        (small_acc[0], small_acc[1], small_acc[2]), ("shard", "ctx")
    )
    attn_rates = jnp.array([2.0 / D**0.5] * 3 + [2.0 / (D // (4 * BLOCK)) ** 0.5], jnp.float32)[
        :, None, None
    ]
    ffn_rates = jnp.array([2.0 / D**0.5, 2.0 / FF**0.5], jnp.float32)[:, None, None]
    attn_moment, attn_square, attn_new = adam_update(
        attn_w, attn_m, attn_v, reduced_attn, attn_rates, decay_rate
    )
    ffn_moment, ffn_square, ffn_new = adam_update(
        ffn_w, ffn_m, ffn_v, reduced_ffn, ffn_rates, decay_rate
    )
    qv_moment, qv_square, qv_new = adam_update(qv_bias, qv_m, qv_v, qv_grad, 0.5, 0.0)
    hid_moment, hid_square, hid_new = adam_update(hid_bias, hid_m, hid_v, hid_grad, 0.5, 0.0)
    vec_moment, vec_square, vec_new = adam_update(vec_par, vec_m, vec_v, vec_grad, 0.5, 0.0)
    out_states = jnp.stack([attn_moment[3], attn_square[3]])
    output = jnp.concatenate(results, axis=0)
    grad_tokens = jnp.concatenate(input_grads, axis=0)
    return (
        output,
        grad_tokens,
        attn_moment[:3],
        attn_square[:3],
        out_states,
        attn_new,
        attn_new.astype(jnp.bfloat16),
        ffn_moment,
        ffn_square,
        ffn_new,
        ffn_new.astype(jnp.bfloat16),
        qv_moment,
        qv_square,
        qv_new,
        hid_moment,
        hid_square,
        hid_new,
        vec_moment,
        vec_square,
        vec_new,
    )


def solution(mesh):
    in_specs = (
        P("shard", "ctx", None),
        P("shard", "ctx", None),
        P("shard", None),
        P("shard", None, None),
        P(None, ("shard", "ctx"), "tensor"),
        P(None, ("shard", "ctx"), "tensor"),
        P(None, ("shard", "ctx"), "tensor"),
        P(None, ("shard", "ctx"), "tensor"),
        P(None, ("shard", "ctx"), "tensor"),
        P(None, ("shard", "ctx"), "tensor"),
        P(None, "tensor"),
        P(None, "tensor"),
        P(None, "tensor"),
        P("tensor"),
        P("tensor"),
        P("tensor"),
        P(),
        P(),
        P(),
    )
    out_specs = (
        P("shard", "ctx", None),
        P("shard", "ctx", None),
        P(None, ("shard", "ctx"), "tensor"),
        P(None, ("shard", "ctx"), "tensor"),
        P(None, ("shard", "ctx"), "tensor"),
        P(None, ("shard", "ctx"), "tensor"),
        P(None, ("shard", "ctx"), "tensor"),
        P(None, ("shard", "ctx"), "tensor"),
        P(None, ("shard", "ctx"), "tensor"),
        P(None, ("shard", "ctx"), "tensor"),
        P(None, ("shard", "ctx"), "tensor"),
        P(None, "tensor"),
        P(None, "tensor"),
        P(None, "tensor"),
        P("tensor"),
        P("tensor"),
        P("tensor"),
        P(),
        P(),
        P(),
    )
    return jax.shard_map(body, mesh=mesh, in_specs=in_specs, out_specs=out_specs, check_vma=False)
```

profile of v0, /device:TPU:0, one launch (start us, length us, event | category | flops | bytes accessed | tf_op | source)
XLA Modules:
  0.0 2403.4 jit_solution(2848705088836493000)
XLA Ops:
  14.0 24.9 %all-gather.7.cloned.1.call-done = bf16[4,768,192]{2,1,0:T(8,128)(2,1)} async-done(((bf16[4,96,192]{2,1,0:T(8,128)(2,1)}), bf16[4,768,192]{2,1,0:T(8,128)(2,1)}) %all-gather.7.cloned.1.call-update) | async-done | bytes 1179664 | tf_op jit(solution)/shard_map/all_gather | solution.py:437
  91.0 22.2 gather_fusion.5
  116.8 22.0 gather_fusion.3
  152.2 22.0 gather_fusion
  187.1 22.3 gather_fusion.2
  209.5 27.0 %reshape.604 = bf16[2,16,512,3,64]{4,3,2,1,0:T(4,128)(2,1)} reshape(bf16[256,12288]{1,0:T(8,128)(2,1)} %gather_fusion.2) | data formatting | bytes 12582912 | tf_op jit(solution)/shard_map/reshape | solution.py:91
  236.5 23.3 copy.236
  259.7 27.0 %reshape.601 = bf16[2,16,512,3,64]{4,3,2,1,0:T(4,128)(2,1)} reshape(bf16[256,12288]{1,0:T(8,128)(2,1)} %gather_fusion) | data formatting | bytes 12582912 | tf_op jit(solution)/shard_map/reshape | solution.py:95
  286.7 23.2 copy.237
  309.9 27.0 %reshape.615 = bf16[2,16,512,3,64]{4,3,2,1,0:T(4,128)(2,1)} reshape(bf16[256,12288]{1,0:T(8,128)(2,1)} %gather_fusion.3) | data formatting | bytes 12582912 | tf_op jit(solution)/shard_map/reshape | solution.py:95
  336.9 23.3 copy.252
  360.2 27.0 %reshape.618 = bf16[2,16,512,3,64]{4,3,2,1,0:T(4,128)(2,1)} reshape(bf16[256,12288]{1,0:T(8,128)(2,1)} %gather_fusion.5) | data formatting | bytes 12582912 | tf_op jit(solution)/shard_map/reshape | solution.py:91
  387.1 23.4 copy.251
  495.5 424.4 %all-reduce.18.cloned.1.call-done = (f32[2048,768]{1,0:T(8,128)}, f32[2048,768]{1,0:T(8,128)}) async-done(((f32[2048,768]{1,0:T(8,128)}, f32[2048,768]{1,0:T(8,128)}), (f32[2048,768]{1,0:T(8,128)}, f32[2048,768]{1,0:T(8,128)})) %all-reduce.18.cloned.1.call-update) | async-done | bytes 12582928 | tf_op jit(solution)/shard_map/psum | solution.py:317
  934.7 15.6 all-gather.13.cloned.1.call-done
  954.5 32.2 %multiply_convert_fusion.5 = (bf16[2048,768]{1,0:T(8,128)(2,1)S(1)}, f32[2048,768]{1,0:T(8,128)}, bf16[2048,768]{1,0:T(8,128)(2,1)S(1)}, f32[2048,768]{1,0:T(8,128)}, f32[2048,768]{1,0:T(8,128)}) fusion(f32[768]{0:T(1024)S(1)} %copy-done.112, f32[2048,768]{1,0:T(8,128)S(1)} %fusion.98, bf16[2048,768]{1,0:T(8,128)(2,1)S(1)} %copy-done.58, ...), kind=kOutput, calls=%fused_computation.142 | convolution fusion | flops 2623537152 | bytes 35786752 | tf_op jit(solution)/shard_map/dot_general | solution.py:25
  995.1 223.1 %all-reduce.24.cloned.1.call-done = (bf16[2048,768]{1,0:T(8,128)(2,1)}, bf16[2048,768]{1,0:T(8,128)(2,1)}) async-done(((bf16[2048,768]{1,0:T(8,128)(2,1)}, bf16[2048,768]{1,0:T(8,128)(2,1)}), (bf16[2048,768]{1,0:T(8,128)(2,1)}, bf16[2048,768]{1,0:T(8,128)(2,1)})) %all-reduce.24.cloned.1.call-update) | async-done | bytes 6291472 | tf_op jit(solution)/shard_map/psum | solution.py:324
  1282.5 220.1 %all-reduce.22.cloned.1.call-done = (bf16[2048,768]{1,0:T(8,128)(2,1)}, bf16[2048,768]{1,0:T(8,128)(2,1)}) async-done(((bf16[2048,768]{1,0:T(8,128)(2,1)}, bf16[2048,768]{1,0:T(8,128)(2,1)}), (bf16[2048,768]{1,0:T(8,128)(2,1)}, bf16[2048,768]{1,0:T(8,128)(2,1)})) %all-reduce.22.cloned.1.call-update) | async-done | bytes 6291472 | tf_op jit(solution)/shard_map/psum | solution.py:338
  1502.6 14.2 multiply_reduce_fusion.7
  1537.8 13.2 multiply_reduce_fusion.4
  1576.7 28.8 %copy.279 = f32[2,16,512,3,64]{4,3,2,1,0:T(4,128)} copy(f32[2,16,512,3,64]{2,4,3,1,0:T(8,128)} %multiply_bitcast_fusion) | data formatting | bytes 25165824 | tf_op jit(solution)/shard_map/mul | solution.py:213
  1605.5 34.0 %reshape.630 = f32[2,128,12288]{2,1,0:T(8,128)} reshape(f32[2,16,512,3,64]{4,3,2,1,0:T(4,128)} %copy.279) | data formatting | bytes 25165824 | tf_op jit(solution)/shard_map/reshape | solution.py:227
  1650.3 30.0 %conditional.7 = (f32[2,1024,192]{1,2,0:T(8,128)}, f32[2,2048,192]{2,1,0:T(8,128)}, f32[2,2048,192]{2,1,0:T(8,128)}) conditional(s32[]{:T(128)} %convert_element_type.296, () %tuple.54, (bf16[2,128,3,64]{1,3,2,0:T(8,128)(2,1)S(1)}, bf16[2,2048,3,64]{1,3,2,0:T(8,128)(2,1)}, f32[2,3,128,1]{2,1,0,3:T(4,128)S(1)}, bf16[2048,192]{0,1:T(8,128)(2,1)}, ...), branch_computations={%region_44.45_spmd, %region_45.47_spmd} | conditional | flops 1026342144 | bytes 119159912 | solution.py:281
  1695.1 29.2 %copy.282 = f32[2,16,512,3,64]{4,3,2,1,0:T(4,128)} copy(f32[2,16,512,3,64]{2,4,3,1,0:T(8,128)} %fusion.75) | data formatting | bytes 25165824 | tf_op jit(solution)/shard_map/sbhqk,sbqhd->sbkhd/transpose | solution.py:218
  1724.3 34.0 %reshape.632 = f32[2,128,12288]{2,1,0:T(8,128)} reshape(f32[2,16,512,3,64]{4,3,2,1,0:T(4,128)} %copy.282) | data formatting | bytes 25165824 | tf_op jit(solution)/shard_map/reshape | solution.py:233
  1810.8 28.8 %copy.264 = f32[2,16,512,3,64]{4,3,2,1,0:T(4,128)} copy(f32[2,16,512,3,64]{2,4,3,1,0:T(8,128)} %multiply_bitcast_fusion.1) | data formatting | bytes 25165824 | tf_op jit(solution)/shard_map/mul | solution.py:213
  1839.6 34.0 %reshape.623 = f32[2,128,12288]{2,1,0:T(8,128)} reshape(f32[2,16,512,3,64]{4,3,2,1,0:T(4,128)} %copy.264) | data formatting | bytes 25165824 | tf_op jit(solution)/shard_map/reshape | solution.py:227
  1887.6 32.5 %conditional.6 = (f32[2,1024,192]{1,2,0:T(8,128)S(1)}, f32[2,2048,192]{2,1,0:T(8,128)}, f32[2,2048,192]{2,1,0:T(8,128)}) conditional(s32[]{:T(128)} %convert_element_type.296, () %tuple.52, (bf16[2,128,3,64]{1,3,2,0:T(8,128)(2,1)S(1)}, bf16[2,2048,3,64]{1,3,2,0:T(8,128)(2,1)}, f32[2,3,128,1]{2,1,0,3:T(4,128)}, bf16[2048,192]{0,1:T(8,128)(2,1)S(1)}, ...), branch_computations={%region_32.33_spmd, %region_33.35_spmd} | conditional | flops 1026342144 | bytes 119159912 | solution.py:281
  1936.4 28.8 %copy.267 = f32[2,16,512,3,64]{4,3,2,1,0:T(4,128)} copy(f32[2,16,512,3,64]{2,4,3,1,0:T(8,128)} %fusion.72) | data formatting | bytes 25165824 | tf_op jit(solution)/shard_map/sbhqk,sbqhd->sbkhd/transpose | solution.py:218
  1965.3 34.0 %reshape.625 = f32[2,128,12288]{2,1,0:T(8,128)} reshape(f32[2,16,512,3,64]{4,3,2,1,0:T(4,128)} %copy.267) | data formatting | bytes 25165824 | tf_op jit(solution)/shard_map/reshape | solution.py:233
  2130.9 23.0 all-reduce.8
  2165.7 209.4 %all-reduce.20.cloned.1.call-done = (bf16[2048,768]{1,0:T(8,128)(2,1)}, bf16[2048,768]{1,0:T(8,128)(2,1)}) async-done(((bf16[2048,768]{1,0:T(8,128)(2,1)}, bf16[2048,768]{1,0:T(8,128)(2,1)}), (bf16[2048,768]{1,0:T(8,128)(2,1)}, bf16[2048,768]{1,0:T(8,128)(2,1)})) %all-reduce.20.cloned.1.call-update) | async-done | bytes 6291472 | tf_op jit(solution)/shard_map/psum | solution.py:373
  (613 shorter events, 657.5 us)
Async XLA Ops:
  7.2 31.7 %all-gather.7.cloned.1.call-start = ((), (), s32[]{:S(2)}) async-start(), calls=%async_computation.6 | async-start | bytes 1769472 | tf_op jit(solution)/shard_map/all_gather | solution.py:437
  9.0 78.2 %all-gather.15.cloned.1.call-start = ((), (), s32[]{:S(2)}) async-start(), calls=%async_computation.10 | async-start | bytes 3145728 | tf_op jit(solution)/shard_map/all_gather | solution.py:305
  14.0 37.8 %copy-start.18 = (bf16[2,1024,768]{2,1,0:T(8,128)(2,1)}, bf16[2,1024,768]{2,1,0:T(8,128)(2,1)S(1)}, u32[]{:S(2)}) copy-start(bf16[2,1024,768]{2,1,0:T(8,128)(2,1)S(1)} %get-tuple-element.317) | copy-start | bytes 9437188
  14.0 31.3 %copy-start.107 = (f32[2,192]{1,0:T(2,128)S(1)}, f32[2,192]{1,0:T(2,128)}, u32[]{:S(2)}) copy-start(f32[2,192]{1,0:T(2,128)} %param.39) | copy-start | bytes 4612
  45.2 68.0 %all-gather.17.cloned.1.call-start = ((), (), s32[]{:S(2)}) async-start(), calls=%async_computation.11 | async-start | bytes 3145728 | tf_op jit(solution)/shard_map/all_gather | solution.py:308
  51.6 96.7 %all-gather.11.cloned.1.call-start = ((), (), s32[]{:S(2)}) async-start(), calls=%async_computation.8 | async-start | bytes 3145728 | tf_op jit(solution)/shard_map/all_gather | solution.py:308
  57.1 126.3 %all-gather.9.cloned.1.call-start = ((), (), s32[]{:S(2)}) async-start(), calls=%async_computation.7 | async-start | bytes 3145728 | tf_op jit(solution)/shard_map/all_gather | solution.py:305
  64.5 855.4 %all-reduce.18.cloned.1.call-start = ((), (), s32[]{:S(2)}) async-start(), calls=%async_computation.18 | async-start | bytes 25165824 | tf_op jit(solution)/shard_map/psum | solution.py:317
  72.8 347.8 %copy-start.13 = (pred[2,16,64,512]{3,2,1,0:T(8,128)(4,1)}, pred[2,16,64,512]{3,2,1,0:T(8,128)(4,1)S(1)}, u32[]{:S(2)}) copy-start(pred[2,16,64,512]{3,2,1,0:T(8,128)(4,1)S(1)} %or_and_fusion) | copy-start | bytes 3145732
  492.9 427.0 %copy-start.19 = (bf16[2,1024,768]{2,1,0:T(8,128)(2,1)S(1)}, bf16[2,1024,768]{2,1,0:T(8,128)(2,1)}, u32[]{:S(2)}) copy-start(bf16[2,1024,768]{2,1,0:T(8,128)(2,1)} %copy-done.18) | copy-start | bytes 9437188
  492.9 457.4 %all-gather.13.cloned.1.call-start = ((), (), s32[]{:S(2)}) async-start(), calls=%async_computation.9 | async-start | bytes 2654208 | tf_op jit(solution)/shard_map/all_gather | solution.py:438
  495.0 723.2 %all-reduce.24.cloned.1.call-start = ((), (), s32[]{:S(2)}) async-start(), calls=%async_computation.21 | async-start | bytes 12582912 | tf_op jit(solution)/shard_map/psum | solution.py:324
  954.5 32.2 %copy-start.128 = (f32[2048,768]{1,0:T(8,128)}, f32[2048,768]{1,0:T(8,128)S(1)}, u32[]{:S(2)}) copy-start(f32[2048,768]{1,0:T(8,128)S(1)} %fusion.98) | copy-start | bytes 18874372
  994.8 234.2 %slice-start.11 = ((s8[6291456]{0:T(1024)(128)(4,1)}), s8[2097152]{0:T(1024)(128)(4,1)S(1)}, s32[]{:S(2)}) async-start(s8[6291456]{0:T(1024)(128)(4,1)} %bitcast.352), calls=%async_computation.33 | async-start | bytes 4194304
  994.8 507.7 %all-reduce.22.cloned.1.call-start = ((), (), s32[]{:S(2)}) async-start(), calls=%async_computation.20 | async-start | bytes 12582912 | tf_op jit(solution)/shard_map/psum | solution.py:338
  1280.2 236.6 %slice-start.3 = ((s8[6291456]{0:T(1024)(128)(4,1)}), s8[2097152]{0:T(1024)(128)(4,1)S(1)}, s32[]{:S(2)}) async-start(s8[6291456]{0:T(1024)(128)(4,1)} %bitcast.344), calls=%async_computation.25 | async-start | bytes 4194304
  1280.3 789.5 %reduce-scatter.13.cloned.1.call-start = ((), (), s32[]{:S(2)}) async-start(), calls=%async_computation.14 | async-start | bytes 3145728 | tf_op jit(solution)/shard_map/reduce_scatter | solution.py:358
  1560.1 125.6 %copy-start.80 = (f32[2048]{0:T(1024)}, f32[2048]{0:T(1024)S(1)}, u32[]{:S(2)}) copy-start(f32[2048]{0:T(1024)S(1)} %negate_multiply_fusion.4) | copy-start | bytes 24580
  1685.6 388.1 %reduce-scatter.15.cloned.1.call-start = ((), (), s32[]{:S(2)}) async-start(), calls=%async_computation.15 | async-start | bytes 3145728 | tf_op jit(solution)/shard_map/reduce_scatter | solution.py:361
  1695.1 82.3 %copy-start.26 = (bf16[2,16,64,3,64]{2,1,0,4,3:T(8,128)(2,1)}, bf16[2,16,64,3,64]{2,1,0,4,3:T(8,128)(2,1)S(1)}, u32[]{:S(2)}) copy-start(bf16[2,16,64,3,64]{2,1,0,4,3:T(8,128)(2,1)S(1)} %reshape.621) | copy-start | bytes 2359300
  1790.5 287.0 %reduce-scatter.9.cloned.1.call-start = ((), (), s32[]{:S(2)}) async-start(), calls=%async_computation.12 | async-start | bytes 3145728 | tf_op jit(solution)/shard_map/reduce_scatter | solution.py:358
  1839.6 34.0 %copy-start.91 = (s32[2,128]{1,0:T(2,128)S(1)}, s32[2,128]{1,0:T(2,128)}, u32[]{:S(2)}) copy-start(s32[2,128]{1,0:T(2,128)} %min.32) | copy-start | bytes 3076
  1926.6 154.9 %reduce-scatter.11.cloned.1.call-start = ((), (), s32[]{:S(2)}) async-start(), calls=%async_computation.13 | async-start | bytes 3145728 | tf_op jit(solution)/shard_map/reduce_scatter | solution.py:361
  2015.5 110.4 %reduce-scatter.17.cloned.1.call-start = ((), (), s32[]{:S(2)}) async-start(), calls=%async_computation.16 | async-start | bytes 5308416 | tf_op jit(solution)/shard_map/reduce_scatter | solution.py:461
  2032.0 123.8 %reduce-scatter.19.cloned.1.call-start = ((), (), s32[]{:S(2)}) async-start(), calls=%async_computation.17 | async-start | bytes 2654208
  2095.0 280.2 %all-reduce.20.cloned.1.call-start = ((), (), s32[]{:S(2)}) async-start(), calls=%async_computation.19 | async-start | bytes 12582912 | tf_op jit(solution)/shard_map/psum | solution.py:373
  2123.9 31.2 %copy-start.77 = (f32[6,768]{1,0:T(8,128)S(1)}, f32[6,768]{1,0:T(8,128)}, u32[]{:S(2)}) copy-start(f32[6,768]{1,0:T(8,128)} %param.45) | copy-start | bytes 55300
  2123.9 31.2 %copy-start.92 = (f32[6,768]{1,0:T(8,128)S(1)}, f32[6,768]{1,0:T(8,128)}, u32[]{:S(2)}) copy-start(f32[6,768]{1,0:T(8,128)} %param.47) | copy-start | bytes 55300
  2123.9 34.1 %copy-start.65 = (f32[4,96,192]{1,2,0:T(8,128)S(1)}, f32[4,96,192]{1,2,0:T(8,128)}, u32[]{:S(2)}) copy-start(f32[4,96,192]{1,2,0:T(8,128)} %copy.292) | copy-start | bytes 884740
  2123.9 34.0 %copy-start.66 = (f32[4,96,192]{1,2,0:T(8,128)S(1)}, f32[4,96,192]{1,2,0:T(8,128)}, u32[]{:S(2)}) copy-start(f32[4,96,192]{1,2,0:T(8,128)} %copy.290) | copy-start | bytes 884740
  2129.0 246.1 %copy-start.81 = (f32[2048]{0:T(1024)S(1)}, f32[2048]{0:T(1024)}, u32[]{:S(2)}) copy-start(f32[2048]{0:T(1024)} %copy-done.80) | copy-start | bytes 24580
  2158.0 224.3 %slice-start.9 = ((s8[6291456]{0:T(1024)(128)(4,1)}), s8[2097152]{0:T(1024)(128)(4,1)S(1)}, s32[]{:S(2)}) async-start(s8[6291456]{0:T(1024)(128)(4,1)} %bitcast.350), calls=%async_computation.31 | async-start | bytes 4194304
  (130 other events, 1074.5 us)
Sparse Core Ops, SparseCore 0:
  10.5 28.3 all-gather.6
  45.3 33.1 all-gather.14
  80.0 33.1 all-gather.16
  115.1 33.1 all-gather.10
  150.3 33.1 all-gather.8
  493.1 426.7 all-reduce.17
  922.4 27.9 all-gather.12
  995.0 223.1 all-reduce.23
  1280.4 222.1 all-reduce.21
  1685.7 29.8 reduce-scatter.12
  1790.6 29.9 reduce-scatter.14
  1926.8 29.9 reduce-scatter.8
  2015.6 29.7 reduce-scatter.10
  2049.2 53.8 reduce-scatter.16
  2106.7 42.9 reduce-scatter.18
  2151.9 223.1 all-reduce.19
where the time goes:
time: 2420 us; the launch traced here: 2400 us
  waiting for transfers between devices  1140 us (47%)
  local copies, waits for them, and re-layouts  716 us (30%)
  matrix products  322 us (13%)
  other arithmetic  187 us (8%)
    psum x1, waiting for transfers between devices, micro_step(): branch = lax.psum(matmul_nt(mixed_low, attn_full[3]), 'tensor') + vec_par[4]  424 us
    psum x1, waiting for transfers between devices, micro_step(): lax.psum(matmul_nt(hidden_low, ffn_full[1]).astype(jnp.bfloat16), 'tensor')  223 us
    psum x1, waiting for transfers between devices, micro_step(): lax.psum(matmul_nt(grad_pre, ffn_full[0]).astype(jnp.bfloat16), 'tensor')  220 us
    psum x1, waiting for transfers between devices, micro_step(): lax.psum(into_tokens.astype(jnp.bfloat16), 'tensor').astype(jnp.float32)  209 us
    reshape x4, local copies, waits for them, and re-layouts, sparse_setup(): key_rows.reshape(seq_count, local_blocks, -1, local_heads, HEAD_DIM)  101 us
    reshape x4, local copies, waits for them, and re-layouts, sparse_setup(): value_rows.reshape(seq_count, local_blocks, -1, local_heads, HEAD_DIM)  100 us
    gather x8, local copies, waits for them, and re-layouts, take_blocks(): block_table[picked_ids]  92.6 us
    dot_general x12, matrix products, matmul(): return jnp.dot(left, right, preferred_element_type=jnp.float32)  81.8 us
  transfers between devices with their start and end apart: 16, of which 8 were waited for; matrix products, arithmetic and copies ran while one was open for 24% of the time, Pallas kernels for 0%

commit v1 on v0

v1 whole, which is shorter than its diff:
```python
from functools import partial

import jax
import jax.numpy as jnp
from jax import lax
from jax.experimental import pallas as pl
from jax.experimental.pallas import tpu as pltpu
from jax.sharding import PartitionSpec as P

D = 768
HEAD_DIM = 64
FF = 3072
BLOCK = 64
STEP = 5
GROUP = 4 * HEAD_DIM
GROUPS = D // GROUP
ROWS = 4 * BLOCK
LISTED = 8
KEYS = LISTED * BLOCK
VMEM_LIMIT = 60 * 2**20

beta_first = 0.9
beta_second = 0.999
adam_eps = 1e-08
decay_rate = 0.01
norm_eps = 1e-06
neg_large = -1e30

f32 = jnp.float32
bf16 = jnp.bfloat16


def matmul(left, right):
    return jnp.dot(left, right, preferred_element_type=f32)


def matmul_tn(left, right):
    return lax.dot_general(left, right, (((0,), (0,)), ((), ())), preferred_element_type=f32)


def matmul_nt(left, right):
    return lax.dot_general(left, right, (((1,), (1,)), ((), ())), preferred_element_type=f32)


def column_sum(array_in):
    return jnp.sum(array_in.astype(f32), axis=0)


def adam_update(weight, moment, square, gradient, step_rates, decay_on):
    moment_new = beta_first * moment + (1.0 - beta_first) * gradient
    square_new = beta_second * square + (1.0 - beta_second) * gradient * gradient
    step_ratio = (
        moment_new
        / (1.0 - beta_first**STEP)
        / (jnp.sqrt(square_new / (1.0 - beta_second**STEP)) + adam_eps)
    )
    weight_new = weight - step_rates * (step_ratio + decay_on * weight)
    return (moment_new, square_new, weight_new)


def same_head():
    row_head = lax.broadcasted_iota(jnp.int32, (ROWS, GROUP), 0) // BLOCK
    col_head = lax.broadcasted_iota(jnp.int32, (ROWS, GROUP), 1) // HEAD_DIM
    return row_head == col_head


def spread_heads(block, keep):
    stacked = jnp.concatenate([block] * 4, axis=0)
    return jnp.where(keep, stacked, jnp.zeros_like(stacked))


def fold_heads(full, keep):
    kept = jnp.where(keep, full, 0.0)
    return sum(kept[h * BLOCK : (h + 1) * BLOCK] for h in range(4))


def load_keys(k_all, v_all, seq, k_buf, v_buf, sems):
    return [
        pltpu.make_async_copy(k_all.at[seq], k_buf, sems.at[0]),
        pltpu.make_async_copy(v_all.at[seq], v_buf, sems.at[1]),
    ]


def picked_rows(buf, spots, cols):
    return jnp.concatenate([buf[at, :, cols] for at in spots], axis=0)


def chunk_rows(buf, i, cols):
    blocks = buf[pl.ds(i * LISTED, LISTED), :, cols]
    return blocks.reshape(KEYS, GROUP)


def listed_blocks(rand, base, blk, first, own, total):
    one = lambda condition: condition.astype(jnp.int32)
    me = first + blk
    ids = [me - 1, me, me + 1, me * 0, me * 0 + 1] + [rand[base + n] for n in range(LISTED - 5)]
    spots, unused, common = [], [], []
    for n, block in enumerate(ids):
        out = one(block < 0) + one(block >= total)
        for earlier in ids[:n]:
            out = out + one(block == earlier)
        out = lax.min(out, jnp.int32(1))
        at = lax.max(jnp.int32(0), lax.min(block, jnp.int32(total - 1))) - first + own
        spots.append(at + total * one(at < 0))
        unused.append(out)
        common.append(one(block < 2) * (1 - out))
    return spots, unused, common


def code_rows(tab_ref, spots, unused, common):
    low_half = lax.broadcasted_iota(jnp.int32, (1, 2 * BLOCK), 1) < BLOCK

    def one(n):
        plain = (1 - unused[n] - common[n]).astype(f32)
        return tab_ref[spots[n]] * plain - (unused[n] + 2 * common[n]).astype(f32)

    return [jnp.where(low_half, one(n), one(n + 1)) for n in range(0, LISTED, 2)]


def column_of(row):
    return jnp.broadcast_to(row, (2 * BLOCK, 2 * BLOCK)).T


def mask_bias(document, code):
    return jnp.where((document == code) | (code == -2.0), 0.0, neg_large)


def row_of(column):
    return jnp.broadcast_to(column, (ROWS, 2 * BLOCK)).T[0:1, :]


def forward_block(q_ref, out_ref, lse_ref, k_buf, v_buf, s_buf, tab_ref, rand, base, blk, first, own):
    keep = same_head()
    total_blocks = k_buf.shape[0]
    chunks = total_blocks // LISTED
    is_global = first + blk < 2

    @pl.when(jnp.logical_not(is_global))
    def _():
        spots, unused, common = listed_blocks(rand, base, blk, first, own, total_blocks)
        mine = column_of(tab_ref[own + blk])[:BLOCK]
        mine = jnp.concatenate([mine] * 4, axis=0)
        codes = code_rows(tab_ref, spots, unused, common)
        bias = jnp.concatenate([mask_bias(mine, code) for code in codes], axis=1)
        for g in range(GROUPS):
            cols = slice(g * GROUP, (g + 1) * GROUP)
            q_full = spread_heads(q_ref[:, cols], keep)
            scores = matmul_nt(q_full, picked_rows(k_buf, spots, cols)) + bias
            largest = jnp.max(scores, axis=-1, keepdims=True)
            weights = jnp.exp(scores - largest)
            total = jnp.sum(weights, axis=-1, keepdims=True)
            full = matmul(weights.astype(bf16), picked_rows(v_buf, spots, cols))
            out_ref[:, cols] = fold_heads(full * (1.0 / total), keep).astype(bf16)
            lse_ref[g : g + 1, :] = row_of(largest + jnp.log(total))

    @pl.when(is_global)
    def _():
        for g in range(GROUPS):
            cols = slice(g * GROUP, (g + 1) * GROUP)
            q_full = spread_heads(q_ref[:, cols], keep)

            def score_chunk(i, largest):
                scores = matmul_nt(q_full, chunk_rows(k_buf, i, cols))
                s_buf[i] = scores
                return jnp.maximum(largest, jnp.max(scores, axis=-1, keepdims=True))

            largest = lax.fori_loop(0, chunks, score_chunk, jnp.full((ROWS, 1), neg_large, f32))

            def mix_chunk(i, carry):
                total, full = carry
                weights = jnp.exp(s_buf[i] - largest)
                total = total + jnp.sum(weights, axis=-1, keepdims=True)
                return total, full + matmul(weights.astype(bf16), chunk_rows(v_buf, i, cols))

            total, full = lax.fori_loop(
                0, chunks, mix_chunk, (jnp.zeros((ROWS, 1), f32), jnp.zeros((ROWS, GROUP), f32))
            )
            out_ref[:, cols] = fold_heads(full * (1.0 / total), keep).astype(bf16)
            lse_ref[g : g + 1, :] = row_of(largest + jnp.log(total))


def forward_kernel(
    rand, meta, q_ref, tab_ref, k_all, v_all, out_ref, lse_ref, k_buf, v_buf, s_buf, sems
):
    seq, blk = pl.program_id(0), pl.program_id(1)
    nb = pl.num_programs(1)

    @pl.when(blk == 0)
    def _():
        copies = load_keys(k_all, v_all, seq, k_buf, v_buf, sems)
        for c in copies:
            c.start()
        for c in copies:
            c.wait()

    base = (seq * nb + blk) * (LISTED - 5)
    forward_block(
        q_ref, out_ref, lse_ref, k_buf, v_buf, s_buf, tab_ref, rand, base, blk, meta[0], meta[1]
    )


def back_tile(k_rows, v_rows, q_full, go_full, bias, lse, centre):
    scores = matmul_nt(k_rows, q_full)
    if bias is not None:
        scores = scores + bias
    probs = jnp.exp(scores - lse)
    grad_probs = matmul_nt(v_rows, go_full)
    grad_scores = (probs * (grad_probs - centre)).astype(bf16)
    dv_rows = matmul(probs.astype(bf16), go_full)
    dk_rows = matmul(grad_scores, q_full)
    return matmul_tn(grad_scores, k_rows), dk_rows, dv_rows


def backward_kernel(
    n_out, rand, meta, q_ref, go_ref, mixed_ref, lse_ref, tab_ref, k_all, v_all, dq_ref, *rest
):
    dk_refs, dv_refs = rest[:n_out], rest[n_out : 2 * n_out]
    k_buf, v_buf, dk_acc, dv_acc, sems = rest[2 * n_out :]
    seq, blk = pl.program_id(0), pl.program_id(1)
    nb = pl.num_programs(1)
    total_blocks = k_buf.shape[0]
    chunks = total_blocks // LISTED

    @pl.when(blk == 0)
    def _():
        copies = load_keys(k_all, v_all, seq, k_buf, v_buf, sems)
        for c in copies:
            c.start()
        dk_acc[...] = jnp.zeros_like(dk_acc)
        dv_acc[...] = jnp.zeros_like(dv_acc)
        for c in copies:
            c.wait()

    keep = same_head()
    is_global = meta[0] + blk < 2
    base = (seq * nb + blk) * (LISTED - 5)

    def operands(g):
        cols = slice(g * GROUP, (g + 1) * GROUP)
        q_full = spread_heads(q_ref[:, cols], keep)
        go_full = spread_heads(go_ref[:, cols], keep)
        mixed = jnp.concatenate([mixed_ref[:, cols]] * 4, axis=0)
        product = go_full.astype(f32) * mixed.astype(f32)
        centre = row_of(jnp.sum(product, axis=-1, keepdims=True))
        return cols, q_full, go_full, lse_ref[g : g + 1, :], centre

    @pl.when(jnp.logical_not(is_global))
    def _():
        spots, unused, common = listed_blocks(rand, base, blk, meta[0], meta[1], total_blocks)
        stores = [at + (total_blocks - at) * out for at, out in zip(spots, unused)]
        own = tab_ref[meta[1] + blk]
        codes = code_rows(tab_ref, spots, unused, common)
        bias = jnp.concatenate([mask_bias(own, column_of(code)) for code in codes], axis=0)
        bias = jnp.concatenate([bias, bias], axis=1)
        for g in range(GROUPS):
            cols, q_full, go_full, lse, centre = operands(g)
            k_rows, v_rows = picked_rows(k_buf, spots, cols), picked_rows(v_buf, spots, cols)
            dq_full, dk_rows, dv_rows = back_tile(
                k_rows, v_rows, q_full, go_full, bias, lse, centre
            )
            dq_ref[:, cols] = (fold_heads(dq_full, keep) * 0.125).astype(bf16)
            places = [pl.ds(pl.multiple_of(at * BLOCK, BLOCK), BLOCK) for at in stores]
            dk_old = [dk_acc[at, cols] for at in places]
            dv_old = [dv_acc[at, cols] for at in places]
            for n, at in enumerate(places):
                own_rows = slice(n * BLOCK, (n + 1) * BLOCK)
                dk_acc[at, cols] = dk_old[n] + dk_rows[own_rows]
                dv_acc[at, cols] = dv_old[n] + dv_rows[own_rows]

    @pl.when(is_global)
    def _():
        for g in range(GROUPS):
            cols, q_full, go_full, lse, centre = operands(g)

            def chunk_back(i, dq_full):
                rows = pl.ds(pl.multiple_of(i * KEYS, KEYS), KEYS)
                dq_now, dk_rows, dv_rows = back_tile(
                    chunk_rows(k_buf, i, cols),
                    chunk_rows(v_buf, i, cols),
                    q_full,
                    go_full,
                    None,
                    lse,
                    centre,
                )
                dk_acc[rows, cols] += dk_rows
                dv_acc[rows, cols] += dv_rows
                return dq_full + dq_now

            dq_full = lax.fori_loop(0, chunks, chunk_back, jnp.zeros((ROWS, GROUP), f32))
            dq_ref[:, cols] = (fold_heads(dq_full, keep) * 0.125).astype(bf16)

    @pl.when(blk == nb - 1)
    def _():
        row = 0
        for dk_ref, dv_ref in zip(dk_refs, dv_refs):
            rows = dk_ref.shape[0]
            dk_ref[...] = dk_acc[row : row + rows].astype(bf16)
            dv_ref[...] = dv_acc[row : row + rows].astype(bf16)
            row += rows


def attention_tables(segments, random, piece, nb, own_first):
    seq_count, length = segments.shape
    total = length // BLOCK
    first = piece * nb
    rand = lax.dynamic_slice_in_dim(random, first, nb, 1).reshape(-1)
    table = segments.reshape(seq_count, total, BLOCK).astype(f32)
    table = jnp.concatenate([table, table], axis=2)[:, :, None, :]
    if own_first:
        table = lax.dynamic_slice_in_dim(jnp.concatenate([table, table], axis=1), first, total, 1)
    meta = jnp.stack([first, jnp.zeros_like(first) if own_first else first]).astype(jnp.int32)
    return rand, meta, table


def as_blocks(rows):
    return rows.reshape(rows.shape[0], -1, BLOCK, D)


def attend(tables, q, keys, values):
    rand, meta, table = tables
    seq_count, piece_len, _ = q.shape
    nb = piece_len // BLOCK
    length = keys.shape[1]
    any_spec = pl.BlockSpec(memory_space=pl.ANY)
    row_spec = pl.BlockSpec((None, BLOCK, D), lambda s, b, *_: (s, b, 0))
    return pl.pallas_call(
        forward_kernel,
        out_shape=[
            jax.ShapeDtypeStruct(q.shape, bf16),
            jax.ShapeDtypeStruct((seq_count, nb, 8, ROWS), f32),
        ],
        grid_spec=pltpu.PrefetchScalarGridSpec(
            num_scalar_prefetch=2,
            grid=(seq_count, nb),
            in_specs=[
                row_spec,
                pl.BlockSpec((None,) + table.shape[1:], lambda s, b, *_: (s, 0, 0, 0)),
                any_spec,
                any_spec,
            ],
            out_specs=[
                row_spec,
                pl.BlockSpec((None, None, 8, ROWS), lambda s, b, *_: (s, b, 0, 0)),
            ],
            scratch_shapes=[
                pltpu.VMEM((length // BLOCK, BLOCK, D), bf16),
                pltpu.VMEM((length // BLOCK, BLOCK, D), bf16),
                pltpu.VMEM((length // KEYS, ROWS, KEYS), f32),
                pltpu.SemaphoreType.DMA((2,)),
            ],
        ),
        compiler_params=pltpu.CompilerParams(vmem_limit_bytes=VMEM_LIMIT),
        name="attend",
    )(rand, meta, q, table, as_blocks(keys), as_blocks(values))


def attend_back(tables, q, grad_mixed, mixed, lse, keys, values, pieces):
    rand, meta, table = tables
    seq_count, piece_len, _ = q.shape
    nb = piece_len // BLOCK
    length = keys.shape[1]
    any_spec = pl.BlockSpec(memory_space=pl.ANY)
    row_spec = pl.BlockSpec((None, BLOCK, D), lambda s, b, *_: (s, b, 0))
    part_specs = [pl.BlockSpec((None, rows, D), lambda s, b, *_: (s, 0, 0)) for rows in pieces]
    part_shapes = [jax.ShapeDtypeStruct((seq_count, rows, D), bf16) for rows in pieces]
    out = pl.pallas_call(
        partial(backward_kernel, len(pieces)),
        out_shape=[jax.ShapeDtypeStruct(q.shape, bf16)] + part_shapes * 2,
        grid_spec=pltpu.PrefetchScalarGridSpec(
            num_scalar_prefetch=2,
            grid=(seq_count, nb),
            in_specs=[
                row_spec,
                row_spec,
                row_spec,
                pl.BlockSpec((None, None, 8, ROWS), lambda s, b, *_: (s, b, 0, 0)),
                pl.BlockSpec((None,) + table.shape[1:], lambda s, b, *_: (s, 0, 0, 0)),
                any_spec,
                any_spec,
            ],
            out_specs=[row_spec] + part_specs * 2,
            scratch_shapes=[
                pltpu.VMEM((length // BLOCK, BLOCK, D), bf16),
                pltpu.VMEM((length // BLOCK, BLOCK, D), bf16),
                pltpu.VMEM((length + BLOCK, D), f32),
                pltpu.VMEM((length + BLOCK, D), f32),
                pltpu.SemaphoreType.DMA((2,)),
            ],
        ),
        compiler_params=pltpu.CompilerParams(vmem_limit_bytes=VMEM_LIMIT),
        cost_estimate=pl.CostEstimate(
            flops=seq_count * nb * GROUPS * 10 * ROWS * KEYS * GROUP,
            bytes_accessed=seq_count * (3 * piece_len + 4 * length) * D * 2,
            transcendentals=seq_count * nb * GROUPS * ROWS * KEYS,
        ),
        name="attend_back",
    )(rand, meta, q, grad_mixed, mixed, lse, table, as_blocks(keys), as_blocks(values))
    return out[0], out[1 : 1 + len(pieces)], out[1 + len(pieces) :]


def norm_parts(hidden):
    centred = hidden - jnp.mean(hidden, axis=-1, keepdims=True)
    scale = lax.rsqrt(jnp.mean(centred * centred, axis=-1, keepdims=True) + norm_eps)
    return centred * scale, scale


def norm_back(grad, unit, scale, gain):
    inner = grad * gain
    return scale * (
        inner
        - jnp.mean(inner, axis=-1, keepdims=True)
        - unit * jnp.mean(inner * unit, axis=-1, keepdims=True)
    )


def gelu_and_slope(pre):
    bell = jnp.exp(-0.5 * pre * pre)
    t = 1.0 / (1.0 + (0.3275911 * 0.5**0.5) * jnp.abs(pre))
    poly = 0.5 * 1.061405429
    for coefficient in (-1.453152027, 1.421413741, -0.284496736, 0.254829592):
        poly = poly * t + 0.5 * coefficient
    tail = poly * t * bell
    phi = jnp.where(pre >= 0.0, 1.0 - tail, tail)
    return pre * phi, phi + pre * bell * 0.3989422804014327


def column_total(array):
    return jnp.sum(array.astype(f32), axis=0, keepdims=True)


def up_kernel(
    chunk,
    x_ref,
    mixed_ref,
    cot_ref,
    wo_ref,
    w1_ref,
    w2_ref,
    hid_ref,
    vec_ref,
    act_ref,
    slope_ref,
    h1_ref,
    res_ref,
    gs_ref,
    sums_ref,
    low,
    down,
):
    step = pl.program_id(0)
    chunks = x_ref.shape[0] // chunk

    @pl.when(step == 0)
    def _():
        @pl.loop(0, chunks)
        def _(i):
            rows = pl.ds(pl.multiple_of(i * chunk, chunk), chunk)
            h1 = x_ref[rows, :].astype(f32) + matmul_nt(mixed_ref[rows, :], wo_ref[...])
            h1 = h1 + vec_ref[4:5, :]
            h1_ref[rows, :] = h1
            unit, _scale = norm_parts(h1)
            low[rows, :] = (unit * vec_ref[0:1, :] + vec_ref[1:2, :]).astype(bf16)
            down[rows, :] = jnp.zeros((chunk, D), f32)

    for i in range(chunks):
        rows = slice(i * chunk, (i + 1) * chunk)
        pre = matmul(low[rows, :], w1_ref[...]) + hid_ref[...]
        act, slope = gelu_and_slope(pre)
        act = act.astype(bf16)
        act_ref[rows, :] = act
        slope_ref[rows, :] = slope.astype(bf16)
        down[rows, :] += matmul_nt(act, w2_ref[...])

    @pl.when(step == pl.num_programs(0) - 1)
    def _():
        sums_ref[...] = jnp.zeros_like(sums_ref)

        @pl.loop(0, chunks)
        def _(i):
            rows = pl.ds(pl.multiple_of(i * chunk, chunk), chunk)
            unit, _scale = norm_parts(h1_ref[rows, :])
            first = unit * vec_ref[0:1, :] + vec_ref[1:2, :]
            unit, scale = norm_parts(first + down[rows, :] + vec_ref[5:6, :])
            res_ref[rows, :] = (unit * vec_ref[2:3, :] + vec_ref[3:4, :]).astype(bf16)
            cot = cot_ref[rows, :].astype(f32)
            grad = norm_back(cot, unit, scale, vec_ref[2:3, :])
            gs_ref[rows, :] = grad
            sums_ref[0:1, :] += column_total(cot * unit)
            sums_ref[1:2, :] += column_total(cot)
            sums_ref[2:3, :] += column_total(grad.astype(bf16))


def feed_forward(x, mixed, cot, attn_full, ffn_full, hid_all, vec_par):
    rows = x.shape[0]
    chunk = min(256, rows)
    steps = FF // D
    whole = lambda shape: pl.BlockSpec(shape, lambda t: (0,) * len(shape))
    once = lambda shape: pl.BlockSpec(
        shape, lambda t: (0,) * len(shape), pipeline_mode=pl.Buffered(1)
    )
    hidden = pl.BlockSpec((rows, D), lambda t: (0, t))
    return pl.pallas_call(
        partial(up_kernel, chunk),
        out_shape=[
            jax.ShapeDtypeStruct((rows, FF), bf16),
            jax.ShapeDtypeStruct((rows, FF), bf16),
            jax.ShapeDtypeStruct((rows, D), f32),
            jax.ShapeDtypeStruct((rows, D), bf16),
            jax.ShapeDtypeStruct((rows, D), f32),
            jax.ShapeDtypeStruct((8, D), f32),
        ],
        grid=(steps,),
        in_specs=[
            once((rows, D)),
            once((rows, D)),
            once((rows, D)),
            pl.BlockSpec((None, D, D), lambda t: (3, 0, 0), pipeline_mode=pl.Buffered(1)),
            pl.BlockSpec((None, D, D), lambda t: (0, 0, t)),
            pl.BlockSpec((None, D, D), lambda t: (1, 0, t)),
            pl.BlockSpec((1, D), lambda t: (0, t)),
            whole((6, D)),
        ],
        out_specs=[
            hidden,
            hidden,
            whole((rows, D)),
            whole((rows, D)),
            whole((rows, D)),
            whole((8, D)),
        ],
        scratch_shapes=[pltpu.VMEM((rows, D), bf16), pltpu.VMEM((rows, D), f32)],
        compiler_params=pltpu.CompilerParams(vmem_limit_bytes=VMEM_LIMIT),
        cost_estimate=pl.CostEstimate(
            flops=2 * rows * D * (D + 2 * FF),
            bytes_accessed=rows * D * 30 + 2 * D * FF * 2,
            transcendentals=2 * rows * FF,
        ),
        name="feed_forward",
    )(x, mixed, cot, attn_full, ffn_full, ffn_full, hid_all.reshape(1, FF), vec_par)


def down_kernel(
    chunk,
    gs_ref,
    h1_ref,
    mixed_ref,
    wo_ref,
    w1_ref,
    w2_ref,
    act_ref,
    slope_ref,
    vec_ref,
    dw1_ref,
    dw2_ref,
    dwo_ref,
    gh1_ref,
    gm_ref,
    hid_ref,
    sums_ref,
    turned,
    low_t,
    pre,
    total,
):
    step = pl.program_id(0)
    n_rows = gs_ref.shape[0]
    chunks = n_rows // chunk

    @pl.when(step == 0)
    def _():
        @pl.loop(0, chunks)
        def _(i):
            rows = pl.ds(pl.multiple_of(i * chunk, chunk), chunk)
            unit, _scale = norm_parts(h1_ref[rows, :])
            low = unit * vec_ref[0:1, :] + vec_ref[1:2, :]
            low_t[:, rows] = low.T.astype(bf16)
            turned[:, rows] = gs_ref[rows, :].T.astype(bf16)
            total[rows, :] = gs_ref[rows, :]

    for i in range(chunks):
        rows = slice(i * chunk, (i + 1) * chunk)
        grad_act = matmul(gs_ref[rows, :].astype(bf16), w2_ref[...]).astype(bf16).astype(f32)
        grad_pre = (grad_act * slope_ref[rows, :].astype(f32)).astype(bf16)
        pre[rows, :] = grad_pre
        total[rows, :] += matmul_nt(grad_pre, w1_ref[...])
    hid_ref[...] = column_total(pre[...])
    part = D // 4
    for j in range(4):
        out = slice(j * part, (j + 1) * part)
        dw1_ref[out, :] = matmul(low_t[out, :], pre[...]).astype(bf16)
        dw2_ref[out, :] = matmul(turned[out, :], act_ref[...]).astype(bf16)

    @pl.when(step == pl.num_programs(0) - 1)
    def _():
        sums_ref[...] = jnp.zeros_like(sums_ref)

        @pl.loop(0, chunks)
        def _(i):
            rows = pl.ds(pl.multiple_of(i * chunk, chunk), chunk)
            unit, scale = norm_parts(h1_ref[rows, :])
            grad_first = total[rows, :]
            grad_h1 = norm_back(grad_first, unit, scale, vec_ref[0:1, :])
            gh1_ref[rows, :] = grad_h1
            low = grad_h1.astype(bf16)
            gm_ref[rows, :] = matmul(low, wo_ref[...]).astype(bf16)
            turned[:, rows] = grad_h1.T.astype(bf16)
            sums_ref[0:1, :] += column_total(grad_first * unit)
            sums_ref[1:2, :] += column_total(grad_first)
            sums_ref[2:3, :] += column_total(low)

        @pl.loop(0, 4)
        def _(j):
            out = pl.ds(pl.multiple_of(j * part, part), part)
            dwo_ref[out, :] = matmul(turned[out, :], mixed_ref[...]).astype(bf16)


def feed_back(gs, h1, mixed, attn_full, ffn_full, act, slope, vec_par):
    rows = gs.shape[0]
    chunk = min(256, rows)
    steps = FF // D
    whole = lambda shape: pl.BlockSpec(shape, lambda t: (0,) * len(shape))
    once = lambda shape: pl.BlockSpec(
        shape, lambda t: (0,) * len(shape), pipeline_mode=pl.Buffered(1)
    )
    hidden = pl.BlockSpec((rows, D), lambda t: (0, t))
    slab = pl.BlockSpec((D, D), lambda t: (0, t))
    return pl.pallas_call(
        partial(down_kernel, chunk),
        out_shape=[
            jax.ShapeDtypeStruct((D, FF), bf16),
            jax.ShapeDtypeStruct((D, FF), bf16),
            jax.ShapeDtypeStruct((D, D), bf16),
            jax.ShapeDtypeStruct((rows, D), f32),
            jax.ShapeDtypeStruct((rows, D), bf16),
            jax.ShapeDtypeStruct((1, FF), f32),
            jax.ShapeDtypeStruct((8, D), f32),
        ],
        grid=(steps,),
        in_specs=[
            once((rows, D)),
            once((rows, D)),
            once((rows, D)),
            pl.BlockSpec((None, D, D), lambda t: (3, 0, 0), pipeline_mode=pl.Buffered(1)),
            pl.BlockSpec((None, D, D), lambda t: (0, 0, t)),
            pl.BlockSpec((None, D, D), lambda t: (1, 0, t)),
            hidden,
            hidden,
            whole((6, D)),
        ],
        out_specs=[
            slab,
            slab,
            whole((D, D)),
            whole((rows, D)),
            whole((rows, D)),
            pl.BlockSpec((1, D), lambda t: (0, t)),
            whole((8, D)),
        ],
        scratch_shapes=[
            pltpu.VMEM((D, rows), bf16),
            pltpu.VMEM((D, rows), bf16),
            pltpu.VMEM((rows, D), bf16),
            pltpu.VMEM((rows, D), f32),
        ],
        compiler_params=pltpu.CompilerParams(vmem_limit_bytes=VMEM_LIMIT),
        cost_estimate=pl.CostEstimate(
            flops=2 * rows * D * (2 * D + 4 * FF),
            bytes_accessed=rows * D * 30 + 4 * D * FF * 2,
            transcendentals=0,
        ),
        name="feed_back",
    )(gs, h1, mixed, attn_full, ffn_full, ffn_full, act, slope, vec_par)


WIDE = 1536
STRIP = 96
PIECES = 8
ITEM = 128
LINE_ITEMS = 5
MESH = pl.DeviceIdType.MESH


def remote(src, dst, send, recv, where):
    return pltpu.make_async_remote_copy(
        src_ref=src,
        dst_ref=dst,
        send_sem=send,
        recv_sem=recv,
        device_id=where,
        device_id_type=MESH,
    )


def greet(partners):
    barrier = pltpu.get_barrier_semaphore()
    for where in partners:
        pl.semaphore_signal(barrier, inc=1, device_id=where, device_id_type=MESH)
    pl.semaphore_wait(barrier, len(partners))


def places(n_tensor):
    s, c, t = lax.axis_index("shard"), lax.axis_index("ctx"), lax.axis_index("tensor")
    x, core = s // 2, s % 2
    sibling = (x * 2 + 1 - core, c, t)
    over_x = ((1 - x) * 2 + core, c, t)
    over_y = (s, 1 - c, t)
    across = (x * 2 + 1 - core, 1 - c, t)
    along_z = [(s, c, lax.rem(t + k, n_tensor)) for k in range(1, n_tensor)]
    return s, c, t, x, core, sibling, over_x, over_y, across, along_z


class Line:
    def __init__(self, s, c, t, last, items, rows, array, up, down):
        self.s, self.c, self.t, self.last, self.items = s, c, t, last, items
        self.rows, self.array, self.up, self.down = rows, array, up, down

    def hop(self, i, src_t, sems, n, to):
        ref = self.array.at[src_t, pl.ds(i * self.rows, self.rows)]
        return remote(ref, ref, sems[0].at[n], sems[1].at[n], (self.s, self.c, to))

    def send_own(self, i):
        t = self.t

        @pl.when(t < self.last)
        def _():
            self.hop(i, t, self.up, i, t + 1).start()

        @pl.when(t > 0)
        def _():
            self.hop(i, t, self.down, i, t - 1).start()

    def tick(self, j):
        t, last = self.t, self.last
        i, hops, n = j % self.items, j // self.items + 1, j + self.items

        @pl.when(t >= hops)
        def _():
            self.hop(i, t - hops, self.up, j, t - 1).wait_recv()

            @pl.when(t < last)
            def _():
                self.hop(i, t - hops, self.up, n, t + 1).start()

        @pl.when(t + hops <= last)
        def _():
            self.hop(i, t + hops, self.down, j, t + 1).wait_recv()

            @pl.when(t > 0)
            def _():
                self.hop(i, t + hops, self.down, n, t - 1).start()

    def settle(self, j):
        t, last = self.t, self.last
        i, hops = j % self.items, j // self.items

        @pl.when((t < last) & (t >= hops))
        def _():
            self.hop(i, t - hops, self.up, j, t + 1).wait_send()

        @pl.when((t > 0) & (t + hops <= last))
        def _():
            self.hop(i, t + hops, self.down, j, t - 1).wait_send()


def start_kernel(n_tensor, *refs):
    attn_ref, ffn_ref, qv_ref, hid_ref, tab_ref, rand, tokens = refs[:7]
    attn_out, ffn_out, hid_out, x_out, q_out, k_out, v_out, mixed_out, lse_out = refs[7:16]
    low, low_z, bias, bias_z, bias_qv, ffn_low, full, xs, qs, ms, k_buf, v_buf, s_buf = refs[16:29]
    (
        z_send,
        z_recv,
        b_send,
        b_recv,
        fz_send,
        fz_recv,
        x_send,
        x_recv,
        g_send,
        g_recv,
        p_send,
        p_recv,
        fg_send,
        fg_recv,
        fp_send,
        fp_recv,
        kv_send,
        kv_recv,
        own_sem,
    ) = refs[29:]
    s, c, t, x, core, sibling, over_x, over_y, across, along_z = places(n_tensor)
    own_cols, own_ff = D // n_tensor, FF // n_tensor
    n_rows = xs.shape[0]

    for m in range(4):
        low[:, m * own_cols : (m + 1) * own_cols] = attn_ref[m].astype(bf16)
    for m in range(2):
        ffn_low[m] = ffn_ref[m].astype(bf16)
    bias[0:2, 0:own_cols] = qv_ref[...]
    bias[2:3, 0:own_ff] = hid_ref[...]

    greet([sibling, over_x, over_y, across] + along_z)

    sent = []

    def put(copy):
        copy.start()
        sent.append(copy)

    half = 2 * own_cols

    def z_hop(path, k, u):
        cols = pl.ds(path * half, half)
        n = path * n_tensor
        return remote(
            low.at[:, cols], low_z.at[u, :, cols], z_send.at[n + k], z_recv.at[n + u], along_z[k]
        )

    for path in range(2):
        for k in range(n_tensor - 1):
            put(z_hop(path, k, t))

    def keep_rows(src, dst, n):
        return pltpu.make_async_copy(src.at[t], dst, x_recv.at[n])

    def swap_rows(src, dst, n):
        return remote(src.at[t], dst, x_send.at[n], x_recv.at[n], across)

    @pl.when(core == c)
    def _():
        keep_rows(tokens, xs, 0).start()

    @pl.when(core != c)
    def _():
        swap_rows(tokens, xs, 0).start()

    low_z[t] = low[...]
    bias_z[t] = bias[...]

    def strip(shard, ctx):
        return pl.ds(pl.multiple_of((2 * shard + ctx) * STRIP, STRIP), STRIP)

    here = strip(s, c)

    def lay_out(path):
        for k, where in enumerate(along_z):
            z_hop(path, k, where[2]).wait_recv()
        for n in range(n_tensor):
            for m in range(2 * path, 2 * path + 2):
                piece = low_z[n, :, m * own_cols : (m + 1) * own_cols]
                full[m, here, n * own_cols : (n + 1) * own_cols] = piece

    far_x, far_y = over_x[0], 1 - c
    labels = ["own", "x", "y", "xy"]
    rows = {
        "own": here,
        "x": strip(far_x, c),
        "y": strip(s, far_y),
        "xy": strip(far_x, far_y),
    }
    far_rows = {
        "own": strip(sibling[0], c),
        "x": strip(2 * (1 - x) + 1 - core, c),
        "y": strip(sibling[0], far_y),
        "xy": strip(2 * (1 - x) + 1 - core, far_y),
    }

    def attn_block(path, at):
        return full.at[pl.ds(2 * path, 2), at, :]

    def ffn_block(path, at):
        return ffn_out.at[path, at, :]

    class Gather:
        def __init__(self, block, ways, gs, gr, ps, pr):
            self.block, self.gs, self.gr, self.ps, self.pr = block, gs, gr, ps, pr
            x_first = (("x", over_x), ("y", over_y))
            self.ways = [x_first if way == 0 else x_first[::-1] for way in ways]

        def hop(self, path, name, label, where):
            n = path * 3 + labels.index(label) - 1
            ref = self.block(path, rows[name])
            return remote(ref, ref, self.gs.at[n], self.gr.at[n], where)

        def give(self, path, name, label, where):
            put(self.hop(path, name, label, where))

        def take(self, path, label):
            self.hop(path, label, label, over_x).wait_recv()

        def share(self, path, name):
            put(self.shared(path, name))

        def take_shared(self, path):
            for n, name in enumerate(labels):
                ref = self.block(path, far_rows[name])
                n = path * 4 + n
                remote(ref, ref, self.ps.at[n], self.pr.at[n], sibling).wait_recv()

        def shared(self, path, name):
            n = path * 4 + labels.index(name)
            ref = self.block(path, rows[name])
            return remote(ref, ref, self.ps.at[n], self.pr.at[n], sibling)

        def again(self, path, number):
            near, far = self.ways[path]
            if number == 1:
                sent.append(self.hop(path, near[0], "xy", far[1]))
            sent.append(self.shared(path, {1: near[0], 2: far[0], 3: "xy"}[number]))

        def step(self, path, number):
            near, far = self.ways[path]
            if number == 0:
                self.give(path, "own", near[0], near[1])
                self.give(path, "own", far[0], far[1])
                self.share(path, "own")
            elif number == 1:
                self.take(path, near[0])
                self.give(path, near[0], "xy", far[1])
                self.share(path, near[0])
            elif number == 2:
                self.take(path, far[0])
                self.share(path, far[0])
            else:
                self.take(path, "xy")
                self.share(path, "xy")

    attn = Gather(attn_block, (1, 1), g_send, g_recv, p_send, p_recv)
    ffn = Gather(ffn_block, (0, 1), fg_send, fg_recv, fp_send, fp_recv)

    def ffn_cols(path, u):
        return ffn_out.at[path, here, pl.ds(pl.multiple_of(u * own_ff, own_ff), own_ff)]

    def ffn_hop(path, k, u):
        n = path * n_tensor
        return remote(
            ffn_low.at[path],
            ffn_cols(path, u),
            fz_send.at[n + k],
            fz_recv.at[n + u],
            along_z[k],
        )

    local = []

    def write(src, dst, n):
        copy = pltpu.make_async_copy(src, dst, own_sem.at[n])
        copy.start()
        local.append(copy)

    def ffn_along_z(path):
        for k in range(n_tensor - 1):
            put(ffn_hop(path, k, t))
        write(ffn_low.at[path], ffn_cols(path, t), 5 + path)

    def ffn_ready(path):
        for k, where in enumerate(along_z):
            ffn_hop(path, k, where[2]).wait_recv()
        local[path].wait()
        ffn.step(path, 0)

    lay_out(0)
    attn.step(0, 0)
    lay_out(1)
    attn.step(1, 0)
    ffn_along_z(0)
    ffn_along_z(1)
    for k, where in enumerate(along_z):
        put(remote(bias, bias_z.at[t], b_send.at[k], b_recv.at[t], where))
    attn.step(0, 1)
    attn.step(1, 1)
    ffn_ready(0)
    attn.step(0, 2)
    attn.step(1, 2)
    attn.step(0, 3)
    attn.step(1, 3)
    for k, where in enumerate(along_z):
        u = where[2]
        remote(bias, bias_z.at[u], b_send.at[k], b_recv.at[u], where).wait_recv()
    for n in range(n_tensor):
        cols = slice(n * own_cols, (n + 1) * own_cols)
        bias_qv[0:2, cols] = bias_z[n, 0:2, 0:own_cols]
        hid_out[:, n * own_ff : (n + 1) * own_ff] = bias_z[n, 2:3, 0:own_ff]

    @pl.when(core == c)
    def _():
        keep_rows(tokens, xs, 0).wait()

    @pl.when(core != c)
    def _():
        swap_rows(tokens, xs, 0).wait()

    chunk = 256
    chunks = n_rows // chunk
    per = chunk // BLOCK

    def kv_hop(buf, i, n):
        at, to = pl.ds(i * per, per), pl.ds(n_rows // BLOCK + i * per, per)
        return remote(buf.at[at], buf.at[to], kv_send.at[n], kv_recv.at[n], sibling)

    attn.take_shared(0)
    for i in range(chunks):
        at = pl.ds(i * chunk, chunk)
        k = matmul(xs[at, :], full[1]).astype(bf16)
        k_buf[pl.ds(i * per, per)] = k.reshape(per, BLOCK, D)
        put(kv_hop(k_buf, i, i))
    ffn_ready(1)
    for i in range(chunks):
        at = pl.ds(i * chunk, chunk)
        q = matmul(xs[at, :], full[0]) + bias_qv[0:1, :]
        qs[at, :] = (q.astype(bf16).astype(f32) * 0.125).astype(bf16)
    attn.take_shared(1)
    for i in range(chunks):
        at = pl.ds(i * chunk, chunk)
        v = (matmul(xs[at, :], full[2]) + bias_qv[1:2, :]).astype(bf16)
        v_buf[pl.ds(i * per, per)] = v.reshape(per, BLOCK, D)
        put(kv_hop(v_buf, i, chunks + i))
    ffn.step(0, 1)
    write(xs, x_out, 0)
    write(qs, q_out, 1)
    write(full, attn_out, 2)
    for i in range(chunks):
        kv_hop(k_buf, i, i).wait_recv()
        kv_hop(v_buf, i, chunks + i).wait_recv()
    write(k_buf, k_out, 3)
    write(v_buf, v_out, 4)

    nb = n_rows // BLOCK
    first = core * nb
    stops = {0: [(1, 1)], 1: [(0, 2), (1, 2)], 9: [(0, 3), (1, 3)]}

    @pl.loop(0, nb)
    def _(blk):
        at = pl.ds(pl.multiple_of(blk * BLOCK, BLOCK), BLOCK)
        forward_block(
            qs.at[at],
            ms.at[at],
            lse_out.at[blk],
            k_buf,
            v_buf,
            s_buf,
            tab_ref,
            rand,
            blk * (LISTED - 5),
            blk,
            first,
            0,
        )

        for at_block, moves in stops.items():

            @pl.when(blk == at_block)
            def _():
                mark = len(sent)
                for path, number in moves:
                    ffn.step(path, number)
                del sent[mark:]

    write(ms, mixed_out, 7)
    for path, number in [move for moves in stops.values() for move in moves]:
        ffn.again(path, number)
    ffn.take_shared(0)
    ffn.take_shared(1)

    for copy in sent:
        copy.wait_send()
    for copy in local[2:]:
        copy.wait()


def start(n_tensor, attn_w, ffn_w, qv_bias, hid_bias, table, rand, tokens):
    rows = tokens.shape[1]
    own_ff = FF // n_tensor
    dma = pltpu.SemaphoreType.DMA
    vmem, anywhere = pl.BlockSpec(memory_space=pltpu.VMEM), pl.BlockSpec(memory_space=pl.ANY)
    smem = pl.BlockSpec(memory_space=pltpu.SMEM)
    tall = jax.ShapeDtypeStruct((rows, D), bf16)
    both = jax.ShapeDtypeStruct((2 * rows // BLOCK, BLOCK, D), bf16)
    items = 2 * (rows // 256)
    return pl.pallas_call(
        partial(start_kernel, n_tensor),
        out_shape=[
            jax.ShapeDtypeStruct((4, D, D), bf16),
            jax.ShapeDtypeStruct((2, D, FF), bf16),
            jax.ShapeDtypeStruct((1, FF), f32),
            tall,
            tall,
            both,
            both,
            tall,
            jax.ShapeDtypeStruct((rows // BLOCK, 8, ROWS), f32),
        ],
        in_specs=[vmem] * 5 + [smem, anywhere],
        out_specs=[anywhere, anywhere, vmem] + [anywhere] * 5 + [vmem],
        scratch_shapes=[
            pltpu.VMEM((STRIP, D), bf16),
            pltpu.VMEM((n_tensor, STRIP, D), bf16),
            pltpu.VMEM((8, D), f32),
            pltpu.VMEM((n_tensor, 8, D), f32),
            pltpu.VMEM((8, D), f32),
            pltpu.VMEM((2, STRIP, own_ff), bf16),
            pltpu.VMEM((4, D, D), bf16),
            pltpu.VMEM((rows, D), bf16),
            pltpu.VMEM((rows, D), bf16),
            pltpu.VMEM((rows, D), bf16),
            pltpu.VMEM((2 * rows // BLOCK, BLOCK, D), bf16),
            pltpu.VMEM((2 * rows // BLOCK, BLOCK, D), bf16),
            pltpu.VMEM((2 * rows // KEYS, ROWS, KEYS), f32),
            dma((2 * n_tensor,)),
            dma((2 * n_tensor,)),
            dma((n_tensor,)),
            dma((n_tensor,)),
            dma((2 * n_tensor,)),
            dma((2 * n_tensor,)),
            dma((2,)),
            dma((2,)),
            dma((6,)),
            dma((6,)),
            dma((8,)),
            dma((8,)),
            dma((6,)),
            dma((6,)),
            dma((8,)),
            dma((8,)),
            dma((items,)),
            dma((items,)),
            dma((8,)),
        ],
        compiler_params=pltpu.CompilerParams(
            collective_id=2, has_side_effects=True, vmem_limit_bytes=VMEM_LIMIT
        ),
        cost_estimate=pl.CostEstimate(
            flops=6 * rows * D * D, bytes_accessed=100 * 2**20, transcendentals=0
        ),
        name="start",
    )(attn_w, ffn_w, qv_bias, hid_bias.reshape(1, own_ff), table, rand, tokens)


def middle_kernel(n_tensor, *refs):
    x_ref, mixed_ref, hid_ref, vec_ref, cotangent, attn_full, ffn_full = refs[:7]
    out_a, out_b, dw1, dw2, dwo, gh1, gm, hid_out, sums_out = refs[7:16]
    w, wo, act, slope, h1, total, gs_low, low_t, turned, pre, dw_s, cot, ready, low, down = refs[16:31]
    (
        w_sem,
        c_send,
        c_recv,
        h_send,
        h_recv,
        up_send,
        up_recv,
        dn_send,
        dn_recv,
        dw_sem,
        own_sem,
    ) = refs[31:]
    s, c, t, x, core, sibling, over_x, over_y, across, along_z = places(n_tensor)
    n_rows = x_ref.shape[0]
    chunk = 256
    chunks = n_rows // chunk
    steps = FF // D
    items, all_items = LINE_ITEMS, n_rows // ITEM
    last = n_tensor - 1

    def block(i):
        return pl.ds(pl.multiple_of(i * D, D), D)

    fetch_o = pltpu.make_async_copy(attn_full.at[3], wo, w_sem.at[2 * steps])
    fetch_o.start()

    def fetch(m, i):
        at = w.at[m, :, block(i)]
        return pltpu.make_async_copy(ffn_full.at[m, :, block(i)], at, w_sem.at[m * steps + i])

    for i in range(steps):
        for m in range(2):
            fetch(m, i).start()

    greet([over_y, across] + along_z)

    def keep_cot():
        return pltpu.make_async_copy(cotangent.at[t], cot, c_recv.at[0])

    def swap_cot():
        return remote(cotangent.at[t], cot, c_send.at[0], c_recv.at[0], across)

    def home_ref(i):
        if i < items:
            return out_a.at[t, pl.ds(i * ITEM, ITEM)]
        return out_b.at[pl.ds((i - items) * ITEM, ITEM)]

    def keep_home(i):
        return pltpu.make_async_copy(ready.at[pl.ds(i * ITEM, ITEM)], home_ref(i), h_recv.at[i])

    def send_home(i):
        src = ready.at[pl.ds(i * ITEM, ITEM)]
        return remote(src, home_ref(i), h_send.at[i], h_recv.at[i], across)

    def if_home(at_home, away):
        @pl.when(core == c)
        def _():
            at_home()

        @pl.when(core != c)
        def _():
            away()

    if_home(lambda: keep_cot().start(), lambda: swap_cot().start())

    up, down_line = (up_send, up_recv), (dn_send, dn_recv)
    chain = Line(s, c, t, last, items, ITEM, out_a, up, down_line)

    def own_ready(i):
        if_home(lambda: keep_home(i).wait(), lambda: send_home(i).wait_recv())

    per = chunk // ITEM
    for i in range(chunks):
        rows = slice(i * chunk, (i + 1) * chunk)
        if i == 0:
            fetch_o.wait()
        pre1 = x_ref[rows, :].astype(f32) + matmul_nt(mixed_ref[rows, :], wo[...])
        pre1 = pre1 + vec_ref[4:5, :]
        h1[rows, :] = pre1
        unit, _scale = norm_parts(pre1)
        first = unit * vec_ref[0:1, :] + vec_ref[1:2, :]
        low[...] = first.astype(bf16)
        down[...] = first + vec_ref[5:6, :]

        @pl.loop(0, steps)
        def _(j):
            if i == 0:
                fetch(0, j).wait()
                fetch(1, j).wait()
            else:

                @pl.when(j == steps // 2)
                def _():
                    for n in range((i - 1) * per, min(i * per, items)):
                        own_ready(n)
                        chain.send_own(n)

            hidden = matmul(low[...], w[0, :, block(j)]) + hid_ref[:, block(j)]
            act_now, slope_now = gelu_and_slope(hidden)
            act_now = act_now.astype(bf16)
            act[rows, block(j)] = act_now
            slope[rows, block(j)] = slope_now.astype(bf16)
            down[...] += matmul_nt(act_now, w[1, :, block(j)])

        second = down[...]
        total[rows, :] = second
        unit, _scale = norm_parts(second)
        ready[rows, :] = (unit * vec_ref[2:3, :] + vec_ref[3:4, :]).astype(bf16)
        for n in range(i * chunk // ITEM, (i + 1) * chunk // ITEM):
            if_home(lambda: keep_home(n).start(), lambda: send_home(n).start())
        if i == chunks - 1:
            chain.tick(0)
            chain.tick(1)
            chain.tick(2)

    if_home(lambda: keep_cot().wait(), lambda: swap_cot().wait())
    sums_out[...] = jnp.zeros_like(sums_out)

    @pl.loop(0, chunks)
    def _(i):
        rows = pl.ds(pl.multiple_of(i * chunk, chunk), chunk)
        unit, scale = norm_parts(total[rows, :])
        grad_out = cot[rows, :].astype(f32)
        grad = norm_back(grad_out, unit, scale, vec_ref[2:3, :])
        sums_out[2:3, :] += column_total(grad_out * unit)
        sums_out[3:4, :] += column_total(grad_out)
        total[rows, :] = grad
        grad_low = grad.astype(bf16)
        gs_low[rows, :] = grad_low
        sums_out[5:6, :] += column_total(grad_low)
        turned[:, rows] = grad.T.astype(bf16)
        unit, _scale = norm_parts(h1[rows, :])
        first = unit * vec_ref[0:1, :] + vec_ref[1:2, :]
        low_t[:, rows] = first.T.astype(bf16)

    chain.tick(3)
    chain.tick(4)
    part = D // 4

    def dw_copy(slot, m, j):
        return pltpu.make_async_copy(
            dw_s.at[slot, m], (dw1, dw2)[m].at[:, block(j)], dw_sem.at[2 * slot + m]
        )

    ticks = {0: [5, 6], 1: [7, 8], 2: [9, 10], 3: [11, 12]}

    @pl.loop(0, steps)
    def _(j):
        slot = lax.rem(j, 2)
        for i in range(chunks):
            rows = slice(i * chunk, (i + 1) * chunk)
            grad_act = matmul(gs_low[rows, :], w[1, :, block(j)]).astype(bf16).astype(f32)
            grad_pre = (grad_act * slope[rows, block(j)].astype(f32)).astype(bf16)
            pre[rows, :] = grad_pre
            total[rows, :] += matmul_nt(grad_pre, w[0, :, block(j)])
        hid_out[:, block(j)] = column_total(pre[...])

        @pl.when(j >= 2)
        def _():
            for m in range(2):
                dw_copy(slot, m, j - 2).wait()

        for n in range(4):
            out = slice(n * part, (n + 1) * part)
            dw_s[slot, 0, out, :] = matmul(low_t[out, :], pre[...]).astype(bf16)
            dw_s[slot, 1, out, :] = matmul(turned[out, :], act[:, block(j)]).astype(bf16)
        for m in range(2):
            dw_copy(slot, m, j).start()
        for at, numbers in ticks.items():

            @pl.when(j == at)
            def _():
                for n in numbers:
                    chain.tick(n)

    gm_s = gs_low

    @pl.loop(0, chunks)
    def _(i):
        rows = pl.ds(pl.multiple_of(i * chunk, chunk), chunk)
        unit, scale = norm_parts(h1[rows, :])
        grad_first = total[rows, :]
        grad_h1 = norm_back(grad_first, unit, scale, vec_ref[0:1, :])
        total[rows, :] = grad_h1
        grad_low = grad_h1.astype(bf16)
        gm_s[rows, :] = matmul(grad_low, wo[...]).astype(bf16)
        turned[:, rows] = grad_h1.T.astype(bf16)
        sums_out[0:1, :] += column_total(grad_first * unit)
        sums_out[1:2, :] += column_total(grad_first)
        sums_out[4:5, :] += column_total(grad_low)

    local = [
        pltpu.make_async_copy(total, gh1, own_sem.at[0]),
        pltpu.make_async_copy(gm_s, gm, own_sem.at[1]),
    ]
    for copy in local:
        copy.start()
    for j in range(steps - 2, steps):
        for m in range(2):
            dw_copy(j % 2, m, j).wait()

    @pl.loop(0, 4)
    def _(n):
        out = pl.ds(pl.multiple_of(n * part, part), part)
        dw_s[0, 0, out, :] = matmul(turned[out, :], mixed_ref[...]).astype(bf16)

    local.append(pltpu.make_async_copy(dw_s.at[0, 0], dwo, own_sem.at[2]))
    local[-1].start()
    for j in range(13, items * last):
        chain.tick(j)
    for i in range(items, all_items):
        own_ready(i)
    for i in range(all_items):

        @pl.when(core != c)
        def _():
            send_home(i).wait_send()

    for j in range(items * last):
        chain.settle(j)
    for copy in local:
        copy.wait()


def middle(n_tensor, x, mixed, hid_all, vec_par, cotangent, attn_full, ffn_full):
    rows = x.shape[0]
    steps = FF // D
    items, all_items = LINE_ITEMS, rows // ITEM
    dma = pltpu.SemaphoreType.DMA
    vmem, anywhere = pl.BlockSpec(memory_space=pltpu.VMEM), pl.BlockSpec(memory_space=pl.ANY)
    low, wide = pltpu.VMEM((rows, D), bf16), pltpu.VMEM((rows, D), f32)
    return pl.pallas_call(
        partial(middle_kernel, n_tensor),
        out_shape=[
            jax.ShapeDtypeStruct((n_tensor, items * ITEM, D), bf16),
            jax.ShapeDtypeStruct((rows - items * ITEM, D), bf16),
            jax.ShapeDtypeStruct((D, FF), bf16),
            jax.ShapeDtypeStruct((D, FF), bf16),
            jax.ShapeDtypeStruct((D, D), bf16),
            jax.ShapeDtypeStruct((rows, D), f32),
            jax.ShapeDtypeStruct((rows, D), bf16),
            jax.ShapeDtypeStruct((1, FF), f32),
            jax.ShapeDtypeStruct((8, D), f32),
        ],
        in_specs=[vmem] * 4 + [anywhere] * 3,
        out_specs=[anywhere] * 7 + [vmem] * 2,
        scratch_shapes=[
            pltpu.VMEM((2, D, FF), bf16),
            pltpu.VMEM((D, D), bf16),
            pltpu.VMEM((rows, FF), bf16),
            pltpu.VMEM((rows, FF), bf16),
            wide,
            wide,
            low,
            pltpu.VMEM((D, rows), bf16),
            pltpu.VMEM((D, rows), bf16),
            low,
            pltpu.VMEM((2, 2, D, D), bf16),
            low,
            low,
            pltpu.VMEM((256, D), bf16),
            pltpu.VMEM((256, D), f32),
            dma((2 * steps + 1,)),
            dma((1,)),
            dma((1,)),
            dma((all_items,)),
            dma((all_items,)),
            dma((items * n_tensor,)),
            dma((items * n_tensor,)),
            dma((items * n_tensor,)),
            dma((items * n_tensor,)),
            dma((4,)),
            dma((3,)),
        ],
        compiler_params=pltpu.CompilerParams(
            collective_id=3, has_side_effects=True, vmem_limit_bytes=VMEM_LIMIT
        ),
        cost_estimate=pl.CostEstimate(
            flops=2 * rows * D * (3 * D + 6 * FF),
            bytes_accessed=60 * 2**20,
            transcendentals=2 * rows * FF,
        ),
        name="middle",
    )(x, mixed, hid_all, vec_par, cotangent, attn_full, ffn_full)


def finish_kernel(n_tensor, *refs):
    dq, dk_own, dk_far, dv_own, dv_far, gh1, x_ref, weights = refs[:8]
    dw1, dw2, dwo, vec_sums, hid_sums = refs[8:13]
    attn_out, ffn_out, vec_out, qv_out, hid_out, tokens_out = refs[13:19]
    (
        dk_got,
        dv_got,
        dk,
        dv,
        x_t,
        partial_sum,
        ready,
        dws,
        acc,
        got0,
        got1a,
        got1b,
        got2,
        zf,
        zf_got,
        za,
        za_got,
        run,
        run_got,
        run_z,
        wts,
    ) = refs[19:40]
    (
        e_send,
        e_recv,
        own_sem,
        s0,
        r0,
        s1,
        r1,
        s2,
        r2,
        zf_send,
        zf_recv,
        za_send,
        za_recv,
        sm,
        rm,
        h_send,
        h_recv,
        up_send,
        up_recv,
        dn_send,
        dn_recv,
        w_sem,
    ) = refs[40:]
    s, c, t, x, core, sibling, over_x, over_y, across, along_z = places(n_tensor)
    n_rows = dq.shape[0]
    rows_each = n_rows // PIECES
    last = n_tensor - 1

    def pieces(path, i):
        if i < 2:
            return [(dw1 if path == 0 else dw2, i * WIDE, WIDE, 0)]
        if path == 0:
            return [(dws.at[0], 0, D, 0), (dws.at[1], 0, D, D)]
        return [(dws.at[2], 0, D, 0), (dwo, 0, D, D)]

    def slot(path, i):
        return path * 3 + i

    order = [(path, i) for i in range(3) for path in range(2)]

    def rows_of(xx, cc):
        return pl.ds(pl.multiple_of((4 * xx + 2 * cc) * STRIP, 2 * STRIP), 2 * STRIP)

    own, first = {}, {}
    for path, i in order:
        k = slot(path, i)
        own[k], first[k] = [], []
        for xx in range(2):
            for j, (ref, col, width, at) in enumerate(pieces(path, i)):
                n = (k * 2 + xx) * 2 + j
                cols, to = pl.ds(col, width), pl.ds(at, width)
                own[k].append(
                    pltpu.make_async_copy(
                        ref.at[rows_of(xx, core), cols], acc.at[k, xx, :, to], own_sem.at[n]
                    )
                )
                first[k].append(
                    remote(
                        ref.at[rows_of(xx, 1 - core), cols],
                        got0.at[k, xx, :, to],
                        s0.at[n],
                        r0.at[n],
                        sibling,
                    )
                )

    def start_own(i):
        for path in range(2):
            for copy in own[slot(path, i)]:
                copy.start()

    def start_first(i):
        for path in range(2):
            for copy in first[slot(path, i)]:
                copy.start()

    fetch = pltpu.make_async_copy(weights.at[pl.ds(0, 3)], wts, w_sem.at[0])
    fetch.start()
    start_own(0)
    start_own(1)
    greet([sibling, over_x, over_y, across] + along_z)

    swaps = [
        remote(dk_far, dk_got, e_send.at[0], e_recv.at[0], sibling),
        remote(dv_far, dv_got, e_send.at[1], e_recv.at[1], sibling),
    ]
    for copy in swaps:
        copy.start()
    start_first(0)

    fetch.wait()
    chunk = 256
    for i in range(n_rows // chunk):
        at = slice(i * chunk, (i + 1) * chunk)
        partial_sum[at, :] = gh1[at, :] + matmul_nt(dq[at, :], wts[0])
        x_t[:, at] = x_ref[at, :].T
    run[0] = jnp.zeros(run.shape[1:], f32)
    run[0, 0:6, :] = vec_sums[0:6, :]
    run[0, 6:7, :] = column_total(dq[...])
    for n in range(FF // D):
        run[0, 8 + n : 9 + n, :] = hid_sums[:, n * D : (n + 1) * D]

    for copy in swaps:
        copy.wait_recv()

    def keep_home(i):
        at = pl.ds(i * rows_each, rows_each)
        return pltpu.make_async_copy(ready.at[at], tokens_out.at[t, at], h_recv.at[i])

    def send_home(i):
        at = pl.ds(i * rows_each, rows_each)
        return remote(ready.at[at], tokens_out.at[t, at], h_send.at[i], h_recv.at[i], across)

    for i in range(PIECES):
        at = slice(i * rows_each, (i + 1) * rows_each)
        dk_piece = (dk_own[at, :].astype(f32) + dk_got[at, :].astype(f32)).astype(bf16)
        dv_piece = (dv_own[at, :].astype(f32) + dv_got[at, :].astype(f32)).astype(bf16)
        dk[at, :] = dk_piece
        dv[at, :] = dv_piece
        total = partial_sum[at, :] + matmul_nt(dk_piece, wts[1]) + matmul_nt(dv_piece, wts[2])
        ready[at, :] = total.astype(bf16)

        @pl.when(core == c)
        def _():
            keep_home(i).start()

        @pl.when(core != c)
        def _():
            send_home(i).start()

    chain = Line(
        s, c, t, last, PIECES, rows_each, tokens_out, (up_send, up_recv), (dn_send, dn_recv)
    )
    tick, settle = chain.tick, chain.settle

    def send_own(i):
        @pl.when(core == c)
        def _():
            keep_home(i).wait()

        @pl.when(core != c)
        def _():
            send_home(i).wait_recv()

        chain.send_own(i)

    def add_rows(target, source, count):
        @pl.loop(0, count // 16)
        def _(j):
            rows = pl.ds(pl.multiple_of(j * 16, 16), 16)
            total = target[rows, :].astype(f32) + source[rows, :].astype(f32)
            target[rows, :] = total.astype(bf16)

    def half(cc):
        return pl.ds(pl.multiple_of(cc * STRIP, STRIP), STRIP)

    second, third = {}, {}

    def stage1(path, i):
        k = slot(path, i)
        for copy in own[k]:
            copy.wait()
        for copy in first[k]:
            copy.wait_recv()
        for xx in range(2):
            add_rows(acc.at[k, xx], got0.at[k, xx], 2 * STRIP)
        if path == 0:
            second[k] = remote(acc.at[k, 1 - x], got1a.at[i], s1.at[k], r1.at[k], over_x)
        else:
            second[k] = remote(
                acc.at[k, :, half(1 - c), :], got1b.at[i], s1.at[k], r1.at[k], over_y
            )
        second[k].start()

    def stage2(path, i):
        k = slot(path, i)
        second[k].wait_recv()
        if path == 0:
            add_rows(acc.at[k, x], got1a.at[i], 2 * STRIP)
            third[k] = remote(
                acc.at[k, x, half(1 - c), :], got2.at[k], s2.at[k], r2.at[k], over_y
            )
        else:
            for xx in range(2):
                add_rows(acc.at[k, xx, half(c), :], got1b.at[i, xx], STRIP)
            third[k] = remote(
                acc.at[k, 1 - x, half(c), :], got2.at[k], s2.at[k], r2.at[k], over_x
            )
        third[k].start()

    own_cols = D // n_tensor
    own_ff = FF // n_tensor
    per = WIDE // own_ff

    def stage3(path, i):
        k = slot(path, i)
        third[k].wait_recv()

        @pl.loop(0, STRIP // 16)
        def _(j):
            rows = pl.ds(pl.multiple_of(j * 16, 16), 16)
            here = pl.ds(pl.multiple_of(c * STRIP + j * 16, 16), 16)
            total = acc[k, x, here, :].astype(f32) + got2[k, rows, :].astype(f32)
            if i < 2:
                for n in range(per):
                    piece = total[:, n * own_ff : (n + 1) * own_ff].astype(bf16)
                    zf[per * i + n, rows, path * own_ff : (path + 1) * own_ff] = piece
            else:
                for n in range(n_tensor):
                    for m in range(2):
                        at = m * D + n * own_cols
                        to = (2 * path + m) * own_cols
                        piece = total[:, at : at + own_cols].astype(bf16)
                        za[n, rows, to : to + own_cols] = piece

    z_sent = []

    def z_step(k, buf, got, send, recv):
        @pl.when(t == k)
        def _():
            for d in range(last, k, -1):
                if k > 0:
                    hop(buf, got, send, recv, d, 0, k - 1).wait_recv()
                    add_rows(buf.at[d], got.at[0, d], STRIP)
                hop(buf, got, send, recv, d, 0, k + 1).start()

        @pl.when(t == last - k)
        def _():
            for d in range(0, last - k):
                if k > 0:
                    hop(buf, got, send, recv, d, 1, last - k + 1).wait_recv()
                    add_rows(buf.at[d], got.at[1, d], STRIP)
                hop(buf, got, send, recv, d, 1, last - k - 1).start()

    def hop(buf, got, send, recv, d, way, to):
        n = way * n_tensor + d
        return remote(buf.at[d], got.at[way, d], send.at[n], recv.at[n], (s, c, to))

    def z_collect(buf, got, send, recv, emit):
        @pl.when(t > 0)
        def _():
            hop(buf, got, send, recv, t, 0, t - 1).wait_recv()
            add_rows(buf.at[t], got.at[0, t], STRIP)

        @pl.when(t < last)
        def _():
            hop(buf, got, send, recv, t, 1, t + 1).wait_recv()
            add_rows(buf.at[t], got.at[1, t], STRIP)

        @pl.loop(0, STRIP // 16)
        def _(j):
            rows = pl.ds(pl.multiple_of(j * 16, 16), 16)
            emit(rows, buf[t, rows, :].astype(f32))

    def z_settle(buf, got, send, recv):
        for d in range(n_tensor):

            @pl.when(t < d)
            def _():
                hop(buf, got, send, recv, d, 0, t + 1).wait_send()

            @pl.when(t > d)
            def _():
                hop(buf, got, send, recv, d, 1, t - 1).wait_send()

    ffn_z = (zf, zf_got, zf_send, zf_recv)
    attn_z = (za, za_got, za_send, za_recv)

    small = []

    def small_send(n, where):
        small.append(remote(run.at[n], run_got.at[n], sm.at[n], rm.at[n], where))
        small[n].start()

    def small_add(n):
        small[n].wait_recv()
        run[n + 1] = run[n] + run_got[n]

    dws[0] = matmul(x_t[...], dq[...]).astype(bf16)
    send_own(0)
    send_own(1)
    start_first(1)
    dws[1] = matmul(x_t[...], dk[...]).astype(bf16)
    send_own(2)
    send_own(3)
    dws[2] = matmul(x_t[...], dv[...]).astype(bf16)
    start_own(2)
    start_first(2)
    run[0, 7:8, :] = column_total(dv[...])
    small_send(0, sibling)
    stage1(0, 0)
    stage1(1, 0)
    send_own(4)
    send_own(5)
    stage1(0, 1)
    stage1(1, 1)
    send_own(6)
    send_own(7)
    tick(0)
    stage1(0, 2)
    stage1(1, 2)
    small_add(0)
    small_send(1, over_x)
    tick(1)
    tick(2)
    tick(3)
    stage2(0, 0)
    stage2(1, 0)
    tick(4)
    tick(5)
    small_add(1)
    small_send(2, over_y)
    tick(6)
    stage2(0, 1)
    stage2(1, 1)
    tick(7)
    tick(8)
    small_add(2)
    run_z[t] = run[3]
    for k, where in enumerate(along_z):
        copy = remote(run.at[3], run_z.at[t], sm.at[3 + k], rm.at[3 + t], where)
        copy.start()
        z_sent.append(copy)
    stage3(0, 0)
    stage3(1, 0)
    stage2(0, 2)
    stage2(1, 2)
    tick(9)
    tick(10)
    stage3(0, 1)
    stage3(1, 1)
    z_step(0, *ffn_z)
    tick(11)
    tick(12)
    z_step(1, *ffn_z)
    stage3(0, 2)
    stage3(1, 2)
    z_step(0, *attn_z)
    tick(13)
    tick(14)
    z_step(2, *ffn_z)
    z_step(1, *attn_z)
    tick(15)
    tick(16)
    z_step(2, *attn_z)
    for j in range(17, PIECES * last):
        tick(j)

    for k, where in enumerate(along_z):
        u = where[2]
        remote(run.at[3], run_z.at[u], sm.at[3 + k], rm.at[3 + u], where).wait_recv()
    total = run_z[0]
    for n in range(1, n_tensor):
        total = total + run_z[n]
    vec_out[...] = total[0:6, :]
    for n in range(n_tensor):

        @pl.when(t == n)
        def _():
            qv_out[...] = total[6:8, n * own_cols : (n + 1) * own_cols]
            hid_out[...] = total[8 + n : 9 + n, :]


    def emit_ffn(rows, total):
        for m in range(2):
            ffn_out[m, rows, :] = total[:, m * own_ff : (m + 1) * own_ff]

    def emit_attn(rows, total):
        for m in range(4):
            attn_out[m, rows, :] = total[:, m * own_cols : (m + 1) * own_cols]

    z_collect(*ffn_z, emit_ffn)
    z_collect(*attn_z, emit_attn)
    z_settle(*ffn_z)
    z_settle(*attn_z)

    for copy in swaps:
        copy.wait_send()
    for path, i in order:
        k = slot(path, i)
        for copy in first[k]:
            copy.wait_send()
        second[k].wait_send()
        third[k].wait_send()
    for copy in small + z_sent:
        copy.wait_send()

    @pl.when(core != c)
    def _():
        for i in range(PIECES):
            send_home(i).wait_send()

    for j in range(PIECES * last):
        settle(j)


def finish_all(n_tensor, grads, gh1, x, attn_full, dws, sums):
    rows = x.shape[0]
    own_cols, own_ff = D // n_tensor, FF // n_tensor
    dma = pltpu.SemaphoreType.DMA
    vmem, anywhere = pl.BlockSpec(memory_space=pltpu.VMEM), pl.BlockSpec(memory_space=pl.ANY)
    dq, dk_own, dk_far, dv_own, dv_far = grads
    tall = pltpu.VMEM((rows, D), bf16)
    items = PIECES * (n_tensor - 1)
    return pl.pallas_call(
        partial(finish_kernel, n_tensor),
        out_shape=[
            jax.ShapeDtypeStruct((4, STRIP, own_cols), f32),
            jax.ShapeDtypeStruct((2, STRIP, own_ff), f32),
            jax.ShapeDtypeStruct((6, D), f32),
            jax.ShapeDtypeStruct((2, own_cols), f32),
            jax.ShapeDtypeStruct((1, own_ff), f32),
            jax.ShapeDtypeStruct((n_tensor, rows, D), bf16),
        ],
        in_specs=[vmem, vmem, anywhere, vmem, anywhere, vmem, vmem, anywhere]
        + [anywhere] * 3
        + [vmem] * 2,
        out_specs=[vmem] * 5 + [anywhere],
        scratch_shapes=[
            tall,
            tall,
            tall,
            tall,
            pltpu.VMEM((D, rows), bf16),
            pltpu.VMEM((rows, D), f32),
            tall,
            pltpu.VMEM((3, D, D), bf16),
            pltpu.VMEM((6, 2, 2 * STRIP, WIDE), bf16),
            pltpu.VMEM((6, 2, 2 * STRIP, WIDE), bf16),
            pltpu.VMEM((3, 2 * STRIP, WIDE), bf16),
            pltpu.VMEM((3, 2, STRIP, WIDE), bf16),
            pltpu.VMEM((6, STRIP, WIDE), bf16),
            pltpu.VMEM((n_tensor, STRIP, 2 * own_ff), bf16),
            pltpu.VMEM((2, n_tensor, STRIP, 2 * own_ff), bf16),
            pltpu.VMEM((n_tensor, STRIP, 4 * own_cols), bf16),
            pltpu.VMEM((2, n_tensor, STRIP, 4 * own_cols), bf16),
            pltpu.VMEM((4, 16, D), f32),
            pltpu.VMEM((3, 16, D), f32),
            pltpu.VMEM((n_tensor, 16, D), f32),
            pltpu.VMEM((3, D, D), bf16),
            dma((2,)),
            dma((2,)),
            dma((24,)),
            dma((24,)),
            dma((24,)),
            dma((6,)),
            dma((6,)),
            dma((6,)),
            dma((6,)),
            dma((2 * n_tensor,)),
            dma((2 * n_tensor,)),
            dma((2 * n_tensor,)),
            dma((2 * n_tensor,)),
            dma((3 + n_tensor,)),
            dma((3 + n_tensor,)),
            dma((PIECES,)),
            dma((PIECES,)),
            dma((items + PIECES,)),
            dma((items + PIECES,)),
            dma((items + PIECES,)),
            dma((items + PIECES,)),
            dma((1,)),
        ],
        compiler_params=pltpu.CompilerParams(
            collective_id=1, has_side_effects=True, vmem_limit_bytes=VMEM_LIMIT
        ),
        cost_estimate=pl.CostEstimate(
            flops=12 * rows * D * D, bytes_accessed=400 * 2**20, transcendentals=0
        ),
        name="finish",
    )(dq, dk_own, dk_far, dv_own, dv_far, gh1, x, attn_full, *dws, *sums)


GROUP_RATES = (
    [2.0 / D**0.5] * 3 + [2.0 / (D // (4 * BLOCK)) ** 0.5],
    [2.0 / D**0.5, 2.0 / FF**0.5],
)


def last_kernel(tokens_ref, out_a, out_b, *refs):
    attn_g, attn_w, attn_m, attn_v, ffn_g, ffn_w, ffn_m, ffn_v = refs[:8]
    plain = [refs[8 + 4 * n : 12 + 4 * n] for n in range(3)]
    tokens_out, output = refs[20:22]
    attn_moment, attn_square, out_states, attn_new, attn_copy = refs[22:27]
    ffn_moment, ffn_square, ffn_new, ffn_copy = refs[27:31]
    plain_out = [refs[31 + 3 * n : 34 + 3 * n] for n in range(3)]
    step = pl.program_id(0)
    rows_a = out_a.shape[1]

    @pl.when(step == 0)
    def _():
        for m in range(4):
            moment, square, new = adam_update(
                attn_w[m], attn_m[m], attn_v[m], attn_g[m], GROUP_RATES[0][m], decay_rate
            )
            if m < 3:
                attn_moment[m], attn_square[m] = moment, square
            else:
                out_states[0], out_states[1] = moment, square
            attn_new[m], attn_copy[m] = new, new.astype(bf16)
        for m in range(2):
            moment, square, new = adam_update(
                ffn_w[m], ffn_m[m], ffn_v[m], ffn_g[m], GROUP_RATES[1][m], decay_rate
            )
            ffn_moment[m], ffn_square[m] = moment, square
            ffn_new[m], ffn_copy[m] = new, new.astype(bf16)
        for (g, w, m, v), outs in zip(plain, plain_out):
            for ref, value in zip(outs, adam_update(w[...], m[...], v[...], g[...], 0.5, 0.0)):
                ref[...] = value

    tokens_out[...] = tokens_ref[...].astype(f32)

    @pl.when(step % 2 == 0)
    def _():
        output[:, :rows_a] = out_a[...]

    @pl.when(step % 2 == 1)
    def _():
        output[:, rows_a:] = out_b[...]


def last(tokens_low, out_a, out_b, attn, ffn, plain):
    count, rows, _ = tokens_low.shape
    tile = lambda size, index: pl.BlockSpec((1, size, D), index)
    whole = lambda shape: pl.BlockSpec(
        shape, lambda i: (0,) * len(shape), pipeline_mode=pl.Buffered(1)
    )
    a, f = attn[0].shape, ffn[0].shape
    shapes = [
        ((3,) + a[1:], f32),
        ((3,) + a[1:], f32),
        ((2,) + a[1:], f32),
        (a, f32),
        (a, bf16),
        (f, f32),
        (f, f32),
        (f, f32),
        (f, bf16),
    ]
    for group in plain:
        shapes += [(group[0].shape, f32)] * 3
    inputs = list(attn) + list(ffn) + [array for group in plain for array in group]
    by_half = lambda i: (i // 2, i % 2, 0)
    by_one = lambda i: (i // 2, 0, 0)
    return pl.pallas_call(
        last_kernel,
        out_shape=[
            jax.ShapeDtypeStruct(tokens_low.shape, f32),
            jax.ShapeDtypeStruct(tokens_low.shape, bf16),
        ]
        + [jax.ShapeDtypeStruct(*entry) for entry in shapes],
        grid=(count * 2,),
        in_specs=[
            tile(rows // 2, by_half),
            tile(out_a.shape[1], by_one),
            tile(out_b.shape[1], by_one),
        ]
        + [whole(array.shape) for array in inputs],
        out_specs=[tile(rows // 2, by_half), tile(rows, by_one)]
        + [whole(shape) for shape, _ in shapes],
        compiler_params=pltpu.CompilerParams(vmem_limit_bytes=VMEM_LIMIT),
        name="last",
    )(tokens_low, out_a, out_b, *inputs)


def make_body(mesh):
    n_shard, n_ctx, n_tensor = mesh.shape["shard"], mesh.shape["ctx"], mesh.shape["tensor"]
    rows_axes = ("shard", "ctx")
    all_axes = ("shard", "ctx", "tensor")
    paired = n_ctx == 2 and n_shard == 4 and n_tensor == 4

    def swapped(s, c):
        return (s - s % 2 + c, s % 2)

    def swap(array):
        if not paired:
            return array
        pairs = []
        for s in range(n_shard):
            for c in range(n_ctx):
                s_to, c_to = swapped(s, c)
                pairs.append((s * n_ctx + c, s_to * n_ctx + c_to))
        return lax.ppermute(array, rows_axes, pairs)

    def spread(array):
        return lax.all_gather(swap(array), "tensor", axis=0, tiled=True)

    def body(
        tokens,
        cotangent,
        segments,
        rand_blocks,
        attn_w,
        attn_m,
        attn_v,
        ffn_w,
        ffn_m,
        ffn_v,
        qv_bias,
        qv_m,
        qv_v,
        hid_bias,
        hid_m,
        hid_v,
        vec_par,
        vec_m,
        vec_v,
    ):
        t_index = lax.axis_index("tensor")
        nseq = tokens.shape[0] // n_tensor
        piece_len = tokens.shape[1]
        nb = piece_len // BLOCK
        own_rows, own_cols = attn_w.shape[1], attn_w.shape[2]
        own_ff = ffn_w.shape[2]

        def mine(array):
            return lax.dynamic_slice_in_dim(array, t_index * nseq, nseq, 0)

        ints = jnp.concatenate(
            [mine(segments), mine(rand_blocks).reshape(nseq, -1)], axis=1
        )
        ints = swap(ints)
        length = segments.shape[1]
        segs, rand = ints[:, :length], ints[:, length:].reshape(nseq, length // BLOCK, -1)
        piece = lax.axis_index("shard") % 2 if paired else lax.axis_index("ctx")
        tables = attention_tables(segs, rand, piece, nb, paired)

        if paired:
            rand_own, _meta, table = tables
            attn_full, ffn_full, hid_all, x, queries, keys, values, mixed, lse = start(
                n_tensor, attn_w, ffn_w, qv_bias, hid_bias, table[0], rand_own, tokens
            )
            flat = x
            x, queries = x[None], queries[None]
            keys, values = keys.reshape(1, length, D), values.reshape(1, length, D)
            pieces = [piece_len, piece_len]
        else:
            x, cot = mine(tokens), mine(cotangent)
            pieces = [length]
            ffn_z = lax.all_gather(ffn_w.astype(bf16), "tensor", axis=0, tiled=False)
            ffn_z = ffn_z.transpose(1, 2, 0, 3).reshape(2, own_rows, FF)
            ffn_full = lax.all_gather(ffn_z, rows_axes, axis=1, tiled=True)
            flat = x.reshape(-1, D)
            attn_low = attn_w.astype(bf16)
            attn_low = jnp.concatenate([attn_low[i] for i in range(4)], axis=1)
            attn_z = lax.all_gather(attn_low, "tensor", axis=0, tiled=False)
            attn_z = attn_z.reshape(n_tensor, own_rows, 4, own_cols).transpose(2, 1, 0, 3)
            attn_full = lax.all_gather(
                attn_z.reshape(4, own_rows, D), rows_axes, axis=1, tiled=True
            )
            bias_own = jnp.concatenate([qv_bias.reshape(-1), hid_bias])
            bias_all = lax.all_gather(bias_own, "tensor", axis=0, tiled=False)
            qv_all = bias_all[:, : 2 * own_cols].reshape(n_tensor, 2, own_cols)
            qv_all = qv_all.transpose(1, 0, 2).reshape(2, D)
            hid_all = bias_all[:, 2 * own_cols :].reshape(FF)
            keys = matmul(flat, attn_full[1]).astype(bf16).reshape(x.shape)
            values = (matmul(flat, attn_full[2]) + qv_all[1]).astype(bf16).reshape(x.shape)
            keys = lax.all_gather(keys, "ctx", axis=1, tiled=True)
            values = lax.all_gather(values, "ctx", axis=1, tiled=True)
            queries = (matmul(flat, attn_full[0]) + qv_all[0]).astype(bf16) * 0.125
            queries = queries.reshape(x.shape)
            mixed, lse = attend(tables, queries, keys, values)
        mixed_low = mixed.reshape(-1, D)
        if paired:
            out_a, out_b, dw1, dw2, dwo, grad_first_in, grad_mixed, hid_sum, vec_sums = middle(
                n_tensor, flat, mixed_low, hid_all, vec_par, cotangent, attn_full, ffn_full
            )
            out_b = lax.all_gather(out_b, "tensor", axis=0, tiled=False)
        else:
            act, slope, h1, result, grad_second, second_sums = feed_forward(
                flat, mixed_low, cot.reshape(-1, D), attn_full, ffn_full, hid_all, vec_par
            )
            output = spread(result.reshape(x.shape))
            dw1, dw2, dwo, grad_first_in, grad_mixed, hid_sum, first_sums = feed_back(
                grad_second, h1, mixed_low, attn_full, ffn_full, act, slope, vec_par
            )

        grad_mixed = grad_mixed.reshape(x.shape)
        grad_query, dk_parts, dv_parts = attend_back(
            tables,
            queries,
            grad_mixed,
            mixed.reshape(x.shape),
            lse.reshape(nseq, nb, 8, ROWS),
            keys,
            values,
            pieces,
        )

        grad_query_low = grad_query.reshape(-1, D)
        if paired:
            attn_grad, ffn_grad, vec_grad, qv_grad, hid_grad, grad_tokens = finish_all(
                n_tensor,
                [grad_query_low] + [part[0] for part in list(dk_parts) + list(dv_parts)],
                grad_first_in,
                flat,
                attn_full,
                (dw1, dw2, dwo),
                (vec_sums, hid_sum),
            )
        else:
            grad_keys = lax.psum_scatter(dk_parts[0], "ctx", scatter_dimension=1, tiled=True)
            grad_values = lax.psum_scatter(dv_parts[0], "ctx", scatter_dimension=1, tiled=True)
            grad_keys_low = grad_keys.reshape(-1, D)
            grad_values_low = grad_values.reshape(-1, D)
            into_tokens = (
                matmul_nt(grad_query_low, attn_full[0])
                + matmul_nt(grad_keys_low, attn_full[1])
                + matmul_nt(grad_values_low, attn_full[2])
            )
            grad_tokens = spread((grad_first_in + into_tokens).astype(bf16).reshape(x.shape))
            dwq = matmul_tn(flat, grad_query_low).astype(bf16)
            dwk = matmul_tn(flat, grad_keys_low).astype(bf16)
            dwv = matmul_tn(flat, grad_values_low).astype(bf16)
            small = jnp.concatenate(
                [
                    first_sums[0],
                    first_sums[1],
                    second_sums[0],
                    second_sums[1],
                    first_sums[2],
                    second_sums[2],
                    column_sum(grad_query_low),
                    column_sum(grad_values_low),
                    hid_sum[0],
                ]
            )
            ffn_grad = lax.psum_scatter(
                jnp.stack([dw1, dw2]), rows_axes, scatter_dimension=1, tiled=True
            )
            ffn_grad = ffn_grad.reshape(2, own_rows, n_tensor, own_ff).transpose(2, 0, 1, 3)
            ffn_grad = lax.psum_scatter(ffn_grad, "tensor", scatter_dimension=0, tiled=False)
            ffn_grad = ffn_grad.astype(f32)
            attn_grad = lax.psum_scatter(
                jnp.stack([dwq, dwk, dwv, dwo]), rows_axes, scatter_dimension=1, tiled=True
            )
            attn_grad = attn_grad.reshape(4, own_rows, n_tensor, own_cols).transpose(2, 1, 0, 3)
            attn_grad = lax.psum_scatter(
                attn_grad.reshape(n_tensor, own_rows, D), "tensor", scatter_dimension=0
            )
            attn_grad = attn_grad.reshape(own_rows, 4, own_cols).transpose(1, 0, 2).astype(f32)
            small = lax.psum(small, all_axes)
            vec_grad = small[: 6 * D].reshape(6, D)
            qv_grad = lax.dynamic_slice_in_dim(
                small[6 * D : 8 * D].reshape(2, D), t_index * own_cols, own_cols, 1
            )
            hid_grad = lax.dynamic_slice_in_dim(
                small[8 * D : 8 * D + FF], t_index * own_ff, own_ff, 0
            )
            out_a, out_b = output[:, : piece_len // 2], output[:, piece_len // 2 :]

        row = lambda array: array.reshape(1, own_ff)
        grad_tokens, output, *updated = last(
            grad_tokens,
            out_a,
            out_b,
            (attn_grad, attn_w, attn_m, attn_v),
            (ffn_grad, ffn_w, ffn_m, ffn_v),
            [
                (qv_grad, qv_bias, qv_m, qv_v),
                (row(hid_grad), row(hid_bias), row(hid_m), row(hid_v)),
                (vec_grad, vec_par, vec_m, vec_v),
            ],
        )
        updated[12:15] = [array.reshape(own_ff) for array in updated[12:15]]
        return (output, grad_tokens, *updated)

    return body


def solution(mesh):
    rows = P("shard", "ctx", None)
    weight = P(None, ("shard", "ctx"), "tensor")
    in_specs = (
        (rows, rows, P("shard", None), P("shard", None, None))
        + (weight,) * 6
        + (P(None, "tensor"),) * 3
        + (P("tensor"),) * 3
        + (P(),) * 3
    )
    out_specs = (
        (rows, rows)
        + (weight,) * 9
        + (P(None, "tensor"),) * 3
        + (P("tensor"),) * 3
        + (P(),) * 3
    )
    return jax.shard_map(
        make_body(mesh), mesh=mesh, in_specs=in_specs, out_specs=out_specs, check_vma=False
    )
```

time: 2420 us -> 417 us (0.17)
  waiting for transfers between devices: 1140 us -> 0.04 us
  local copies, waits for them, and re-layouts: 716 us -> 4.17 us
  Pallas kernels: 0 us -> 387 us
  matrix products: 322 us -> 0 us
  other arithmetic: 187 us -> 5.93 us
    psum x4 -> x0, waiting for transfers between devices: 1080 us -> none  [the longest x1 424 us: micro_step(): branch = lax.psum(matmul_nt(mixed_low, attn_full[3]), 'tensor') + vec_par[4]]
    reshape x42 -> x6, local copies, waits for them, and re-layouts: 397 us -> 3.23 us  [the longest x1 1.27 us: start(): hid_bias.reshape(1, own_ff)]
    pallas_call x0 -> x5, Pallas kernels: none -> 387 us  [the longest x1 147 us: finish_all(): pl.pallas_call(partial(finish_kernel, n_tensor), out_shape=[jax.ShapeDtyp...]
    dot_general x66 -> x0, matrix products: 322 us -> none  [the longest x12 81.8 us: matmul(): return jnp.dot(left, right, preferred_element_type=jnp.float32)]
    gather x8 -> x0, local copies, waits for them, and re-layouts: 92.6 us -> none  [take_blocks(): block_table[picked_ids]]
    reduce_sum x23 -> x0, other arithmetic: 88.7 us -> none  [the longest x4 37 us: layer_norm(): centred = hidden - jnp.mean(hidden, axis=-1, keepdims=True)]
    mul x4 -> x0, local copies, waits for them, and re-layouts: 62.9 us -> none  [the longest x2 57.6 us: attend_backward(): jnp.einsum('sbhqk,sbqhd->sbkhd', grad_scores, query_blocks, preferred_ele...]
    transpose x4 -> x0, local copies, waits for them, and re-layouts: 62.4 us -> none  [the longest x2 58 us: attend_backward(): jnp.einsum('sbhqk,sbqhd->sbkhd', probs.astype(jnp.bfloat16), grad_sparse,...]
  transfers between devices with their start and end apart: 16 -> 2, of which waited for: 8 -> 0; matrix products, arithmetic and copies ran while one was open for 24% -> 1% of each run, Pallas kernels for 0% -> 47%
where the time goes in v1:
time: 417 us; the launch traced here: 412 us
  Pallas kernels  387 us (93%)
  between operations  14.4 us (3%)
  other arithmetic  5.93 us (1%)
  local copies, waits for them, and re-layouts  4.17 us (1%)
    pallas_call x1, Pallas kernels, finish_all(): pl.pallas_call(partial(finish_kernel, n_tensor), out_shape=[jax.ShapeDtyp...  147 us
    pallas_call x1, Pallas kernels, start(): pl.pallas_call(partial(start_kernel, n_tensor), out_shape=[jax.ShapeDtype...  94.1 us
    pallas_call x1, Pallas kernels, middle(): pl.pallas_call(partial(middle_kernel, n_tensor), out_shape=[jax.ShapeDtyp...  80.7 us
    pallas_call x1, Pallas kernels, attend_back(): pl.pallas_call(partial(backward_kernel, len(pieces)), out_shape=[jax.Shap...  47.2 us
    pallas_call x1, Pallas kernels, last(): pl.pallas_call(last_kernel, out_shape=[jax.ShapeDtypeStruct(tokens_low.sh...  18.1 us
  transfers between devices with their start and end apart: 2, of which 0 were waited for; matrix products, arithmetic and copies ran while one was open for 1% of the time, Pallas kernels for 47%

profile of v1, /device:TPU:0, one launch (start us, length us, event | category | flops | bytes accessed | tf_op | source)
XLA Modules:
  0.0 411.9 jit_solution(412481465323575094)
XLA Ops:
  7.2 0.0 copy-start
  7.2 0.0 all-gather.3.cloned.1.call-start
  7.3 0.7 constant_dynamic-slice_fusion.1
  8.0 0.1 copy.40
  8.0 0.1 reshape.94
  8.2 0.7 collective-permute-start
  8.9 1.3 reshape.97.refs_3_.refs_13_
  10.2 0.0 collective-permute-done
  10.2 0.1 convert_element_type.15
  10.3 0.1 pad_maximum_fusion
  10.4 0.1 reshape.95
  10.5 0.6 reshape.96.refs_5_.rand
  11.1 0.7 fusion.2.refs_4_
  11.8 94.1 %start.1 = (bf16[4,768,768]{2,1,0:T(8,128)(2,1)}, bf16[2,768,3072]{2,1,0:T(8,128)(2,1)}, f32[1,3072]{1,0:T(1,128)}, bf16[1024,768]{1,0:T(8,128)(2,1)}, bf16[1024...) custom-call(f32[4,96,192]{2,1,0:T(8,128)} %refs_1_.3, ...), custom_call_target="tpu_custom_call" | custom-call | flops 3623878656 | bytes 104857600 | tf_op jit(solution)/shard_map/start/pallas_call | solution.py:1080
  105.9 0.0 copy-start.2
  105.9 0.0 copy-start.3
  105.9 80.7 %middle.1 = (bf16[4,640,768]{2,1,0:T(8,128)(2,1)}, bf16[384,768]{1,0:T(8,128)(2,1)}, bf16[768,3072]{1,0:T(8,128)(2,1)}, bf16[768,3072]{1,0:T(8,128)(2,1)}, bf16[...) custom-call(bf16[1024,768]{1,0:T(8,128)(2,1)} %get-tuple-element.70., ...), custom_call_target="tpu_custom_call" | custom-call | flops 32614907904 | bytes 62914560 | tf_op jit(solution)/shard_map/middle/pallas_call | solution.py:1375
  186.6 0.0 all-gather.3.cloned.1.call-update
  186.7 0.0 copy-done.2
  186.7 0.6 reshape.102.refs_14_
  187.3 0.0 copy-done.3
  187.3 0.6 reshape.103.refs_15_
  187.8 0.6 pad_add_fusion.1.meta
  188.4 0.7 fusion.tab_ref
  189.1 47.2 %attend_back.1 = (bf16[1,1024,768]{2,1,0:T(8,128)(2,1)}, bf16[1,1024,768]{2,1,0:T(8,128)(2,1)}, bf16[1,1024,768]{2,1,0:T(8,128)(2,1)}, bf16[1,1024,768]{2,1,0:T(8,128)(2,1)}, bf16[1,1024,768]{2,1,0:T(8,128)(2,1)}) custom-call(s32[48]{0:T(128)} %reshape.96.refs_5_.rand, s32[2]{0:T(128)} %pad_add_fusion.1.meta, bf16[1,1024,768]{2,1,0:T(8,128)(2,1)} %bitcast.26, ...), custom_call_target="tpu_custom_call" | custom-call | flops 16106127360 | bytes 17301504 | tf_op jit(solution)/shard_map/attend_back/pallas_call | solution.py:367
  236.3 146.5 %finish.1 = (f32[4,96,192]{2,1,0:T(8,128)}, f32[2,96,768]{2,1,0:T(8,128)}, f32[6,768]{1,0:T(8,128)}, f32[2,192]{1,0:T(2,128)}, f32[1,768]{1,0:T(1,128)}, /*index=5*/bf16[4,1024,768]{2,1,0:T(8,128)(2,1)}) custom-call(bf16[1024,768]{1,0:T(8,128)(2,1)} %bitcast.17, bf16[1024,768]{1,0:T(8,128)(2,1)} %bitcast.18, bf16[1024,768]{1,0:T(8,128)(2,1)} %bitcast.19, ...), custom_call_target="tpu_custom_call" | custom-call | flops 7247757312 | bytes 419430400 | tf_op jit(solution)/shard_map/finish/pallas_call | solution.py:1862
  382.8 0.0 all-gather.3.cloned.1.call-done
  382.9 0.0 copy-start.1
  382.9 18.1 %last.1 = (f32[4,1024,768]{2,1,0:T(8,128)}, bf16[4,1024,768]{2,1,0:T(8,128)(2,1)}, f32[3,96,192]{2,1,0:T(8,128)}, f32[3,96,192]{2,1,0:T(8,128)}, f32[2,96,192]{2...) custom-call(bf16[4,1024,768]{2,1,0:T(8,128)(2,1)} %get-tuple-element, ...), custom_call_target="tpu_custom_call" | custom-call | tf_op jit(solution)/shard_map/last/pallas_call | solution.py:2002
  401.0 1.3 reduce.2
  402.3 1.3 reduce.3
  403.6 1.3 reduce.4
  (7 shorter events, 0.1 us)
Async XLA Ops:
  7.2 1.0 copy-start
  7.2 375.7 %all-gather.3.cloned.1.call-start = ((), (), s32[]{:S(2)}) async-start(), calls=%async_computation | async-start | bytes 2949120 | tf_op jit(solution)/shard_map/all_gather | solution.py:2125
  8.2 2.0 collective-permute-start
  105.9 80.8 %copy-start.2 = (f32[768]{0:T(1024)S(1)}, f32[768]{0:T(1024)}, u32[]{:S(2)}) copy-start(f32[768]{0:T(1024)} %param.33) | copy-start | bytes 9220
  105.9 81.3 %copy-start.3 = (f32[768]{0:T(1024)S(1)}, f32[768]{0:T(1024)}, u32[]{:S(2)}) copy-start(f32[768]{0:T(1024)} %param.34) | copy-start | bytes 9220
  382.9 22.0 %copy-start.1 = (s32[4,2048]{1,0:T(4,128)S(1)}, s32[4,2048]{1,0:T(4,128)}, u32[]{:S(2)}) copy-start(s32[4,2048]{1,0:T(4,128)} %param.21) | copy-start | bytes 98308
Sparse Core Ops, SparseCore 0:
  186.8 60.7 all-gather.2

commit v2 on v1

--- a/solution.py
+++ b/solution.py
@@ -711,14 +711,18 @@
 
 
 class Line:
-    def __init__(self, s, c, t, last, items, rows, array, up, down):
+    def __init__(self, s, c, t, last, items, rows, array, out, up, down, copied):
         self.s, self.c, self.t, self.last, self.items = s, c, t, last, items
-        self.rows, self.array, self.up, self.down = rows, array, up, down
+        self.rows, self.array, self.out, self.up, self.down = rows, array, out, up, down
+        self.copied = copied
 
     def hop(self, i, src_t, sems, n, to):
         ref = self.array.at[src_t, pl.ds(i * self.rows, self.rows)]
         return remote(ref, ref, sems[0].at[n], sems[1].at[n], (self.s, self.c, to))
 
+    def keep(self, src_t, n):
+        return pltpu.make_async_copy(self.array.at[src_t], self.out.at[src_t], self.copied.at[n])
+
     def send_own(self, i):
         t = self.t
 
@@ -730,6 +734,9 @@
         def _():
             self.hop(i, t, self.down, i, t - 1).start()
 
+        if i == self.items - 1:
+            self.keep(t, 2 * self.last).start()
+
     def tick(self, j):
         t, last = self.t, self.last
         i, hops, n = j % self.items, j // self.items + 1, j + self.items
@@ -742,6 +749,9 @@
             def _():
                 self.hop(i, t - hops, self.up, n, t + 1).start()
 
+            if i == self.items - 1:
+                self.keep(t - hops, hops - 1).start()
+
         @pl.when(t + hops <= last)
         def _():
             self.hop(i, t + hops, self.down, j, t + 1).wait_recv()
@@ -750,23 +760,38 @@
             def _():
                 self.hop(i, t + hops, self.down, n, t - 1).start()
 
-    def settle(self, j):
+            if i == self.items - 1:
+                self.keep(t + hops, last + hops - 1).start()
+
+    def settle(self):
         t, last = self.t, self.last
-        i, hops = j % self.items, j // self.items
-
-        @pl.when((t < last) & (t >= hops))
-        def _():
-            self.hop(i, t - hops, self.up, j, t + 1).wait_send()
-
-        @pl.when((t > 0) & (t + hops <= last))
-        def _():
-            self.hop(i, t + hops, self.down, j, t - 1).wait_send()
+        for j in range(self.items * last):
+            i, hops = j % self.items, j // self.items
+
+            @pl.when((t < last) & (t >= hops))
+            def _():
+                self.hop(i, t - hops, self.up, j, t + 1).wait_send()
+
+            @pl.when((t > 0) & (t + hops <= last))
+            def _():
+                self.hop(i, t + hops, self.down, j, t - 1).wait_send()
+
+        self.keep(t, 2 * last).wait()
+        for hops in range(1, last + 1):
+
+            @pl.when(t >= hops)
+            def _():
+                self.keep(t - hops, hops - 1).wait()
+
+            @pl.when(t + hops <= last)
+            def _():
+                self.keep(t + hops, last + hops - 1).wait()
 
 
 def start_kernel(n_tensor, *refs):
     attn_ref, ffn_ref, qv_ref, hid_ref, tab_ref, rand, tokens = refs[:7]
     attn_out, ffn_out, hid_out, x_out, q_out, k_out, v_out, mixed_out, lse_out = refs[7:16]
-    low, low_z, bias, bias_z, bias_qv, ffn_low, full, xs, qs, ms, k_buf, v_buf, s_buf = refs[16:29]
+    low, low_z, bias, bias_z, bias_qv, ffn_low, full, xs, qs, ms, k_buf, v_buf, s_buf, ffn_full = refs[16:30]
     (
         z_send,
         z_recv,
@@ -787,7 +812,7 @@
         kv_send,
         kv_recv,
         own_sem,
-    ) = refs[29:]
+    ) = refs[30:]
     s, c, t, x, core, sibling, over_x, over_y, across, along_z = places(n_tensor)
     own_cols, own_ff = D // n_tensor, FF // n_tensor
     n_rows = xs.shape[0]
@@ -869,7 +894,7 @@
         return full.at[pl.ds(2 * path, 2), at, :]
 
     def ffn_block(path, at):
-        return ffn_out.at[path, at, :]
+        return ffn_full.at[path, at, :]
 
     class Gather:
         def __init__(self, block, ways, gs, gr, ps, pr):
@@ -929,7 +954,7 @@
     ffn = Gather(ffn_block, (0, 1), fg_send, fg_recv, fp_send, fp_recv)
 
     def ffn_cols(path, u):
-        return ffn_out.at[path, here, pl.ds(pl.multiple_of(u * own_ff, own_ff), own_ff)]
+        return ffn_full.at[path, here, pl.ds(pl.multiple_of(u * own_ff, own_ff), own_ff)]
 
     def ffn_hop(path, k, u):
         n = path * n_tensor
@@ -1059,8 +1084,9 @@
     write(ms, mixed_out, 7)
     for path, number in [move for moves in stops.values() for move in moves]:
         ffn.again(path, number)
-    ffn.take_shared(0)
-    ffn.take_shared(1)
+    for path in range(2):
+        ffn.take_shared(path)
+        write(ffn_full.at[path], ffn_out.at[path], 8 + path)
 
     for copy in sent:
         copy.wait_send()
@@ -1106,6 +1132,7 @@
             pltpu.VMEM((2 * rows // BLOCK, BLOCK, D), bf16),
             pltpu.VMEM((2 * rows // BLOCK, BLOCK, D), bf16),
             pltpu.VMEM((2 * rows // KEYS, ROWS, KEYS), f32),
+            pltpu.VMEM((2, D, FF), bf16),
             dma((2 * n_tensor,)),
             dma((2 * n_tensor,)),
             dma((n_tensor,)),
@@ -1124,7 +1151,7 @@
             dma((8,)),
             dma((items,)),
             dma((items,)),
-            dma((8,)),
+            dma((10,)),
         ],
         compiler_params=pltpu.CompilerParams(
             collective_id=2, has_side_effects=True, vmem_limit_bytes=VMEM_LIMIT
@@ -1139,7 +1166,7 @@
 def middle_kernel(n_tensor, *refs):
     x_ref, mixed_ref, hid_ref, vec_ref, cotangent, attn_full, ffn_full = refs[:7]
     out_a, out_b, dw1, dw2, dwo, gh1, gm, hid_out, sums_out = refs[7:16]
-    w, wo, act, slope, h1, total, gs_low, low_t, turned, pre, dw_s, cot, ready, low, down = refs[16:31]
+    w, wo, act, slope, h1, total, gs_low, low_t, turned, pre, dw_s, cot, ready, low, down, held = refs[16:32]
     (
         w_sem,
         c_send,
@@ -1152,7 +1179,8 @@
         dn_recv,
         dw_sem,
         own_sem,
-    ) = refs[31:]
+        copied,
+    ) = refs[32:]
     s, c, t, x, core, sibling, over_x, over_y, across, along_z = places(n_tensor)
     n_rows = x_ref.shape[0]
     chunk = 256
@@ -1185,7 +1213,7 @@
 
     def home_ref(i):
         if i < items:
-            return out_a.at[t, pl.ds(i * ITEM, ITEM)]
+            return held.at[t, pl.ds(i * ITEM, ITEM)]
         return out_b.at[pl.ds((i - items) * ITEM, ITEM)]
 
     def keep_home(i):
@@ -1207,7 +1235,7 @@
     if_home(lambda: keep_cot().start(), lambda: swap_cot().start())
 
     up, down_line = (up_send, up_recv), (dn_send, dn_recv)
-    chain = Line(s, c, t, last, items, ITEM, out_a, up, down_line)
+    chain = Line(s, c, t, last, items, ITEM, held, out_a, up, down_line, copied)
 
     def own_ready(i):
         if_home(lambda: keep_home(i).wait(), lambda: send_home(i).wait_recv())
@@ -1359,8 +1387,7 @@
         def _():
             send_home(i).wait_send()
 
-    for j in range(items * last):
-        chain.settle(j)
+    chain.settle()
     for copy in local:
         copy.wait()
 
@@ -1403,6 +1430,7 @@
             low,
             pltpu.VMEM((256, D), bf16),
             pltpu.VMEM((256, D), f32),
+            pltpu.VMEM((n_tensor, items * ITEM, D), bf16),
             dma((2 * steps + 1,)),
             dma((1,)),
             dma((1,)),
@@ -1414,6 +1442,7 @@
             dma((items * n_tensor,)),
             dma((4,)),
             dma((3,)),
+            dma((2 * n_tensor - 1,)),
         ],
         compiler_params=pltpu.CompilerParams(
             collective_id=3, has_side_effects=True, vmem_limit_bytes=VMEM_LIMIT
@@ -1432,10 +1461,10 @@
     dw1, dw2, dwo, vec_sums, hid_sums = refs[8:13]
     attn_out, ffn_out, vec_out, qv_out, hid_out, tokens_out = refs[13:19]
     (
-        dk_got,
-        dv_got,
         dk,
         dv,
+        xs,
+        held,
         x_t,
         partial_sum,
         ready,
@@ -1477,6 +1506,7 @@
         dn_send,
         dn_recv,
         w_sem,
+        copied,
     ) = refs[40:]
     s, c, t, x, core, sibling, over_x, over_y, across, along_z = places(n_tensor)
     n_rows = dq.shape[0]
@@ -1531,64 +1561,60 @@
             for copy in first[slot(path, i)]:
                 copy.start()
 
-    fetch = pltpu.make_async_copy(weights.at[pl.ds(0, 3)], wts, w_sem.at[0])
-    fetch.start()
+    fetches = [
+        pltpu.make_async_copy(gh1, partial_sum, w_sem.at[1]),
+        pltpu.make_async_copy(weights.at[pl.ds(0, 3)], wts, w_sem.at[0]),
+        pltpu.make_async_copy(x_ref, xs, w_sem.at[2]),
+    ]
+    for copy in fetches:
+        copy.start()
     start_own(0)
     start_own(1)
     greet([sibling, over_x, over_y, across] + along_z)
 
-    swaps = [
-        remote(dk_far, dk_got, e_send.at[0], e_recv.at[0], sibling),
-        remote(dv_far, dv_got, e_send.at[1], e_recv.at[1], sibling),
-    ]
+    chunk = 256
+    chunks = n_rows // chunk
+
+    def exchange(i, n):
+        at = pl.ds(i * chunk, chunk)
+        src, dst = ((dk_far, dk), (dv_far, dv))[n]
+        k = 2 * i + n
+        return remote(src.at[at], dst.at[at], e_send.at[k], e_recv.at[k], sibling)
+
+    swaps = [exchange(i, n) for i in range(chunks) for n in range(2)]
     for copy in swaps:
         copy.start()
     start_first(0)
-
-    fetch.wait()
-    chunk = 256
-    for i in range(n_rows // chunk):
-        at = slice(i * chunk, (i + 1) * chunk)
-        partial_sum[at, :] = gh1[at, :] + matmul_nt(dq[at, :], wts[0])
-        x_t[:, at] = x_ref[at, :].T
+    fetches[0].wait()
+    fetches[1].wait()
+
     run[0] = jnp.zeros(run.shape[1:], f32)
     run[0, 0:6, :] = vec_sums[0:6, :]
-    run[0, 6:7, :] = column_total(dq[...])
     for n in range(FF // D):
         run[0, 8 + n : 9 + n, :] = hid_sums[:, n * D : (n + 1) * D]
 
-    for copy in swaps:
-        copy.wait_recv()
-
     def keep_home(i):
         at = pl.ds(i * rows_each, rows_each)
-        return pltpu.make_async_copy(ready.at[at], tokens_out.at[t, at], h_recv.at[i])
+        return pltpu.make_async_copy(ready.at[at], held.at[t, at], h_recv.at[i])
 
     def send_home(i):
         at = pl.ds(i * rows_each, rows_each)
-        return remote(ready.at[at], tokens_out.at[t, at], h_send.at[i], h_recv.at[i], across)
-
-    for i in range(PIECES):
-        at = slice(i * rows_each, (i + 1) * rows_each)
-        dk_piece = (dk_own[at, :].astype(f32) + dk_got[at, :].astype(f32)).astype(bf16)
-        dv_piece = (dv_own[at, :].astype(f32) + dv_got[at, :].astype(f32)).astype(bf16)
-        dk[at, :] = dk_piece
-        dv[at, :] = dv_piece
-        total = partial_sum[at, :] + matmul_nt(dk_piece, wts[1]) + matmul_nt(dv_piece, wts[2])
-        ready[at, :] = total.astype(bf16)
-
-        @pl.when(core == c)
-        def _():
-            keep_home(i).start()
-
-        @pl.when(core != c)
-        def _():
-            send_home(i).start()
+        return remote(ready.at[at], held.at[t, at], h_send.at[i], h_recv.at[i], across)
 
     chain = Line(
-        s, c, t, last, PIECES, rows_each, tokens_out, (up_send, up_recv), (dn_send, dn_recv)
+        s,
+        c,
+        t,
+        last,
+        PIECES,
+        rows_each,
+        held,
+        tokens_out,
+        (up_send, up_recv),
+        (dn_send, dn_recv),
+        copied,
     )
-    tick, settle = chain.tick, chain.settle
+    tick = chain.tick
 
     def send_own(i):
         @pl.when(core == c)
@@ -1600,6 +1626,30 @@
             send_home(i).wait_recv()
 
         chain.send_own(i)
+
+    for i in range(PIECES):
+        at = slice(i * rows_each, (i + 1) * rows_each)
+        if i * rows_each % chunk == 0:
+            for n in range(2):
+                exchange(i * rows_each // chunk, n).wait_recv()
+        dk_piece = (dk_own[at, :].astype(f32) + dk[at, :].astype(f32)).astype(bf16)
+        dv_piece = (dv_own[at, :].astype(f32) + dv[at, :].astype(f32)).astype(bf16)
+        dk[at, :] = dk_piece
+        dv[at, :] = dv_piece
+        total = partial_sum[at, :] + matmul_nt(dq[at, :], wts[0])
+        total = total + matmul_nt(dk_piece, wts[1]) + matmul_nt(dv_piece, wts[2])
+        ready[at, :] = total.astype(bf16)
+
+        @pl.when(core == c)
+        def _():
+            keep_home(i).start()
+
+        @pl.when(core != c)
+        def _():
+            send_home(i).start()
+
+        if i > 0:
+            send_own(i - 1)
 
     def add_rows(target, source, count):
         @pl.loop(0, count // 16)
@@ -1733,26 +1783,24 @@
         small[n].wait_recv()
         run[n + 1] = run[n] + run_got[n]
 
+    start_first(1)
+    fetches[2].wait()
+    for i in range(chunks):
+        at = slice(i * chunk, (i + 1) * chunk)
+        x_t[:, at] = xs[at, :].T
     dws[0] = matmul(x_t[...], dq[...]).astype(bf16)
-    send_own(0)
-    send_own(1)
-    start_first(1)
+    send_own(7)
     dws[1] = matmul(x_t[...], dk[...]).astype(bf16)
-    send_own(2)
-    send_own(3)
     dws[2] = matmul(x_t[...], dv[...]).astype(bf16)
     start_own(2)
     start_first(2)
+    run[0, 6:7, :] = column_total(dq[...])
     run[0, 7:8, :] = column_total(dv[...])
     small_send(0, sibling)
     stage1(0, 0)
     stage1(1, 0)
-    send_own(4)
-    send_own(5)
     stage1(0, 1)
     stage1(1, 1)
-    send_own(6)
-    send_own(7)
     tick(0)
     stage1(0, 2)
     stage1(1, 2)
@@ -1847,8 +1895,7 @@
         for i in range(PIECES):
             send_home(i).wait_send()
 
-    for j in range(PIECES * last):
-        settle(j)
+    chain.settle()
 
 
 def finish_all(n_tensor, grads, gh1, x, attn_full, dws, sums):
@@ -1869,15 +1916,14 @@
             jax.ShapeDtypeStruct((1, own_ff), f32),
             jax.ShapeDtypeStruct((n_tensor, rows, D), bf16),
         ],
-        in_specs=[vmem, vmem, anywhere, vmem, anywhere, vmem, vmem, anywhere]
-        + [anywhere] * 3
+        in_specs=[vmem, vmem, anywhere, vmem, anywhere] + [anywhere] * 6
         + [vmem] * 2,
         out_specs=[vmem] * 5 + [anywhere],
         scratch_shapes=[
             tall,
             tall,
             tall,
-            tall,
+            pltpu.VMEM((n_tensor, rows, D), bf16),
             pltpu.VMEM((D, rows), bf16),
             pltpu.VMEM((rows, D), f32),
             tall,
@@ -1895,8 +1941,8 @@
             pltpu.VMEM((3, 16, D), f32),
             pltpu.VMEM((n_tensor, 16, D), f32),
             pltpu.VMEM((3, D, D), bf16),
-            dma((2,)),
-            dma((2,)),
+            dma((2 * rows // 256,)),
+            dma((2 * rows // 256,)),
             dma((24,)),
             dma((24,)),
             dma((24,)),
@@ -1916,7 +1962,8 @@
             dma((items + PIECES,)),
             dma((items + PIECES,)),
             dma((items + PIECES,)),
-            dma((1,)),
+            dma((3,)),
+            dma((2 * n_tensor - 1,)),
         ],
         compiler_params=pltpu.CompilerParams(
             collective_id=1, has_side_effects=True, vmem_limit_bytes=VMEM_LIMIT
@@ -2206,7 +2253,6 @@
             )
             out_a, out_b = output[:, : piece_len // 2], output[:, piece_len // 2 :]
 
-        row = lambda array: array.reshape(1, own_ff)
         grad_tokens, output, *updated = last(
             grad_tokens,
             out_a,
@@ -2215,11 +2261,10 @@
             (ffn_grad, ffn_w, ffn_m, ffn_v),
             [
                 (qv_grad, qv_bias, qv_m, qv_v),
-                (row(hid_grad), row(hid_bias), row(hid_m), row(hid_v)),
+                (hid_grad.reshape(own_ff), hid_bias, hid_m, hid_v),
                 (vec_grad, vec_par, vec_m, vec_v),
             ],
         )
-        updated[12:15] = [array.reshape(own_ff) for array in updated[12:15]]
         return (output, grad_tokens, *updated)
 
     return body

time: 417 us -> 419 us (level)
    pallas_call x1, Pallas kernels: 147 us -> 136 us  [finish_all(): pl.pallas_call(partial(finish_kernel, n_tensor), out_shape=[jax.ShapeDtyp...]
    pallas_call x1, Pallas kernels: 47.2 us -> 55.3 us  [attend_back(): pl.pallas_call(partial(backward_kernel, len(pieces)), out_shape=[jax.Shap...]
  transfers between devices with their start and end apart: 2 -> 2, of which waited for: 0 -> 0; matrix products, arithmetic and copies ran while one was open for 1% -> 1% of each run, Pallas kernels for 47% -> 46%
where the time goes in v2:
time: 419 us; the launch traced here: 412 us
  Pallas kernels  390 us (93%)
  between operations  14.4 us (3%)
    pallas_call x1, Pallas kernels, finish_all(): pl.pallas_call(partial(finish_kernel, n_tensor), out_shape=[jax.ShapeDtyp...  136 us
    pallas_call x1, Pallas kernels, start(): pl.pallas_call(partial(start_kernel, n_tensor), out_shape=[jax.ShapeDtype...  96.6 us
    pallas_call x1, Pallas kernels, middle(): pl.pallas_call(partial(middle_kernel, n_tensor), out_shape=[jax.ShapeDtyp...  84.7 us
    pallas_call x1, Pallas kernels, attend_back(): pl.pallas_call(partial(backward_kernel, len(pieces)), out_shape=[jax.Shap...  55.3 us
    pallas_call x1, Pallas kernels, last(): pl.pallas_call(last_kernel, out_shape=[jax.ShapeDtypeStruct(tokens_low.sh...  18 us
  transfers between devices with their start and end apart: 2, of which 0 were waited for; matrix products, arithmetic and copies ran while one was open for 1% of the time, Pallas kernels for 46%

profile of v2, /device:TPU:0, one launch (start us, length us, event | category | flops | bytes accessed | tf_op | source)
XLA Modules:
  0.0 411.9 jit_solution(4671413670712548352)
XLA Ops:
  7.2 0.0 copy-start
  7.2 0.0 all-gather.3.cloned.1.call-start
  7.3 0.7 constant_dynamic-slice_fusion.1
  8.0 0.0 copy-done
  8.0 0.1 copy.40
  8.1 0.1 reshape.81
  8.2 0.7 collective-permute-start
  8.9 1.3 reshape.84.refs_3_
  10.1 0.0 collective-permute-done
  10.2 0.1 convert_element_type.15
  10.2 0.1 pad_maximum_fusion
  10.3 0.1 reshape.82
  10.5 0.6 reshape.83.refs_5_.rand
  11.1 0.7 fusion.2.refs_4_
  11.8 96.6 %start.1 = (bf16[4,768,768]{2,1,0:T(8,128)(2,1)}, bf16[2,768,3072]{2,1,0:T(8,128)(2,1)}, f32[1,3072]{1,0:T(1,128)}, bf16[1024,768]{1,0:T(8,128)(2,1)}, bf16[1024...) custom-call(f32[4,96,192]{2,1,0:T(8,128)} %refs_1_.3, ...), custom_call_target="tpu_custom_call" | custom-call | flops 3623878656 | bytes 104857600 | tf_op jit(solution)/shard_map/start/pallas_call | solution.py:1106
  108.3 84.7 %middle.1 = (bf16[4,640,768]{2,1,0:T(8,128)(2,1)}, bf16[384,768]{1,0:T(8,128)(2,1)}, bf16[768,3072]{1,0:T(8,128)(2,1)}, bf16[768,3072]{1,0:T(8,128)(2,1)}, bf16[...) custom-call(bf16[1024,768]{1,0:T(8,128)(2,1)} %get-tuple-element.70., ...), custom_call_target="tpu_custom_call" | custom-call | flops 32614907904 | bytes 62914560 | tf_op jit(solution)/shard_map/middle/pallas_call | solution.py:1402
  193.1 0.0 all-gather.3.cloned.1.call-update
  193.1 0.6 pad_add_fusion.1.meta
  193.7 0.7 fusion.tab_ref
  194.4 55.3 %attend_back.1 = (bf16[1,1024,768]{2,1,0:T(8,128)(2,1)}, bf16[1,1024,768]{2,1,0:T(8,128)(2,1)}, bf16[1,1024,768]{2,1,0:T(8,128)(2,1)}, bf16[1,1024,768]{2,1,0:T(8,128)(2,1)}, bf16[1,1024,768]{2,1,0:T(8,128)(2,1)}) custom-call(s32[48]{0:T(128)} %reshape.83.refs_5_.rand, s32[2]{0:T(128)} %pad_add_fusion.1.meta, bf16[1,1024,768]{2,1,0:T(8,128)(2,1)} %bitcast.26, ...), custom_call_target="tpu_custom_call" | custom-call | flops 16106127360 | bytes 17301504 | tf_op jit(solution)/shard_map/attend_back/pallas_call | solution.py:367
  249.7 135.8 %finish.1 = (f32[4,96,192]{2,1,0:T(8,128)}, f32[2,96,768]{2,1,0:T(8,128)}, f32[6,768]{1,0:T(8,128)}, f32[2,192]{1,0:T(2,128)}, f32[1,768]{1,0:T(1,128)}, /*index=5*/bf16[4,1024,768]{2,1,0:T(8,128)(2,1)}) custom-call(bf16[1024,768]{1,0:T(8,128)(2,1)} %bitcast.17, bf16[1024,768]{1,0:T(8,128)(2,1)} %bitcast.18, bf16[1024,768]{1,0:T(8,128)(2,1)} %bitcast.19, ...), custom_call_target="tpu_custom_call" | custom-call | flops 7247757312 | bytes 419430400 | tf_op jit(solution)/shard_map/finish/pallas_call | solution.py:1909
  385.5 1.3 reduce.2.refs_12_
  386.8 0.0 all-gather.3.cloned.1.call-done
  386.8 0.0 copy-start.1
  386.8 18.0 %last.1 = (f32[4,1024,768]{2,1,0:T(8,128)}, bf16[4,1024,768]{2,1,0:T(8,128)(2,1)}, f32[3,96,192]{2,1,0:T(8,128)}, f32[3,96,192]{2,1,0:T(8,128)}, f32[2,96,192]{2...) custom-call(bf16[4,1024,768]{2,1,0:T(8,128)(2,1)} %get-tuple-element, ...), custom_call_target="tpu_custom_call" | custom-call | tf_op jit(solution)/shard_map/last/pallas_call | solution.py:2049
  404.8 0.0 copy-done.1
  (5 shorter events, 0.1 us)
Async XLA Ops:
  7.2 0.8 copy-start
  7.2 379.6 %all-gather.3.cloned.1.call-start = ((), (), s32[]{:S(2)}) async-start(), calls=%async_computation | async-start | bytes 2949120 | tf_op jit(solution)/shard_map/all_gather | solution.py:2172
  8.2 2.0 collective-permute-start
  386.8 18.0 %copy-start.1 = (s32[4,2048]{1,0:T(4,128)S(1)}, s32[4,2048]{1,0:T(4,128)}, u32[]{:S(2)}) copy-start(s32[4,2048]{1,0:T(4,128)} %param.21) | copy-start | bytes 98308
Sparse Core Ops, SparseCore 0:
  193.2 58.7 all-gather.2

commit v3 on v2

--- a/solution.py
+++ b/solution.py
@@ -212,14 +212,17 @@
 
 
 def backward_kernel(
-    n_out, rand, meta, q_ref, go_ref, mixed_ref, lse_ref, tab_ref, k_all, v_all, dq_ref, *rest
+    n_out, rand, meta, q_ref, go_ref, mixed_ref, lse_ref, tab_ref, out_a, k_all, v_all, *rest
 ):
+    dq_ref, out_ref, *rest = rest
     dk_refs, dv_refs = rest[:n_out], rest[n_out : 2 * n_out]
     k_buf, v_buf, dk_acc, dv_acc, sems = rest[2 * n_out :]
     seq, blk = pl.program_id(0), pl.program_id(1)
     nb = pl.num_programs(1)
     total_blocks = k_buf.shape[0]
     chunks = total_blocks // LISTED
+
+    out_ref[...] = out_a[...]
 
     @pl.when(blk == 0)
     def _():
@@ -355,18 +358,31 @@
     )(rand, meta, q, table, as_blocks(keys), as_blocks(values))
 
 
-def attend_back(tables, q, grad_mixed, mixed, lse, keys, values, pieces):
+def attend_back(tables, q, grad_mixed, mixed, lse, out_a, keys, values, pieces):
     rand, meta, table = tables
     seq_count, piece_len, _ = q.shape
     nb = piece_len // BLOCK
     length = keys.shape[1]
     any_spec = pl.BlockSpec(memory_space=pl.ANY)
     row_spec = pl.BlockSpec((None, BLOCK, D), lambda s, b, *_: (s, b, 0))
+    count, half, _ = out_a.shape
+    share = count * half // (seq_count * nb)
+    if share <= half:
+        per = half // share
+        tile = pl.BlockSpec(
+            (None, share, D), lambda s, b, *_: ((s * nb + b) // per, (s * nb + b) % per, 0)
+        )
+    else:
+        tile = pl.BlockSpec((share // half, half, D), lambda s, b, *_: (s * nb + b, 0, 0))
     part_specs = [pl.BlockSpec((None, rows, D), lambda s, b, *_: (s, 0, 0)) for rows in pieces]
     part_shapes = [jax.ShapeDtypeStruct((seq_count, rows, D), bf16) for rows in pieces]
     out = pl.pallas_call(
         partial(backward_kernel, len(pieces)),
-        out_shape=[jax.ShapeDtypeStruct(q.shape, bf16)] + part_shapes * 2,
+        out_shape=[
+            jax.ShapeDtypeStruct(q.shape, bf16),
+            jax.ShapeDtypeStruct((count, 2 * half, D), bf16),
+        ]
+        + part_shapes * 2,
         grid_spec=pltpu.PrefetchScalarGridSpec(
             num_scalar_prefetch=2,
             grid=(seq_count, nb),
@@ -376,10 +392,11 @@
                 row_spec,
                 pl.BlockSpec((None, None, 8, ROWS), lambda s, b, *_: (s, b, 0, 0)),
                 pl.BlockSpec((None,) + table.shape[1:], lambda s, b, *_: (s, 0, 0, 0)),
+                tile,
                 any_spec,
                 any_spec,
             ],
-            out_specs=[row_spec] + part_specs * 2,
+            out_specs=[row_spec, tile] + part_specs * 2,
             scratch_shapes=[
                 pltpu.VMEM((length // BLOCK, BLOCK, D), bf16),
                 pltpu.VMEM((length // BLOCK, BLOCK, D), bf16),
@@ -395,8 +412,8 @@
             transcendentals=seq_count * nb * GROUPS * ROWS * KEYS,
         ),
         name="attend_back",
-    )(rand, meta, q, grad_mixed, mixed, lse, table, as_blocks(keys), as_blocks(values))
-    return out[0], out[1 : 1 + len(pieces)], out[1 + len(pieces) :]
+    )(rand, meta, q, grad_mixed, mixed, lse, table, out_a, as_blocks(keys), as_blocks(values))
+    return out[0], out[1], out[2 : 2 + len(pieces)], out[2 + len(pieces) :]
 
 
 def norm_parts(hidden):
@@ -677,7 +694,7 @@
 STRIP = 96
 PIECES = 8
 ITEM = 128
-LINE_ITEMS = 5
+LINE_ITEMS = 4
 MESH = pl.DeviceIdType.MESH
 
 
@@ -1029,7 +1046,6 @@
         k = matmul(xs[at, :], full[1]).astype(bf16)
         k_buf[pl.ds(i * per, per)] = k.reshape(per, BLOCK, D)
         put(kv_hop(k_buf, i, i))
-    ffn_ready(1)
     for i in range(chunks):
         at = pl.ds(i * chunk, chunk)
         q = matmul(xs[at, :], full[0]) + bias_qv[0:1, :]
@@ -1040,7 +1056,6 @@
         v = (matmul(xs[at, :], full[2]) + bias_qv[1:2, :]).astype(bf16)
         v_buf[pl.ds(i * per, per)] = v.reshape(per, BLOCK, D)
         put(kv_hop(v_buf, i, chunks + i))
-    ffn.step(0, 1)
     write(xs, x_out, 0)
     write(qs, q_out, 1)
     write(full, attn_out, 2)
@@ -1049,10 +1064,12 @@
         kv_hop(v_buf, i, chunks + i).wait_recv()
     write(k_buf, k_out, 3)
     write(v_buf, v_out, 4)
+    ffn_ready(1)
+    ffn.step(0, 1)
 
     nb = n_rows // BLOCK
     first = core * nb
-    stops = {0: [(1, 1)], 1: [(0, 2), (1, 2)], 9: [(0, 3), (1, 3)]}
+    stops = {1: [(1, 1), (0, 2)], 3: [(1, 2)], 10: [(0, 3), (1, 3)]}
 
     @pl.loop(0, nb)
     def _(blk):
@@ -1205,11 +1222,13 @@
 
     greet([over_y, across] + along_z)
 
-    def keep_cot():
-        return pltpu.make_async_copy(cotangent.at[t], cot, c_recv.at[0])
-
-    def swap_cot():
-        return remote(cotangent.at[t], cot, c_send.at[0], c_recv.at[0], across)
+    def keep_cot(i):
+        at = pl.ds(i * chunk, chunk)
+        return pltpu.make_async_copy(cotangent.at[t, at], cot.at[at], c_recv.at[i])
+
+    def swap_cot(i):
+        at = pl.ds(i * chunk, chunk)
+        return remote(cotangent.at[t, at], cot.at[at], c_send.at[i], c_recv.at[i], across)
 
     def home_ref(i):
         if i < items:
@@ -1232,7 +1251,7 @@
         def _():
             away()
 
-    if_home(lambda: keep_cot().start(), lambda: swap_cot().start())
+    if_home(lambda: keep_cot(0).start(), lambda: swap_cot(0).start())
 
     up, down_line = (up_send, up_recv), (dn_send, dn_recv)
     chain = Line(s, c, t, last, items, ITEM, held, out_a, up, down_line, copied)
@@ -1240,9 +1259,19 @@
     def own_ready(i):
         if_home(lambda: keep_home(i).wait(), lambda: send_home(i).wait_recv())
 
-    per = chunk // ITEM
-    for i in range(chunks):
-        rows = slice(i * chunk, (i + 1) * chunk)
+    events = {
+        (1, 1): ([0], []),
+        (2, 1): ([1], []),
+        (2, 2): ([2], []),
+        (2, 3): ([], [0]),
+        (3, 1): ([3], [1]),
+        (3, 3): ([], [2]),
+    }
+    sizes = [ITEM] + [chunk] * (chunks - 1) + [chunk - ITEM]
+    start_row = 0
+    for i, size in enumerate(sizes):
+        rows = slice(start_row, start_row + size)
+        top = slice(0, size)
         if i == 0:
             fetch_o.wait()
         pre1 = x_ref[rows, :].astype(f32) + matmul_nt(mixed_ref[rows, :], wo[...])
@@ -1250,46 +1279,51 @@
         h1[rows, :] = pre1
         unit, _scale = norm_parts(pre1)
         first = unit * vec_ref[0:1, :] + vec_ref[1:2, :]
-        low[...] = first.astype(bf16)
-        down[...] = first + vec_ref[5:6, :]
+        low[top, :] = first.astype(bf16)
+        down[top, :] = first + vec_ref[5:6, :]
 
         @pl.loop(0, steps)
         def _(j):
             if i == 0:
                 fetch(0, j).wait()
                 fetch(1, j).wait()
-            else:
-
-                @pl.when(j == steps // 2)
+            for (at_chunk, at_step), (own, passing) in events.items():
+                if at_chunk != i:
+                    continue
+
+                @pl.when(j == at_step)
                 def _():
-                    for n in range((i - 1) * per, min(i * per, items)):
+                    for n in own:
                         own_ready(n)
                         chain.send_own(n)
-
-            hidden = matmul(low[...], w[0, :, block(j)]) + hid_ref[:, block(j)]
+                    for n in passing:
+                        chain.tick(n)
+
+            hidden = matmul(low[top, :], w[0, :, block(j)]) + hid_ref[:, block(j)]
             act_now, slope_now = gelu_and_slope(hidden)
             act_now = act_now.astype(bf16)
             act[rows, block(j)] = act_now
             slope[rows, block(j)] = slope_now.astype(bf16)
-            down[...] += matmul_nt(act_now, w[1, :, block(j)])
-
-        second = down[...]
+            down[top, :] += matmul_nt(act_now, w[1, :, block(j)])
+
+        second = down[top, :]
         total[rows, :] = second
         unit, _scale = norm_parts(second)
         ready[rows, :] = (unit * vec_ref[2:3, :] + vec_ref[3:4, :]).astype(bf16)
-        for n in range(i * chunk // ITEM, (i + 1) * chunk // ITEM):
+        for n in range(start_row // ITEM, (start_row + size) // ITEM):
             if_home(lambda: keep_home(n).start(), lambda: send_home(n).start())
-        if i == chunks - 1:
-            chain.tick(0)
-            chain.tick(1)
-            chain.tick(2)
-
-    if_home(lambda: keep_cot().wait(), lambda: swap_cot().wait())
+        if i + 1 < chunks:
+            if_home(lambda: keep_cot(i + 1).start(), lambda: swap_cot(i + 1).start())
+        start_row += size
+    chain.tick(3)
+    chain.tick(4)
+
     sums_out[...] = jnp.zeros_like(sums_out)
 
     @pl.loop(0, chunks)
     def _(i):
         rows = pl.ds(pl.multiple_of(i * chunk, chunk), chunk)
+        if_home(lambda: keep_cot(i).wait(), lambda: swap_cot(i).wait())
         unit, scale = norm_parts(total[rows, :])
         grad_out = cot[rows, :].astype(f32)
         grad = norm_back(grad_out, unit, scale, vec_ref[2:3, :])
@@ -1304,8 +1338,7 @@
         first = unit * vec_ref[0:1, :] + vec_ref[1:2, :]
         low_t[:, rows] = first.T.astype(bf16)
 
-    chain.tick(3)
-    chain.tick(4)
+    chain.tick(5)
     part = D // 4
 
     def dw_copy(slot, m, j):
@@ -1313,7 +1346,7 @@
             dw_s.at[slot, m], (dw1, dw2)[m].at[:, block(j)], dw_sem.at[2 * slot + m]
         )
 
-    ticks = {0: [5, 6], 1: [7, 8], 2: [9, 10], 3: [11, 12]}
+    ticks = {0: [6, 7], 1: [8, 9], 2: [10, 11]}
 
     @pl.loop(0, steps)
     def _(j):
@@ -1377,8 +1410,6 @@
 
     local.append(pltpu.make_async_copy(dw_s.at[0, 0], dwo, own_sem.at[2]))
     local[-1].start()
-    for j in range(13, items * last):
-        chain.tick(j)
     for i in range(items, all_items):
         own_ready(i)
     for i in range(all_items):
@@ -1432,8 +1463,8 @@
             pltpu.VMEM((256, D), f32),
             pltpu.VMEM((n_tensor, items * ITEM, D), bf16),
             dma((2 * steps + 1,)),
-            dma((1,)),
-            dma((1,)),
+            dma((rows // 256,)),
+            dma((rows // 256,)),
             dma((all_items,)),
             dma((all_items,)),
             dma((items * n_tensor,)),
@@ -1981,7 +2012,7 @@
 )
 
 
-def last_kernel(tokens_ref, out_a, out_b, *refs):
+def last_kernel(tokens_ref, out_b, _output_a, *refs):
     attn_g, attn_w, attn_m, attn_v, ffn_g, ffn_w, ffn_m, ffn_v = refs[:8]
     plain = [refs[8 + 4 * n : 12 + 4 * n] for n in range(3)]
     tokens_out, output = refs[20:22]
@@ -1989,7 +2020,6 @@
     ffn_moment, ffn_square, ffn_new, ffn_copy = refs[27:31]
     plain_out = [refs[31 + 3 * n : 34 + 3 * n] for n in range(3)]
     step = pl.program_id(0)
-    rows_a = out_a.shape[1]
 
     @pl.when(step == 0)
     def _():
@@ -2014,16 +2044,10 @@
 
     tokens_out[...] = tokens_ref[...].astype(f32)
 
-    @pl.when(step % 2 == 0)
-    def _():
-        output[:, :rows_a] = out_a[...]
-
-    @pl.when(step % 2 == 1)
-    def _():
-        output[:, rows_a:] = out_b[...]
-
-
-def last(tokens_low, out_a, out_b, attn, ffn, plain):
+    output[...] = out_b[...]
+
+
+def last(tokens_low, output, out_b, attn, ffn, plain):
     count, rows, _ = tokens_low.shape
     tile = lambda size, index: pl.BlockSpec((1, size, D), index)
     whole = lambda shape: pl.BlockSpec(
@@ -2045,7 +2069,9 @@
         shapes += [(group[0].shape, f32)] * 3
     inputs = list(attn) + list(ffn) + [array for group in plain for array in group]
     by_half = lambda i: (i // 2, i % 2, 0)
-    by_one = lambda i: (i // 2, 0, 0)
+    by_one = lambda i: (i // 2, i % 2, 0)
+    second = lambda i: (i // 2, 2 + i % 2, 0)
+    quarter = rows // 4
     return pl.pallas_call(
         last_kernel,
         out_shape=[
@@ -2056,15 +2082,16 @@
         grid=(count * 2,),
         in_specs=[
             tile(rows // 2, by_half),
-            tile(out_a.shape[1], by_one),
-            tile(out_b.shape[1], by_one),
+            tile(quarter, by_one),
+            pl.BlockSpec(memory_space=pl.ANY),
         ]
         + [whole(array.shape) for array in inputs],
-        out_specs=[tile(rows // 2, by_half), tile(rows, by_one)]
+        out_specs=[tile(rows // 2, by_half), tile(quarter, second)]
         + [whole(shape) for shape, _ in shapes],
+        input_output_aliases={2: 1},
         compiler_params=pltpu.CompilerParams(vmem_limit_bytes=VMEM_LIMIT),
         name="last",
-    )(tokens_low, out_a, out_b, *inputs)
+    )(tokens_low, out_b, output, *inputs)
 
 
 def make_body(mesh):
@@ -2175,17 +2202,19 @@
                 flat, mixed_low, cot.reshape(-1, D), attn_full, ffn_full, hid_all, vec_par
             )
             output = spread(result.reshape(x.shape))
+            out_a, out_b = output[:, : piece_len // 2], output[:, piece_len // 2 :]
             dw1, dw2, dwo, grad_first_in, grad_mixed, hid_sum, first_sums = feed_back(
                 grad_second, h1, mixed_low, attn_full, ffn_full, act, slope, vec_par
             )
 
         grad_mixed = grad_mixed.reshape(x.shape)
-        grad_query, dk_parts, dv_parts = attend_back(
+        grad_query, output, dk_parts, dv_parts = attend_back(
             tables,
             queries,
             grad_mixed,
             mixed.reshape(x.shape),
             lse.reshape(nseq, nb, 8, ROWS),
+            out_a,
             keys,
             values,
             pieces,
@@ -2251,11 +2280,10 @@
             hid_grad = lax.dynamic_slice_in_dim(
                 small[8 * D : 8 * D + FF], t_index * own_ff, own_ff, 0
             )
-            out_a, out_b = output[:, : piece_len // 2], output[:, piece_len // 2 :]
 
         grad_tokens, output, *updated = last(
             grad_tokens,
-            out_a,
+            output,
             out_b,
             (attn_grad, attn_w, attn_m, attn_v),
             (ffn_grad, ffn_w, ffn_m, ffn_v),

time: 419 us -> 411 us (0.981)
  Pallas kernels: 390 us -> 382 us
    pallas_call x1, Pallas kernels: 84.7 us -> 80.1 us  [middle(): pl.pallas_call(partial(middle_kernel, n_tensor), out_shape=[jax.ShapeDtyp...]
  transfers between devices with their start and end apart: 2 -> 2, of which waited for: 0 -> 0; matrix products, arithmetic and copies ran while one was open for 1% -> 1% of each run, Pallas kernels for 46% -> 47%
where the time goes in v3:
time: 411 us; the launch traced here: 403 us
  Pallas kernels  382 us (93%)
  between operations  14.4 us (4%)
    pallas_call x1, Pallas kernels, finish_all(): pl.pallas_call(partial(finish_kernel, n_tensor), out_shape=[jax.ShapeDtyp...  132 us
    pallas_call x1, Pallas kernels, start(): pl.pallas_call(partial(start_kernel, n_tensor), out_shape=[jax.ShapeDtype...  98.4 us
    pallas_call x1, Pallas kernels, middle(): pl.pallas_call(partial(middle_kernel, n_tensor), out_shape=[jax.ShapeDtyp...  80.1 us
    pallas_call x1, Pallas kernels, attend_back(): pl.pallas_call(partial(backward_kernel, len(pieces)), out_shape=[jax.Shap...  56.8 us
    pallas_call x1, Pallas kernels, last(): pl.pallas_call(last_kernel, out_shape=[jax.ShapeDtypeStruct(tokens_low.sh...  14.2 us
  transfers between devices with their start and end apart: 2, of which 0 were waited for; matrix products, arithmetic and copies ran while one was open for 1% of the time, Pallas kernels for 47%

profile of v3, /device:TPU:0, one launch (start us, length us, event | category | flops | bytes accessed | tf_op | source)
XLA Modules:
  0.0 403.4 jit_solution(17069024081177328616)
XLA Ops:
  7.2 0.0 copy-start
  7.2 0.0 all-gather.3.cloned.1.call-start
  7.3 0.7 constant_dynamic-slice_fusion.1
  8.0 0.0 copy-done
  8.0 0.1 copy.41
  8.1 0.1 reshape.81
  8.2 0.7 collective-permute-start
  8.9 1.3 reshape.84.refs_3_
  10.1 0.0 collective-permute-done
  10.2 0.1 convert_element_type.15
  10.2 0.1 pad_maximum_fusion
  10.3 0.1 reshape.82
  10.5 0.6 reshape.83.refs_5_.rand
  11.1 0.7 fusion.2.refs_4_
  11.8 98.4 %start.1 = (bf16[4,768,768]{2,1,0:T(8,128)(2,1)}, bf16[2,768,3072]{2,1,0:T(8,128)(2,1)}, f32[1,3072]{1,0:T(1,128)}, bf16[1024,768]{1,0:T(8,128)(2,1)}, bf16[1024...) custom-call(f32[4,96,192]{2,1,0:T(8,128)} %refs_1_.3, ...), custom_call_target="tpu_custom_call" | custom-call | flops 3623878656 | bytes 104857600 | tf_op jit(solution)/shard_map/start/pallas_call | solution.py:1123
  110.2 80.1 %middle.1 = (bf16[4,512,768]{2,1,0:T(8,128)(2,1)}, bf16[512,768]{1,0:T(8,128)(2,1)}, bf16[768,3072]{1,0:T(8,128)(2,1)}, bf16[768,3072]{1,0:T(8,128)(2,1)}, bf16[...) custom-call(bf16[1024,768]{1,0:T(8,128)(2,1)} %get-tuple-element.71., ...), custom_call_target="tpu_custom_call" | custom-call | flops 32614907904 | bytes 62914560 | tf_op jit(solution)/shard_map/middle/pallas_call | solution.py:1433
  190.3 0.0 all-gather.3.cloned.1.call-update
  190.3 0.6 pad_add_fusion.1.meta
  190.9 0.7 fusion.tab_ref
  191.6 56.8 %attend_back.1 = (bf16[1,1024,768]{2,1,0:T(8,128)(2,1)}, bf16[4,1024,768]{2,1,0:T(8,128)(2,1)}, bf16[1,1024,768]{2,1,0:T(8,128)(2,1)}, bf16[1,1024,768]{2,1,0:T(...) custom-call(s32[48]{0:T(128)} %reshape.83.refs_5_.rand, s32[2]{0:T(128)} %pad_add_fusion.1.meta, ...), custom_call_target="tpu_custom_call" | custom-call | flops 16106127360 | bytes 17301504 | tf_op jit(solution)/shard_map/attend_back/pallas_call | solution.py:379
  248.4 132.4 %finish.1 = (f32[4,96,192]{2,1,0:T(8,128)}, f32[2,96,768]{2,1,0:T(8,128)}, f32[6,768]{1,0:T(8,128)}, f32[2,192]{1,0:T(2,128)}, f32[1,768]{1,0:T(1,128)}, /*index=5*/bf16[4,1024,768]{2,1,0:T(8,128)(2,1)}) custom-call(bf16[1024,768]{1,0:T(8,128)(2,1)} %bitcast.17, bf16[1024,768]{1,0:T(8,128)(2,1)} %bitcast.18, bf16[1024,768]{1,0:T(8,128)(2,1)} %bitcast.19, ...), custom_call_target="tpu_custom_call" | custom-call | flops 7247757312 | bytes 419430400 | tf_op jit(solution)/shard_map/finish/pallas_call | solution.py:1940
  380.8 1.3 reduce.2.refs_12_
  382.1 0.0 all-gather.3.cloned.1.call-done
  382.1 0.0 copy-start.1
  382.1 14.2 %last.1 = (f32[4,1024,768]{2,1,0:T(8,128)}, bf16[4,1024,768]{2,1,0:T(8,128)(2,1)}, f32[3,96,192]{2,1,0:T(8,128)}, f32[3,96,192]{2,1,0:T(8,128)}, f32[2,96,192]{2...) custom-call(bf16[4,1024,768]{2,1,0:T(8,128)(2,1)} %get-tuple-element, ...), custom_call_target="tpu_custom_call", output_to_operand_aliasing={{1}: (2, {})} | custom-call | tf_op jit(solution)/shard_map/last/pallas_call | solution.py:2075
  396.3 0.0 copy-done.1
  (5 shorter events, 0.1 us)
Async XLA Ops:
  7.2 0.8 copy-start
  7.2 374.9 %all-gather.3.cloned.1.call-start = ((), (), s32[]{:S(2)}) async-start(), calls=%async_computation | async-start | bytes 3932160 | tf_op jit(solution)/shard_map/all_gather | solution.py:2199
  8.2 2.0 collective-permute-start
  382.1 14.2 %copy-start.1 = (s32[4,2048]{1,0:T(4,128)S(1)}, s32[4,2048]{1,0:T(4,128)}, u32[]{:S(2)}) copy-start(s32[4,2048]{1,0:T(4,128)} %param.21) | copy-start | bytes 98308
Sparse Core Ops, SparseCore 0:
  190.4 67.2 all-gather.2

commit v4 on v3

--- a/solution.py
+++ b/solution.py
@@ -862,20 +862,27 @@
         for k in range(n_tensor - 1):
             put(z_hop(path, k, t))
 
-    def keep_rows(src, dst, n):
-        return pltpu.make_async_copy(src.at[t], dst, x_recv.at[n])
-
-    def swap_rows(src, dst, n):
-        return remote(src.at[t], dst, x_send.at[n], x_recv.at[n], across)
-
-    @pl.when(core == c)
-    def _():
-        keep_rows(tokens, xs, 0).start()
-
-    @pl.when(core != c)
-    def _():
-        swap_rows(tokens, xs, 0).start()
-
+    quarter = n_rows // 4
+
+    def keep_rows(n):
+        at = pl.ds(n * quarter, quarter)
+        return pltpu.make_async_copy(tokens.at[t, at], xs.at[at], x_recv.at[n])
+
+    def swap_rows(n):
+        at = pl.ds(n * quarter, quarter)
+        return remote(tokens.at[t, at], xs.at[at], x_send.at[n], x_recv.at[n], across)
+
+    def start_rows(n):
+        @pl.when(core == c)
+        def _():
+            keep_rows(n).start()
+
+        @pl.when(core != c)
+        def _():
+            swap_rows(n).start()
+
+    start_rows(0)
+    start_rows(1)
     low_z[t] = low[...]
     bias_z[t] = bias[...]
 
@@ -1003,19 +1010,18 @@
 
     lay_out(0)
     attn.step(0, 0)
+    start_rows(2)
+    ffn_along_z(0)
     lay_out(1)
     attn.step(1, 0)
-    ffn_along_z(0)
+    start_rows(3)
     ffn_along_z(1)
     for k, where in enumerate(along_z):
         put(remote(bias, bias_z.at[t], b_send.at[k], b_recv.at[t], where))
     attn.step(0, 1)
     attn.step(1, 1)
-    ffn_ready(0)
     attn.step(0, 2)
-    attn.step(1, 2)
     attn.step(0, 3)
-    attn.step(1, 3)
     for k, where in enumerate(along_z):
         u = where[2]
         remote(bias, bias_z.at[u], b_send.at[k], b_recv.at[u], where).wait_recv()
@@ -1024,13 +1030,15 @@
         bias_qv[0:2, cols] = bias_z[n, 0:2, 0:own_cols]
         hid_out[:, n * own_ff : (n + 1) * own_ff] = bias_z[n, 2:3, 0:own_ff]
 
-    @pl.when(core == c)
-    def _():
-        keep_rows(tokens, xs, 0).wait()
-
-    @pl.when(core != c)
-    def _():
-        swap_rows(tokens, xs, 0).wait()
+    for n in range(4):
+
+        @pl.when(core == c)
+        def _():
+            keep_rows(n).wait()
+
+        @pl.when(core != c)
+        def _():
+            swap_rows(n).wait()
 
     chunk = 256
     chunks = n_rows // chunk
@@ -1050,6 +1058,9 @@
         at = pl.ds(i * chunk, chunk)
         q = matmul(xs[at, :], full[0]) + bias_qv[0:1, :]
         qs[at, :] = (q.astype(bf16).astype(f32) * 0.125).astype(bf16)
+    attn.step(1, 2)
+    attn.step(1, 3)
+    ffn_ready(0)
     attn.take_shared(1)
     for i in range(chunks):
         at = pl.ds(i * chunk, chunk)
@@ -1069,7 +1080,7 @@
 
     nb = n_rows // BLOCK
     first = core * nb
-    stops = {1: [(1, 1), (0, 2)], 3: [(1, 2)], 10: [(0, 3), (1, 3)]}
+    stops = {1: [(1, 1), (0, 2)], 3: [(1, 2)]}
 
     @pl.loop(0, nb)
     def _(blk):
@@ -1101,6 +1112,8 @@
     write(ms, mixed_out, 7)
     for path, number in [move for moves in stops.values() for move in moves]:
         ffn.again(path, number)
+    ffn.step(0, 3)
+    ffn.step(1, 3)
     for path in range(2):
         ffn.take_shared(path)
         write(ffn_full.at[path], ffn_out.at[path], 8 + path)
@@ -1156,8 +1169,8 @@
             dma((n_tensor,)),
             dma((2 * n_tensor,)),
             dma((2 * n_tensor,)),
-            dma((2,)),
-            dma((2,)),
+            dma((4,)),
+            dma((4,)),
             dma((6,)),
             dma((6,)),
             dma((8,)),
@@ -1260,12 +1273,12 @@
         if_home(lambda: keep_home(i).wait(), lambda: send_home(i).wait_recv())
 
     events = {
-        (1, 1): ([0], []),
-        (2, 1): ([1], []),
-        (2, 2): ([2], []),
-        (2, 3): ([], [0]),
-        (3, 1): ([3], [1]),
-        (3, 3): ([], [2]),
+        (1, 2): ([0], []),
+        (2, 2): ([1], []),
+        (2, 3): ([2], [0]),
+        (3, 2): ([], [1]),
+        (3, 3): ([3], []),
+        (4, 0): ([], [2]),
     }
     sizes = [ITEM] + [chunk] * (chunks - 1) + [chunk - ITEM]
     start_row = 0
@@ -1315,7 +1328,6 @@
         if i + 1 < chunks:
             if_home(lambda: keep_cot(i + 1).start(), lambda: swap_cot(i + 1).start())
         start_row += size
-    chain.tick(3)
     chain.tick(4)
 
     sums_out[...] = jnp.zeros_like(sums_out)
@@ -1338,7 +1350,6 @@
         first = unit * vec_ref[0:1, :] + vec_ref[1:2, :]
         low_t[:, rows] = first.T.astype(bf16)
 
-    chain.tick(5)
     part = D // 4
 
     def dw_copy(slot, m, j):
@@ -1346,17 +1357,27 @@
             dw_s.at[slot, m], (dw1, dw2)[m].at[:, block(j)], dw_sem.at[2 * slot + m]
         )
 
-    ticks = {0: [6, 7], 1: [8, 9], 2: [10, 11]}
+    ticks = {(0, 1): 5, (1, 0): 3, (1, 1): 6, (2, 0): 8, (2, 1): 9, (3, 0): 7, (3, 1): 10}
+
+    def pass_on(j, when):
+        for (at, place), n in ticks.items():
+            if place == when:
+
+                @pl.when(j == at)
+                def _():
+                    chain.tick(n)
 
     @pl.loop(0, steps)
     def _(j):
         slot = lax.rem(j, 2)
+        pass_on(j, 0)
         for i in range(chunks):
             rows = slice(i * chunk, (i + 1) * chunk)
             grad_act = matmul(gs_low[rows, :], w[1, :, block(j)]).astype(bf16).astype(f32)
             grad_pre = (grad_act * slope[rows, block(j)].astype(f32)).astype(bf16)
             pre[rows, :] = grad_pre
             total[rows, :] += matmul_nt(grad_pre, w[0, :, block(j)])
+        pass_on(j, 1)
         hid_out[:, block(j)] = column_total(pre[...])
 
         @pl.when(j >= 2)
@@ -1370,12 +1391,6 @@
             dw_s[slot, 1, out, :] = matmul(turned[out, :], act[:, block(j)]).astype(bf16)
         for m in range(2):
             dw_copy(slot, m, j).start()
-        for at, numbers in ticks.items():
-
-            @pl.when(j == at)
-            def _():
-                for n in numbers:
-                    chain.tick(n)
 
     gm_s = gs_low
 
@@ -1410,6 +1425,7 @@
 
     local.append(pltpu.make_async_copy(dw_s.at[0, 0], dwo, own_sem.at[2]))
     local[-1].start()
+    chain.tick(11)
     for i in range(items, all_items):
         own_ready(i)
     for i in range(all_items):

time: 411 us -> 412 us (level)
    pallas_call x1, Pallas kernels: 98.4 us -> 108 us  [start(): pl.pallas_call(partial(start_kernel, n_tensor), out_shape=[jax.ShapeDtype...]
    pallas_call x1, Pallas kernels: 80.1 us -> 75.7 us  [middle(): pl.pallas_call(partial(middle_kernel, n_tensor), out_shape=[jax.ShapeDtyp...]
  transfers between devices with their start and end apart: 2 -> 2, of which waited for: 0 -> 0; matrix products, arithmetic and copies ran while one was open for 1% -> 1% of each run, Pallas kernels for 47% -> 46%
where the time goes in v4:
time: 412 us; the launch traced here: 406 us
  Pallas kernels  385 us (93%)
  between operations  14.4 us (3%)
    pallas_call x1, Pallas kernels, finish_all(): pl.pallas_call(partial(finish_kernel, n_tensor), out_shape=[jax.ShapeDtyp...  130 us
    pallas_call x1, Pallas kernels, start(): pl.pallas_call(partial(start_kernel, n_tensor), out_shape=[jax.ShapeDtype...  108 us
    pallas_call x1, Pallas kernels, middle(): pl.pallas_call(partial(middle_kernel, n_tensor), out_shape=[jax.ShapeDtyp...  75.7 us
    pallas_call x1, Pallas kernels, attend_back(): pl.pallas_call(partial(backward_kernel, len(pieces)), out_shape=[jax.Shap...  56.4 us
    pallas_call x1, Pallas kernels, last(): pl.pallas_call(last_kernel, out_shape=[jax.ShapeDtypeStruct(tokens_low.sh...  14.2 us
  transfers between devices with their start and end apart: 2, of which 0 were waited for; matrix products, arithmetic and copies ran while one was open for 1% of the time, Pallas kernels for 46%

profile of v4, /device:TPU:0, one launch (start us, length us, event | category | flops | bytes accessed | tf_op | source)
XLA Modules:
  0.0 406.1 jit_solution(15118569042196165823)
XLA Ops:
  7.2 0.0 copy-start
  7.2 0.0 all-gather.3.cloned.1.call-start
  7.3 0.7 constant_dynamic-slice_fusion.1
  8.0 0.0 copy-done
  8.0 0.1 copy.41
  8.1 0.1 reshape.81
  8.2 0.7 collective-permute-start
  8.9 1.3 reshape.84.refs_3_
  10.1 0.0 collective-permute-done
  10.2 0.1 convert_element_type.15
  10.2 0.1 pad_maximum_fusion
  10.3 0.1 reshape.82
  10.5 0.6 reshape.83.refs_5_.rand
  11.1 0.7 fusion.2.refs_4_
  11.8 108.0 %start.1 = (bf16[4,768,768]{2,1,0:T(8,128)(2,1)}, bf16[2,768,3072]{2,1,0:T(8,128)(2,1)}, f32[1,3072]{1,0:T(1,128)}, bf16[1024,768]{1,0:T(8,128)(2,1)}, bf16[1024...) custom-call(f32[4,96,192]{2,1,0:T(8,128)} %refs_1_.3, ...), custom_call_target="tpu_custom_call" | custom-call | flops 3623878656 | bytes 104857600 | tf_op jit(solution)/shard_map/start/pallas_call | solution.py:1136
  119.8 75.7 %middle.1 = (bf16[4,512,768]{2,1,0:T(8,128)(2,1)}, bf16[512,768]{1,0:T(8,128)(2,1)}, bf16[768,3072]{1,0:T(8,128)(2,1)}, bf16[768,3072]{1,0:T(8,128)(2,1)}, bf16[...) custom-call(bf16[1024,768]{1,0:T(8,128)(2,1)} %get-tuple-element.71., ...), custom_call_target="tpu_custom_call" | custom-call | flops 32614907904 | bytes 62914560 | tf_op jit(solution)/shard_map/middle/pallas_call | solution.py:1449
  195.5 0.0 all-gather.3.cloned.1.call-update
  195.5 0.6 pad_add_fusion.1.meta
  196.1 0.7 fusion.tab_ref
  196.8 56.4 %attend_back.1 = (bf16[1,1024,768]{2,1,0:T(8,128)(2,1)}, bf16[4,1024,768]{2,1,0:T(8,128)(2,1)}, bf16[1,1024,768]{2,1,0:T(8,128)(2,1)}, bf16[1,1024,768]{2,1,0:T(...) custom-call(s32[48]{0:T(128)} %reshape.83.refs_5_.rand, s32[2]{0:T(128)} %pad_add_fusion.1.meta, ...), custom_call_target="tpu_custom_call" | custom-call | flops 16106127360 | bytes 17301504 | tf_op jit(solution)/shard_map/attend_back/pallas_call | solution.py:379
  253.2 130.3 %finish.1 = (f32[4,96,192]{2,1,0:T(8,128)}, f32[2,96,768]{2,1,0:T(8,128)}, f32[6,768]{1,0:T(8,128)}, f32[2,192]{1,0:T(2,128)}, f32[1,768]{1,0:T(1,128)}, /*index=5*/bf16[4,1024,768]{2,1,0:T(8,128)(2,1)}) custom-call(bf16[1024,768]{1,0:T(8,128)(2,1)} %bitcast.17, bf16[1024,768]{1,0:T(8,128)(2,1)} %bitcast.18, bf16[1024,768]{1,0:T(8,128)(2,1)} %bitcast.19, ...), custom_call_target="tpu_custom_call" | custom-call | flops 7247757312 | bytes 419430400 | tf_op jit(solution)/shard_map/finish/pallas_call | solution.py:1956
  383.5 1.3 reduce.2.refs_12_
  384.8 0.0 all-gather.3.cloned.1.call-done
  384.8 0.0 copy-start.1
  384.8 14.2 %last.1 = (f32[4,1024,768]{2,1,0:T(8,128)}, bf16[4,1024,768]{2,1,0:T(8,128)(2,1)}, f32[3,96,192]{2,1,0:T(8,128)}, f32[3,96,192]{2,1,0:T(8,128)}, f32[2,96,192]{2...) custom-call(bf16[4,1024,768]{2,1,0:T(8,128)(2,1)} %get-tuple-element, ...), custom_call_target="tpu_custom_call", output_to_operand_aliasing={{1}: (2, {})} | custom-call | tf_op jit(solution)/shard_map/last/pallas_call | solution.py:2091
  399.0 0.0 copy-done.1
  (5 shorter events, 0.1 us)
Async XLA Ops:
  7.2 0.8 copy-start
  7.2 377.6 %all-gather.3.cloned.1.call-start = ((), (), s32[]{:S(2)}) async-start(), calls=%async_computation | async-start | bytes 3932160 | tf_op jit(solution)/shard_map/all_gather | solution.py:2215
  8.2 2.0 collective-permute-start
  384.8 14.2 %copy-start.1 = (s32[4,2048]{1,0:T(4,128)S(1)}, s32[4,2048]{1,0:T(4,128)}, u32[]{:S(2)}) copy-start(s32[4,2048]{1,0:T(4,128)} %param.21) | copy-start | bytes 98308
Sparse Core Ops, SparseCore 0:
  195.6 62.9 all-gather.2

commit v5 on v3

--- a/solution.py
+++ b/solution.py
@@ -808,7 +808,7 @@
 def start_kernel(n_tensor, *refs):
     attn_ref, ffn_ref, qv_ref, hid_ref, tab_ref, rand, tokens = refs[:7]
     attn_out, ffn_out, hid_out, x_out, q_out, k_out, v_out, mixed_out, lse_out = refs[7:16]
-    low, low_z, bias, bias_z, bias_qv, ffn_low, full, xs, qs, ms, k_buf, v_buf, s_buf, ffn_full = refs[16:30]
+    low, low_z, bias, bias_z, bias_qv, ffn_low, full, xs, qs, ms, k_buf, v_buf, s_buf = refs[16:29]
     (
         z_send,
         z_recv,
@@ -829,7 +829,7 @@
         kv_send,
         kv_recv,
         own_sem,
-    ) = refs[30:]
+    ) = refs[29:]
     s, c, t, x, core, sibling, over_x, over_y, across, along_z = places(n_tensor)
     own_cols, own_ff = D // n_tensor, FF // n_tensor
     n_rows = xs.shape[0]
@@ -911,7 +911,7 @@
         return full.at[pl.ds(2 * path, 2), at, :]
 
     def ffn_block(path, at):
-        return ffn_full.at[path, at, :]
+        return ffn_out.at[path, at, :]
 
     class Gather:
         def __init__(self, block, ways, gs, gr, ps, pr):
@@ -971,7 +971,7 @@
     ffn = Gather(ffn_block, (0, 1), fg_send, fg_recv, fp_send, fp_recv)
 
     def ffn_cols(path, u):
-        return ffn_full.at[path, here, pl.ds(pl.multiple_of(u * own_ff, own_ff), own_ff)]
+        return ffn_out.at[path, here, pl.ds(pl.multiple_of(u * own_ff, own_ff), own_ff)]
 
     def ffn_hop(path, k, u):
         n = path * n_tensor
@@ -1046,6 +1046,7 @@
         k = matmul(xs[at, :], full[1]).astype(bf16)
         k_buf[pl.ds(i * per, per)] = k.reshape(per, BLOCK, D)
         put(kv_hop(k_buf, i, i))
+    ffn_ready(1)
     for i in range(chunks):
         at = pl.ds(i * chunk, chunk)
         q = matmul(xs[at, :], full[0]) + bias_qv[0:1, :]
@@ -1056,6 +1057,7 @@
         v = (matmul(xs[at, :], full[2]) + bias_qv[1:2, :]).astype(bf16)
         v_buf[pl.ds(i * per, per)] = v.reshape(per, BLOCK, D)
         put(kv_hop(v_buf, i, chunks + i))
+    ffn.step(0, 1)
     write(xs, x_out, 0)
     write(qs, q_out, 1)
     write(full, attn_out, 2)
@@ -1064,12 +1066,10 @@
         kv_hop(v_buf, i, chunks + i).wait_recv()
     write(k_buf, k_out, 3)
     write(v_buf, v_out, 4)
-    ffn_ready(1)
-    ffn.step(0, 1)
 
     nb = n_rows // BLOCK
     first = core * nb
-    stops = {1: [(1, 1), (0, 2)], 3: [(1, 2)], 10: [(0, 3), (1, 3)]}
+    stops = {0: [(1, 1)], 1: [(0, 2), (1, 2)], 9: [(0, 3), (1, 3)]}
 
     @pl.loop(0, nb)
     def _(blk):
@@ -1101,9 +1101,8 @@
     write(ms, mixed_out, 7)
     for path, number in [move for moves in stops.values() for move in moves]:
         ffn.again(path, number)
-    for path in range(2):
-        ffn.take_shared(path)
-        write(ffn_full.at[path], ffn_out.at[path], 8 + path)
+    ffn.take_shared(0)
+    ffn.take_shared(1)
 
     for copy in sent:
         copy.wait_send()
@@ -1149,7 +1148,6 @@
             pltpu.VMEM((2 * rows // BLOCK, BLOCK, D), bf16),
             pltpu.VMEM((2 * rows // BLOCK, BLOCK, D), bf16),
             pltpu.VMEM((2 * rows // KEYS, ROWS, KEYS), f32),
-            pltpu.VMEM((2, D, FF), bf16),
             dma((2 * n_tensor,)),
             dma((2 * n_tensor,)),
             dma((n_tensor,)),
@@ -1168,7 +1166,7 @@
             dma((8,)),
             dma((items,)),
             dma((items,)),
-            dma((10,)),
+            dma((8,)),
         ],
         compiler_params=pltpu.CompilerParams(
             collective_id=2, has_side_effects=True, vmem_limit_bytes=VMEM_LIMIT
@@ -1260,12 +1258,12 @@
         if_home(lambda: keep_home(i).wait(), lambda: send_home(i).wait_recv())
 
     events = {
-        (1, 1): ([0], []),
-        (2, 1): ([1], []),
-        (2, 2): ([2], []),
-        (2, 3): ([], [0]),
-        (3, 1): ([3], [1]),
-        (3, 3): ([], [2]),
+        (1, 2): ([0], []),
+        (2, 2): ([1], []),
+        (2, 3): ([2], [0]),
+        (3, 2): ([], [1]),
+        (3, 3): ([3], []),
+        (4, 0): ([], [2]),
     }
     sizes = [ITEM] + [chunk] * (chunks - 1) + [chunk - ITEM]
     start_row = 0
@@ -1315,7 +1313,6 @@
         if i + 1 < chunks:
             if_home(lambda: keep_cot(i + 1).start(), lambda: swap_cot(i + 1).start())
         start_row += size
-    chain.tick(3)
     chain.tick(4)
 
     sums_out[...] = jnp.zeros_like(sums_out)
@@ -1338,7 +1335,6 @@
         first = unit * vec_ref[0:1, :] + vec_ref[1:2, :]
         low_t[:, rows] = first.T.astype(bf16)
 
-    chain.tick(5)
     part = D // 4
 
     def dw_copy(slot, m, j):
@@ -1346,17 +1342,27 @@
             dw_s.at[slot, m], (dw1, dw2)[m].at[:, block(j)], dw_sem.at[2 * slot + m]
         )
 
-    ticks = {0: [6, 7], 1: [8, 9], 2: [10, 11]}
+    ticks = {(0, 1): 5, (1, 0): 3, (1, 1): 6, (2, 0): 8, (2, 1): 9, (3, 0): 7, (3, 1): 10}
+
+    def pass_on(j, when):
+        for (at, place), n in ticks.items():
+            if place == when:
+
+                @pl.when(j == at)
+                def _():
+                    chain.tick(n)
 
     @pl.loop(0, steps)
     def _(j):
         slot = lax.rem(j, 2)
+        pass_on(j, 0)
         for i in range(chunks):
             rows = slice(i * chunk, (i + 1) * chunk)
             grad_act = matmul(gs_low[rows, :], w[1, :, block(j)]).astype(bf16).astype(f32)
             grad_pre = (grad_act * slope[rows, block(j)].astype(f32)).astype(bf16)
             pre[rows, :] = grad_pre
             total[rows, :] += matmul_nt(grad_pre, w[0, :, block(j)])
+        pass_on(j, 1)
         hid_out[:, block(j)] = column_total(pre[...])
 
         @pl.when(j >= 2)
@@ -1370,12 +1376,6 @@
             dw_s[slot, 1, out, :] = matmul(turned[out, :], act[:, block(j)]).astype(bf16)
         for m in range(2):
             dw_copy(slot, m, j).start()
-        for at, numbers in ticks.items():
-
-            @pl.when(j == at)
-            def _():
-                for n in numbers:
-                    chain.tick(n)
 
     gm_s = gs_low
 
@@ -1410,6 +1410,7 @@
 
     local.append(pltpu.make_async_copy(dw_s.at[0, 0], dwo, own_sem.at[2]))
     local[-1].start()
+    chain.tick(11)
     for i in range(items, all_items):
         own_ready(i)
     for i in range(all_items):

time: 411 us -> 403 us (0.981)
  Pallas kernels: 382 us -> 377 us
    pallas_call x1, Pallas kernels: 98.4 us -> 94.2 us  [start(): pl.pallas_call(partial(start_kernel, n_tensor), out_shape=[jax.ShapeDtype...]
where the time goes in v5:
time: 403 us; the launch traced here: 398 us
  Pallas kernels  377 us (94%)
  between operations  14.4 us (4%)
    pallas_call x1, Pallas kernels, finish_all(): pl.pallas_call(partial(finish_kernel, n_tensor), out_shape=[jax.ShapeDtyp...  130 us
    pallas_call x1, Pallas kernels, start(): pl.pallas_call(partial(start_kernel, n_tensor), out_shape=[jax.ShapeDtype...  94.2 us
    pallas_call x1, Pallas kernels, middle(): pl.pallas_call(partial(middle_kernel, n_tensor), out_shape=[jax.ShapeDtyp...  82.2 us
    pallas_call x1, Pallas kernels, attend_back(): pl.pallas_call(partial(backward_kernel, len(pieces)), out_shape=[jax.Shap...  56.4 us
    pallas_call x1, Pallas kernels, last(): pl.pallas_call(last_kernel, out_shape=[jax.ShapeDtypeStruct(tokens_low.sh...  14.2 us
  transfers between devices with their start and end apart: 2, of which 0 were waited for; matrix products, arithmetic and copies ran while one was open for 1% of the time, Pallas kernels for 47%

profile of v5, /device:TPU:0, one launch (start us, length us, event | category | flops | bytes accessed | tf_op | source)
XLA Modules:
  0.0 398.3 jit_solution(630256179057632298)
XLA Ops:
  7.2 0.0 copy-start
  7.2 0.0 all-gather.3.cloned.1.call-start
  7.3 0.7 constant_dynamic-slice_fusion.1
  8.0 0.0 copy-done
  8.0 0.1 copy.41
  8.1 0.1 reshape.81
  8.2 0.7 collective-permute-start
  8.9 1.3 reshape.84.refs_3_
  10.1 0.0 collective-permute-done
  10.2 0.1 convert_element_type.15
  10.2 0.1 pad_maximum_fusion
  10.3 0.1 reshape.82
  10.5 0.6 reshape.83.refs_5_.rand
  11.1 0.7 fusion.2.refs_4_
  11.8 94.2 %start.1 = (bf16[4,768,768]{2,1,0:T(8,128)(2,1)}, bf16[2,768,3072]{2,1,0:T(8,128)(2,1)}, f32[1,3072]{1,0:T(1,128)}, bf16[1024,768]{1,0:T(8,128)(2,1)}, bf16[1024...) custom-call(f32[4,96,192]{2,1,0:T(8,128)} %refs_1_.3, ...), custom_call_target="tpu_custom_call" | custom-call | flops 3623878656 | bytes 104857600 | tf_op jit(solution)/shard_map/start/pallas_call | solution.py:1122
  105.9 82.2 %middle.1 = (bf16[4,512,768]{2,1,0:T(8,128)(2,1)}, bf16[512,768]{1,0:T(8,128)(2,1)}, bf16[768,3072]{1,0:T(8,128)(2,1)}, bf16[768,3072]{1,0:T(8,128)(2,1)}, bf16[...) custom-call(bf16[1024,768]{1,0:T(8,128)(2,1)} %get-tuple-element.71., ...), custom_call_target="tpu_custom_call" | custom-call | flops 32614907904 | bytes 62914560 | tf_op jit(solution)/shard_map/middle/pallas_call | solution.py:1434
  188.1 0.0 all-gather.3.cloned.1.call-update
  188.2 0.6 pad_add_fusion.1.meta
  188.8 0.7 fusion.tab_ref
  189.5 56.4 %attend_back.1 = (bf16[1,1024,768]{2,1,0:T(8,128)(2,1)}, bf16[4,1024,768]{2,1,0:T(8,128)(2,1)}, bf16[1,1024,768]{2,1,0:T(8,128)(2,1)}, bf16[1,1024,768]{2,1,0:T(...) custom-call(s32[48]{0:T(128)} %reshape.83.refs_5_.rand, s32[2]{0:T(128)} %pad_add_fusion.1.meta, ...), custom_call_target="tpu_custom_call" | custom-call | flops 16106127360 | bytes 17301504 | tf_op jit(solution)/shard_map/attend_back/pallas_call | solution.py:379
  245.9 129.8 %finish.1 = (f32[4,96,192]{2,1,0:T(8,128)}, f32[2,96,768]{2,1,0:T(8,128)}, f32[6,768]{1,0:T(8,128)}, f32[2,192]{1,0:T(2,128)}, f32[1,768]{1,0:T(1,128)}, /*index=5*/bf16[4,1024,768]{2,1,0:T(8,128)(2,1)}) custom-call(bf16[1024,768]{1,0:T(8,128)(2,1)} %bitcast.17, bf16[1024,768]{1,0:T(8,128)(2,1)} %bitcast.18, bf16[1024,768]{1,0:T(8,128)(2,1)} %bitcast.19, ...), custom_call_target="tpu_custom_call" | custom-call | flops 7247757312 | bytes 419430400 | tf_op jit(solution)/shard_map/finish/pallas_call | solution.py:1941
  375.7 1.3 reduce.2.refs_12_
  377.0 0.0 all-gather.3.cloned.1.call-done
  377.0 0.0 copy-start.1
  377.0 14.2 %last.1 = (f32[4,1024,768]{2,1,0:T(8,128)}, bf16[4,1024,768]{2,1,0:T(8,128)(2,1)}, f32[3,96,192]{2,1,0:T(8,128)}, f32[3,96,192]{2,1,0:T(8,128)}, f32[2,96,192]{2...) custom-call(bf16[4,1024,768]{2,1,0:T(8,128)(2,1)} %get-tuple-element, ...), custom_call_target="tpu_custom_call", output_to_operand_aliasing={{1}: (2, {})} | custom-call | tf_op jit(solution)/shard_map/last/pallas_call | solution.py:2076
  391.2 0.0 copy-done.1
  (5 shorter events, 0.1 us)
Async XLA Ops:
  7.2 0.8 copy-start
  7.2 369.8 %all-gather.3.cloned.1.call-start = ((), (), s32[]{:S(2)}) async-start(), calls=%async_computation | async-start | bytes 3932160 | tf_op jit(solution)/shard_map/all_gather | solution.py:2200
  8.2 2.0 collective-permute-start
  377.0 14.2 %copy-start.1 = (s32[4,2048]{1,0:T(4,128)S(1)}, s32[4,2048]{1,0:T(4,128)}, u32[]{:S(2)}) copy-start(s32[4,2048]{1,0:T(4,128)} %param.21) | copy-start | bytes 98308
Sparse Core Ops, SparseCore 0:
  188.3 60.8 all-gather.2

commit v6 on v5

--- a/solution.py
+++ b/solution.py
@@ -803,6 +803,61 @@
             @pl.when(t + hops <= last)
             def _():
                 self.keep(t + hops, last + hops - 1).wait()
+
+
+class Relay:
+    def __init__(self, s, c, t, items, rows, array, out, send, recv, passed, copied):
+        self.s, self.c, self.t, self.items, self.rows = s, c, t, items, rows
+        self.array, self.out, self.send, self.recv = array, out, send, recv
+        self.passed, self.copied = passed, copied
+
+    def copy(self, i, source, send, to):
+        ref = self.array.at[source, pl.ds(i * self.rows, self.rows)]
+        return remote(ref, ref, send, self.recv.at[source * self.items + i], (self.s, self.c, to))
+
+    def keep(self, u):
+        return pltpu.make_async_copy(self.array.at[u], self.out.at[u], self.copied.at[u])
+
+    def own(self, i, act):
+        t = self.t
+        for n, step in enumerate((2, -2, 1, -1)):
+
+            @pl.when((t + step >= 0) & (t + step < 4))
+            def _():
+                act(self.copy(i, t, self.send.at[4 * i + n], t + step))
+
+    def send_own(self, i):
+        self.own(i, lambda copy: copy.start())
+
+    def through(self, i, act):
+        for t, source, to in ((2, 0, 3), (1, 3, 0)):
+
+            @pl.when(self.t == t)
+            def _():
+                act(self.copy(i, source, self.passed.at[i], to))
+
+    def relay(self, i):
+        def act(copy):
+            copy.wait_recv()
+            copy.start()
+
+        self.through(i, act)
+
+    def settle(self):
+        t = self.t
+        for u, relayed_by in ((1, 1), (2, 2), (0, 2), (3, 1)):
+
+            @pl.when((t != u) & (t != relayed_by))
+            def _():
+                for i in range(self.items):
+                    self.copy(i, u, self.send.at[0], lax.rem(t + 1, 4)).wait_recv()
+
+            self.keep(u).start()
+        for i in range(self.items):
+            self.own(i, lambda copy: copy.wait_send())
+            self.through(i, lambda copy: copy.wait_send())
+        for u in range(4):
+            self.keep(u).wait()
 
 
 def start_kernel(n_tensor, *refs):
@@ -1188,10 +1243,9 @@
         c_recv,
         h_send,
         h_recv,
-        up_send,
-        up_recv,
-        dn_send,
-        dn_recv,
+        z_send,
+        z_recv,
+        z_passed,
         dw_sem,
         own_sem,
         copied,
@@ -1202,7 +1256,6 @@
     chunks = n_rows // chunk
     steps = FF // D
     items, all_items = LINE_ITEMS, n_rows // ITEM
-    last = n_tensor - 1
 
     def block(i):
         return pl.ds(pl.multiple_of(i * D, D), D)
@@ -1251,8 +1304,7 @@
 
     if_home(lambda: keep_cot(0).start(), lambda: swap_cot(0).start())
 
-    up, down_line = (up_send, up_recv), (dn_send, dn_recv)
-    chain = Line(s, c, t, last, items, ITEM, held, out_a, up, down_line, copied)
+    chain = Relay(s, c, t, items, ITEM, held, out_a, z_send, z_recv, z_passed, copied)
 
     def own_ready(i):
         if_home(lambda: keep_home(i).wait(), lambda: send_home(i).wait_recv())
@@ -1260,10 +1312,9 @@
     events = {
         (1, 2): ([0], []),
         (2, 2): ([1], []),
-        (2, 3): ([2], [0]),
-        (3, 2): ([], [1]),
+        (2, 3): ([2], []),
+        (3, 2): ([], [0]),
         (3, 3): ([3], []),
-        (4, 0): ([], [2]),
     }
     sizes = [ITEM] + [chunk] * (chunks - 1) + [chunk - ITEM]
     start_row = 0
@@ -1295,7 +1346,7 @@
                         own_ready(n)
                         chain.send_own(n)
                     for n in passing:
-                        chain.tick(n)
+                        chain.relay(n)
 
             hidden = matmul(low[top, :], w[0, :, block(j)]) + hid_ref[:, block(j)]
             act_now, slope_now = gelu_and_slope(hidden)
@@ -1313,7 +1364,6 @@
         if i + 1 < chunks:
             if_home(lambda: keep_cot(i + 1).start(), lambda: swap_cot(i + 1).start())
         start_row += size
-    chain.tick(4)
 
     sums_out[...] = jnp.zeros_like(sums_out)
 
@@ -1342,15 +1392,15 @@
             dw_s.at[slot, m], (dw1, dw2)[m].at[:, block(j)], dw_sem.at[2 * slot + m]
         )
 
-    ticks = {(0, 1): 5, (1, 0): 3, (1, 1): 6, (2, 0): 8, (2, 1): 9, (3, 0): 7, (3, 1): 10}
+    passing_on = {(0, 1): 1, (2, 0): 2, (3, 1): 3}
 
     def pass_on(j, when):
-        for (at, place), n in ticks.items():
+        for (at, place), n in passing_on.items():
             if place == when:
 
                 @pl.when(j == at)
                 def _():
-                    chain.tick(n)
+                    chain.relay(n)
 
     @pl.loop(0, steps)
     def _(j):
@@ -1410,7 +1460,6 @@
 
     local.append(pltpu.make_async_copy(dw_s.at[0, 0], dwo, own_sem.at[2]))
     local[-1].start()
-    chain.tick(11)
     for i in range(items, all_items):
         own_ready(i)
     for i in range(all_items):
@@ -1470,11 +1519,10 @@
             dma((all_items,)),
             dma((items * n_tensor,)),
             dma((items * n_tensor,)),
-            dma((items * n_tensor,)),
-            dma((items * n_tensor,)),
+            dma((items,)),
             dma((4,)),
             dma((3,)),
-            dma((2 * n_tensor - 1,)),
+            dma((n_tensor,)),
         ],
         compiler_params=pltpu.CompilerParams(
             collective_id=3, has_side_effects=True, vmem_limit_bytes=VMEM_LIMIT
@@ -2040,7 +2088,8 @@
             ffn_moment[m], ffn_square[m] = moment, square
             ffn_new[m], ffn_copy[m] = new, new.astype(bf16)
         for (g, w, m, v), outs in zip(plain, plain_out):
-            for ref, value in zip(outs, adam_update(w[...], m[...], v[...], g[...], 0.5, 0.0)):
+            gradient = g[...] if len(g.shape) == len(w.shape) else g[0, :]
+            for ref, value in zip(outs, adam_update(w[...], m[...], v[...], gradient, 0.5, 0.0)):
                 ref[...] = value
 
     tokens_out[...] = tokens_ref[...].astype(f32)
@@ -2067,7 +2116,7 @@
         (f, bf16),
     ]
     for group in plain:
-        shapes += [(group[0].shape, f32)] * 3
+        shapes += [(group[1].shape, f32)] * 3
     inputs = list(attn) + list(ffn) + [array for group in plain for array in group]
     by_half = lambda i: (i // 2, i % 2, 0)
     by_one = lambda i: (i // 2, i % 2, 0)
@@ -2290,7 +2339,7 @@
             (ffn_grad, ffn_w, ffn_m, ffn_v),
             [
                 (qv_grad, qv_bias, qv_m, qv_v),
-                (hid_grad.reshape(own_ff), hid_bias, hid_m, hid_v),
+                (hid_grad.reshape(1, own_ff), hid_bias, hid_m, hid_v),
                 (vec_grad, vec_par, vec_m, vec_v),
             ],
         )

time: 403 us -> 400 us (level)
  transfers between devices with their start and end apart: 2 -> 2, of which waited for: 0 -> 0; matrix products, arithmetic and copies ran while one was open for 1% -> 1% of each run, Pallas kernels for 47% -> 48%
where the time goes in v6:
time: 400 us; the launch traced here: 395 us
  Pallas kernels  375 us (94%)
  between operations  14.4 us (4%)
    pallas_call x1, Pallas kernels, finish_all(): pl.pallas_call(partial(finish_kernel, n_tensor), out_shape=[jax.ShapeDtyp...  132 us
    pallas_call x1, Pallas kernels, start(): pl.pallas_call(partial(start_kernel, n_tensor), out_shape=[jax.ShapeDtype...  94.2 us
    pallas_call x1, Pallas kernels, middle(): pl.pallas_call(partial(middle_kernel, n_tensor), out_shape=[jax.ShapeDtyp...  78.3 us
    pallas_call x1, Pallas kernels, attend_back(): pl.pallas_call(partial(backward_kernel, len(pieces)), out_shape=[jax.Shap...  56.5 us
    pallas_call x1, Pallas kernels, last(): pl.pallas_call(last_kernel, out_shape=[jax.ShapeDtypeStruct(tokens_low.sh...  14.3 us
  transfers between devices with their start and end apart: 2, of which 0 were waited for; matrix products, arithmetic and copies ran while one was open for 1% of the time, Pallas kernels for 48%

profile of v6, /device:TPU:0, one launch (start us, length us, event | category | flops | bytes accessed | tf_op | source)
XLA Modules:
  0.0 395.2 jit_solution(11933566610891130731)
XLA Ops:
  7.2 0.0 copy-start
  7.2 0.0 all-gather.3.cloned.1.call-start
  7.3 0.7 constant_dynamic-slice_fusion.1
  8.0 0.0 copy-done
  8.0 0.1 copy.41
  8.1 0.1 reshape.78
  8.2 0.7 collective-permute-start
  8.9 1.3 reshape.81.refs_3_
  10.1 0.0 collective-permute-done
  10.2 0.1 convert_element_type.15
  10.2 0.1 pad_maximum_fusion
  10.3 0.1 reshape.79
  10.5 0.6 reshape.80.refs_5_.rand
  11.1 0.7 fusion.2.refs_4_
  11.8 94.2 %start.1 = (bf16[4,768,768]{2,1,0:T(8,128)(2,1)}, bf16[2,768,3072]{2,1,0:T(8,128)(2,1)}, f32[1,3072]{1,0:T(1,128)}, bf16[1024,768]{1,0:T(8,128)(2,1)}, bf16[1024...) custom-call(f32[4,96,192]{2,1,0:T(8,128)} %refs_1_.3, ...), custom_call_target="tpu_custom_call" | custom-call | flops 3623878656 | bytes 104857600 | tf_op jit(solution)/shard_map/start/pallas_call | solution.py:1177
  105.9 78.3 %middle.1 = (bf16[4,512,768]{2,1,0:T(8,128)(2,1)}, bf16[512,768]{1,0:T(8,128)(2,1)}, bf16[768,3072]{1,0:T(8,128)(2,1)}, bf16[768,3072]{1,0:T(8,128)(2,1)}, bf16[...) custom-call(bf16[1024,768]{1,0:T(8,128)(2,1)} %get-tuple-element.71., ...), custom_call_target="tpu_custom_call" | custom-call | flops 32614907904 | bytes 62914560 | tf_op jit(solution)/shard_map/middle/pallas_call | solution.py:1483
  184.3 0.0 all-gather.3.cloned.1.call-update
  184.3 0.6 pad_add_fusion.1.meta
  184.9 0.7 fusion.tab_ref
  185.6 56.5 %attend_back.1 = (bf16[1,1024,768]{2,1,0:T(8,128)(2,1)}, bf16[4,1024,768]{2,1,0:T(8,128)(2,1)}, bf16[1,1024,768]{2,1,0:T(8,128)(2,1)}, bf16[1,1024,768]{2,1,0:T(...) custom-call(s32[48]{0:T(128)} %reshape.80.refs_5_.rand, s32[2]{0:T(128)} %pad_add_fusion.1.meta, ...), custom_call_target="tpu_custom_call" | custom-call | flops 16106127360 | bytes 17301504 | tf_op jit(solution)/shard_map/attend_back/pallas_call | solution.py:379
  242.1 131.7 %finish.1 = (f32[4,96,192]{2,1,0:T(8,128)}, f32[2,96,768]{2,1,0:T(8,128)}, f32[6,768]{1,0:T(8,128)}, f32[2,192]{1,0:T(2,128)}, f32[1,768]{1,0:T(1,128)}, /*index=5*/bf16[4,1024,768]{2,1,0:T(8,128)(2,1)}) custom-call(bf16[1024,768]{1,0:T(8,128)(2,1)} %bitcast.17, bf16[1024,768]{1,0:T(8,128)(2,1)} %bitcast.18, bf16[1024,768]{1,0:T(8,128)(2,1)} %bitcast.19, ...), custom_call_target="tpu_custom_call" | custom-call | flops 7247757312 | bytes 419430400 | tf_op jit(solution)/shard_map/finish/pallas_call | solution.py:1989
  373.7 0.0 all-gather.3.cloned.1.call-done
  373.8 0.0 copy-start.1
  373.8 14.3 %last.1 = (f32[4,1024,768]{2,1,0:T(8,128)}, bf16[4,1024,768]{2,1,0:T(8,128)(2,1)}, f32[3,96,192]{2,1,0:T(8,128)}, f32[3,96,192]{2,1,0:T(8,128)}, f32[2,96,192]{2...) custom-call(bf16[4,1024,768]{2,1,0:T(8,128)(2,1)} %get-tuple-element, ...), custom_call_target="tpu_custom_call", output_to_operand_aliasing={{1}: (2, {})} | custom-call | tf_op jit(solution)/shard_map/last/pallas_call | solution.py:2125
  388.1 0.0 copy-done.1
  (5 shorter events, 0.1 us)
Async XLA Ops:
  7.2 0.8 copy-start
  7.2 366.5 %all-gather.3.cloned.1.call-start = ((), (), s32[]{:S(2)}) async-start(), calls=%async_computation | async-start | bytes 3932160 | tf_op jit(solution)/shard_map/all_gather | solution.py:2249
  8.2 2.0 collective-permute-start
  373.8 14.3 %copy-start.1 = (s32[4,2048]{1,0:T(4,128)S(1)}, s32[4,2048]{1,0:T(4,128)}, u32[]{:S(2)}) copy-start(s32[4,2048]{1,0:T(4,128)} %param.21) | copy-start | bytes 98308
Sparse Core Ops, SparseCore 0:
  184.4 61.0 all-gather.2

commit v7 on v6

--- a/solution.py
+++ b/solution.py
@@ -1310,13 +1310,14 @@
         if_home(lambda: keep_home(i).wait(), lambda: send_home(i).wait_recv())
 
     events = {
-        (1, 2): ([0], []),
-        (2, 2): ([1], []),
-        (2, 3): ([2], []),
-        (3, 2): ([], [0]),
-        (3, 3): ([3], []),
+        (2, 0): ([0], []),
+        (3, 0): ([1], []),
+        (4, 0): ([2], []),
+        (4, 2): ([3], []),
+        (5, 1): ([], [0]),
     }
-    sizes = [ITEM] + [chunk] * (chunks - 1) + [chunk - ITEM]
+    sizes = [ITEM] * items + [chunk] * ((n_rows - items * ITEM) // chunk)
+    cot_after = {items - 1: (1, 2), items: (3,)}
     start_row = 0
     for i, size in enumerate(sizes):
         rows = slice(start_row, start_row + size)
@@ -1361,8 +1362,8 @@
         ready[rows, :] = (unit * vec_ref[2:3, :] + vec_ref[3:4, :]).astype(bf16)
         for n in range(start_row // ITEM, (start_row + size) // ITEM):
             if_home(lambda: keep_home(n).start(), lambda: send_home(n).start())
-        if i + 1 < chunks:
-            if_home(lambda: keep_cot(i + 1).start(), lambda: swap_cot(i + 1).start())
+        for n in cot_after.get(i, ()):
+            if_home(lambda: keep_cot(n).start(), lambda: swap_cot(n).start())
         start_row += size
 
     sums_out[...] = jnp.zeros_like(sums_out)

time: 400 us -> 404 us (1.010)
  transfers between devices with their start and end apart: 2 -> 2, of which waited for: 0 -> 0; matrix products, arithmetic and copies ran while one was open for 1% -> 1% of each run, Pallas kernels for 48% -> 47%
where the time goes in v7:
time: 404 us; the launch traced here: 399 us
  Pallas kernels  379 us (94%)
  between operations  14.4 us (4%)
    pallas_call x1, Pallas kernels, finish_all(): pl.pallas_call(partial(finish_kernel, n_tensor), out_shape=[jax.ShapeDtyp...  132 us
    pallas_call x1, Pallas kernels, start(): pl.pallas_call(partial(start_kernel, n_tensor), out_shape=[jax.ShapeDtype...  94.2 us
    pallas_call x1, Pallas kernels, middle(): pl.pallas_call(partial(middle_kernel, n_tensor), out_shape=[jax.ShapeDtyp...  81.5 us
    pallas_call x1, Pallas kernels, attend_back(): pl.pallas_call(partial(backward_kernel, len(pieces)), out_shape=[jax.Shap...  56.4 us
    pallas_call x1, Pallas kernels, last(): pl.pallas_call(last_kernel, out_shape=[jax.ShapeDtypeStruct(tokens_low.sh...  14.3 us
  transfers between devices with their start and end apart: 2, of which 0 were waited for; matrix products, arithmetic and copies ran while one was open for 1% of the time, Pallas kernels for 47%

profile of v7, /device:TPU:0, one launch (start us, length us, event | category | flops | bytes accessed | tf_op | source)
XLA Modules:
  0.0 398.8 jit_solution(9337445901518057159)
XLA Ops:
  7.2 0.0 copy-start
  7.2 0.0 all-gather.3.cloned.1.call-start
  7.3 0.7 constant_dynamic-slice_fusion.1
  8.0 0.0 copy-done
  8.0 0.1 copy.41
  8.1 0.1 reshape.78
  8.2 0.7 collective-permute-start
  8.9 1.3 reshape.81.refs_3_
  10.1 0.0 collective-permute-done
  10.2 0.1 convert_element_type.15
  10.2 0.1 pad_maximum_fusion
  10.3 0.1 reshape.79
  10.5 0.6 reshape.80.refs_5_.rand
  11.1 0.7 fusion.2.refs_4_
  11.8 94.2 %start.1 = (bf16[4,768,768]{2,1,0:T(8,128)(2,1)}, bf16[2,768,3072]{2,1,0:T(8,128)(2,1)}, f32[1,3072]{1,0:T(1,128)}, bf16[1024,768]{1,0:T(8,128)(2,1)}, bf16[1024...) custom-call(f32[4,96,192]{2,1,0:T(8,128)} %refs_1_.3, ...), custom_call_target="tpu_custom_call" | custom-call | flops 3623878656 | bytes 104857600 | tf_op jit(solution)/shard_map/start/pallas_call | solution.py:1177
  105.9 81.5 %middle.1 = (bf16[4,512,768]{2,1,0:T(8,128)(2,1)}, bf16[512,768]{1,0:T(8,128)(2,1)}, bf16[768,3072]{1,0:T(8,128)(2,1)}, bf16[768,3072]{1,0:T(8,128)(2,1)}, bf16[...) custom-call(bf16[1024,768]{1,0:T(8,128)(2,1)} %get-tuple-element.71., ...), custom_call_target="tpu_custom_call" | custom-call | flops 32614907904 | bytes 62914560 | tf_op jit(solution)/shard_map/middle/pallas_call | solution.py:1484
  187.4 0.0 all-gather.3.cloned.1.call-update
  187.4 0.6 pad_add_fusion.1.meta
  188.0 0.7 fusion.tab_ref
  188.7 56.4 %attend_back.1 = (bf16[1,1024,768]{2,1,0:T(8,128)(2,1)}, bf16[4,1024,768]{2,1,0:T(8,128)(2,1)}, bf16[1,1024,768]{2,1,0:T(8,128)(2,1)}, bf16[1,1024,768]{2,1,0:T(...) custom-call(s32[48]{0:T(128)} %reshape.80.refs_5_.rand, s32[2]{0:T(128)} %pad_add_fusion.1.meta, ...), custom_call_target="tpu_custom_call" | custom-call | flops 16106127360 | bytes 17301504 | tf_op jit(solution)/shard_map/attend_back/pallas_call | solution.py:379
  245.2 132.2 %finish.1 = (f32[4,96,192]{2,1,0:T(8,128)}, f32[2,96,768]{2,1,0:T(8,128)}, f32[6,768]{1,0:T(8,128)}, f32[2,192]{1,0:T(2,128)}, f32[1,768]{1,0:T(1,128)}, /*index=5*/bf16[4,1024,768]{2,1,0:T(8,128)(2,1)}) custom-call(bf16[1024,768]{1,0:T(8,128)(2,1)} %bitcast.17, bf16[1024,768]{1,0:T(8,128)(2,1)} %bitcast.18, bf16[1024,768]{1,0:T(8,128)(2,1)} %bitcast.19, ...), custom_call_target="tpu_custom_call" | custom-call | flops 7247757312 | bytes 419430400 | tf_op jit(solution)/shard_map/finish/pallas_call | solution.py:1990
  377.4 0.0 all-gather.3.cloned.1.call-done
  377.4 0.0 copy-start.1
  377.4 14.3 %last.1 = (f32[4,1024,768]{2,1,0:T(8,128)}, bf16[4,1024,768]{2,1,0:T(8,128)(2,1)}, f32[3,96,192]{2,1,0:T(8,128)}, f32[3,96,192]{2,1,0:T(8,128)}, f32[2,96,192]{2...) custom-call(bf16[4,1024,768]{2,1,0:T(8,128)(2,1)} %get-tuple-element, ...), custom_call_target="tpu_custom_call", output_to_operand_aliasing={{1}: (2, {})} | custom-call | tf_op jit(solution)/shard_map/last/pallas_call | solution.py:2126
  391.7 0.0 copy-done.1
  (5 shorter events, 0.1 us)
Async XLA Ops:
  7.2 0.8 copy-start
  7.2 370.2 %all-gather.3.cloned.1.call-start = ((), (), s32[]{:S(2)}) async-start(), calls=%async_computation | async-start | bytes 3932160 | tf_op jit(solution)/shard_map/all_gather | solution.py:2250
  8.2 2.0 collective-permute-start
  377.4 14.3 %copy-start.1 = (s32[4,2048]{1,0:T(4,128)S(1)}, s32[4,2048]{1,0:T(4,128)}, u32[]{:S(2)}) copy-start(s32[4,2048]{1,0:T(4,128)} %param.21) | copy-start | bytes 98308
Sparse Core Ops, SparseCore 0:
  187.6 63.6 all-gather.2
